TPU v7x, 32 devices: a whole 2x2x4 slice. The times are simulated.
32 devices in a mesh: ctx: 4 (over y, core), tp: 4 (over z), pp: 2 (over x).
Axes of the slice: x: 2, y: 2, z: 4, core: 2. Of those that a mesh axis runs over, the one named last changes fastest.
Arguments:
- queries: bfloat16 [2, 1024, 12288], P('pp', 'ctx', 'tp'), may hold values from -8 to 8
- latents: bfloat16 [2, 1024, 576], P('pp', ('ctx', 'tp')), may hold values from -8 to 8
- latent_gain: float32 [2, 512], P('pp'), may hold values from 0.5 to 2
- w_ukv: bfloat16 [2, 512, 16384], P('pp', None, 'tp'), may hold values from -0.25 to 0.25
- w_o: bfloat16 [2, 8192, 7168], P('pp', 'tp'), may hold values from -0.1875 to 0.1875
- residual: bfloat16 [2, 1024, 7168], P('pp', ('ctx', 'tp')), may hold values from -3 to 3
- block_order: int32 [2, 8], P('pp'), may hold values from 0 to 7, each once within a row
Outputs:
- handed: bfloat16 [2, 1024, 7168], P('pp', ('ctx', 'tp'))
Inputs may be any that keep to these rules, and one draw needn't show every extreme that they name: `block_order`: each row names each of the 8 sequence blocks once.
All inputs are finite; a program needn't handle non-finite values.
Results may differ from a plain program's by a relative error of at most 0.02.
Values may be sent and summed in bfloat16 or wider, within the bound.
No kernel may reach another device: no remote copies, remote signals or barrier semaphores. Data moves between devices by JAX's collectives and lax.ppermute only.
A program may use at most 128 MiB of HBM per device.

v0:
```python
import jax
import jax.numpy as jnp
from jax import lax
from jax.sharding import PartitionSpec as P

NOPE = 128
ROPE = 64
VDIM = 128
LATENT = 512


score_scale = 0.135


def passed_along(value, axis, steps):
    count = lax.axis_size(axis)
    pairs = [(source, (source + steps) % count) for source in range(count)]
    return lax.ppermute(value, axis, pairs)


def rotate(values, places):
    middle = values.shape[-1] // 2
    freqs = 10000.0 ** (-(jnp.arange(middle).astype(jnp.float32) * 2.0 / values.shape[-1]))
    angles = places[..., None] * freqs
    first_half = values[..., :middle]
    second_half = values[..., middle:]
    return jnp.concatenate(
        [
            first_half * jnp.cos(angles) - second_half * jnp.sin(angles),
            first_half * jnp.sin(angles) + second_half * jnp.cos(angles),
        ],
        axis=-1,
    )


def place_rows(order_row, first, count, block_len):
    row_ids = first + jnp.arange(count, dtype=jnp.int32)
    owners = row_ids // block_len
    table = jnp.arange(order_row.shape[0], dtype=jnp.int32)
    base = jnp.sum(jnp.where(owners[:, None] == table[None, :], order_row[None, :], 0), axis=1)
    return base * block_len + row_ids % block_len


def local(queries, latents, latent_gain, w_ukv, w_o, residual, block_order):
    order_row = block_order[0]
    tp_count = lax.axis_size("tp")
    tok_dev = queries.shape[1]
    block_len = tok_dev // 2
    lat_rows = latents.shape[1]
    heads_here = w_o.shape[1] // VDIM
    query_places = place_rows(order_row, lax.axis_index("ctx") * tok_dev, tok_dev, block_len)
    query_all = queries[0].reshape(tok_dev, heads_here, NOPE + ROPE)
    query_nope = query_all[..., :NOPE]
    query_rope = rotate(
        query_all[..., NOPE:].astype(jnp.float32), query_places.astype(jnp.float32)[:, None]
    ).astype(jnp.bfloat16)
    own_first = (lax.axis_index("ctx") * tp_count + lax.axis_index("tp")) * lat_rows
    own_places = place_rows(order_row, own_first, lat_rows, block_len)
    latent_rows = latents[0].astype(jnp.float32)
    compressed = latent_rows[:, :LATENT]
    scale_rows = lax.rsqrt(jnp.mean(compressed * compressed, axis=-1, keepdims=True) + 1e-06)
    normed = (compressed * scale_rows * latent_gain[0][None, :]).astype(jnp.bfloat16)
    own_rope = rotate(latent_rows[:, LATENT:], own_places.astype(jnp.float32)).astype(jnp.bfloat16)
    own_keys = jnp.concatenate([normed, own_rope], axis=-1)
    up_weights = w_ukv[0]

    def expand(latent_part):
        produced = jnp.dot(latent_part, up_weights, preferred_element_type=jnp.float32).astype(
            jnp.bfloat16
        )
        return produced.reshape(latent_part.shape[0], heads_here, NOPE + VDIM)

    piece = lax.all_gather(own_keys, ("ctx", "tp"), axis=0, tiled=True)
    make_keys = lambda: (expand(piece[:, :LATENT]), piece[:, LATENT:])
    key_places = place_rows(order_row, jnp.int32(0), piece.shape[0], block_len)
    running_max = jnp.full((tok_dev, heads_here), -1e30, jnp.float32)
    key_value, key_rope = make_keys()
    scores = (
        jnp.einsum(
            "thd,nhd->thn", query_nope, key_value[..., :NOPE], preferred_element_type=jnp.float32
        )
        + jnp.einsum("thr,nr->thn", query_rope, key_rope, preferred_element_type=jnp.float32)
    ) * score_scale
    allowed = (key_places[None, :] <= query_places[:, None])[:, None, :]
    scores = jnp.where(allowed, scores, -1e30)
    new_max = jnp.maximum(running_max, jnp.max(scores, axis=-1))
    weights = jnp.where(allowed, jnp.exp(scores - new_max[..., None]), 0.0)
    new_total = jnp.sum(weights, axis=-1)
    new_sum = jnp.einsum(
        "thn,nhd->thd",
        weights.astype(jnp.bfloat16),
        key_value[..., NOPE:],
        preferred_element_type=jnp.float32,
    )
    attention = (
        (new_sum / new_total[..., None]).astype(jnp.bfloat16).reshape(tok_dev, heads_here * VDIM)
    )
    out_weights = w_o[0]
    summed = lax.psum_scatter(
        jnp.dot(attention, out_weights, preferred_element_type=jnp.float32).astype(jnp.bfloat16),
        "tp",
        scatter_dimension=0,
        tiled=True,
    ).astype(jnp.float32)
    mixed = (summed + residual[0].astype(jnp.float32)).astype(jnp.bfloat16)
    handed = passed_along(mixed, "pp", 1)
    return handed[None]


def solution(mesh):
    in_specs = (
        P("pp", "ctx", "tp"),
        P("pp", ("ctx", "tp"), None),
        P("pp", None),
        P("pp", None, "tp"),
        P("pp", "tp", None),
        P("pp", ("ctx", "tp"), None),
        P("pp", None),
    )
    out_specs = P("pp", ("ctx", "tp"), None)
    return jax.shard_map(local, mesh=mesh, in_specs=in_specs, out_specs=out_specs, check_vma=False)
```

profile of v0, /device:TPU:16, one launch (start us, length us, event | category | flops | bytes accessed | tf_op | source)
XLA Modules:
  0.0 217.5 jit_solution(3498588951620757480)
XLA Ops:
  6.5 0.0 copy-start.2
  6.5 0.0 all-gather.2.cloned.1.call-start
  6.6 0.8 select_reduce_fusion.2
  7.4 1.0 copy.35
  8.4 0.1 multiply_reduce_fusion
  8.5 0.1 fusion.34
  8.7 0.8 multiply_convert_fusion
  9.5 0.8 copy.36
  10.3 0.0 all-gather.2.cloned.1.call-update
  10.3 0.0 reduce-scatter.2.cloned.1.call-start
  10.4 1.7 copy.39
  12.1 0.0 copy-done.2
  12.1 0.1 select_reduce_fusion.1
  12.2 0.1 select_reduce_fusion
  12.3 0.2 multiply_cosine_fusion
  12.5 0.2 broadcast_compare_fusion
  12.7 0.1 slice_convert_fusion
  12.8 0.2 subtract_convert_fusion
  13.0 35.7 %all-gather.2.cloned.1.call-done = bf16[1024,576]{1,0:T(8,128)(2,1)} async-done(((bf16[64,576]{1,0:T(8,128)(2,1)}), bf16[1024,576]{1,0:T(8,128)(2,1)}) %all-gather.2.cloned.1.call-update) | async-done | bytes 1179664 | tf_op jit(solution)/shard_map/all_gather | solution.py:73
  48.7 10.2 %convolution_convert_fusion = bf16[1024,4096]{1,0:T(8,128)(2,1)} fusion(bf16[1,512,4096]{2,1,0:T(8,128)(2,1)} %param.10, bf16[1024,576]{1,0:T(8,128)(2,1)} %all-gather.2.cloned.1.call-done), kind=kOutput, calls=%fused_computation.13 | convolution fusion | flops 4299161600 | bytes 13631488 | tf_op jit(solution)/shard_map/dot_general | solution.py:68
  59.0 9.7 %copy.50 = bf16[128,8,16,256]{3,2,1,0:T(8,128)(2,1)} copy(bf16[128,8,16,256]{3,1,2,0:T(8,128)(2,1)} %bitcast.41) | data formatting | bytes 16777216
  68.7 5.5 %fusion.53 = (bf16[1024,16,128]{2,1,0:T(8,128)(2,1)}, bf16[1024,16,128]{2,1,0:T(8,128)(2,1)S(1)}) fusion(bf16[1024,16,256]{2,1,0:T(8,128)(2,1)} %bitcast.38), kind=kLoop, calls=%fused_computation.89 | loop fusion | bytes 16777216 | tf_op jit(solution)/shard_map/slice | solution.py:92
  74.1 2.3 %fusion.14 = f32[16,1024,256]{2,1,0:T(8,128)S(1)} fusion(bf16[1024,16,128]{2,1,0:T(8,128)(2,1)S(1)} %get-tuple-element.8, bf16[256,16,192]{0,2,1:T(8,128)(2,1)S(1)} %bitcast.40), kind=kOutput, calls=%fused_computation.14 | convolution fusion | flops 1073741824 | bytes 22020096 | tf_op jit(solution)/shard_map/thd,nhd->thn/dot_general | solution.py:79
  76.5 8.8 %fusion.54 = (f32[256,16]{0,1:T(8,128)S(1)}, f32[256,16,1024]{0,2,1:T(8,128)}) fusion(bf16[256,16,32]{0,2,1:T(8,128)(2,1)S(1)} %get-tuple-element.10, bf16[256,16,32]{0,2,1:T(8,128)(2,1)S(1)} %get-tuple-element.9, bf16[1024,576]{1,0:T(8,128)(2,1)} %all-gather.2.cloned.1.call-done, f32[16,1024,256]{2,1,0:T(8,128)S(1)} %fusion.14, ...), kind=kOutput, calls=%fused_computation.90 | convolution fusion | flops 554692608 | bytes 34619392 | tf_op jit(solution)/shard_map/thr,nr->thn/dot_general | solution.py:82
  85.3 0.0 copy-start
  85.3 8.7 %fusion.4 = f32[256,16]{0,1:T(8,128)S(1)} fusion(f32[256,16,1024]{0,2,1:T(8,128)} %get-tuple-element.16, f32[256,16]{0,1:T(8,128)S(1)} %broadcast_maximum_fusion, pred[256,1024]{0,1:T(8,128)(4,1)S(1)} %broadcast_compare_fusion), kind=kLoop, calls=%fused_computation.6 | loop fusion | flops 12578816 | bytes 17072128 | tf_op jit(solution)/shard_map/reduce_sum | solution.py:88
  94.0 0.0 copy-done
  94.0 8.0 %fusion.18 = bf16[256,16,128]{0,2,1:T(8,128)(2,1)S(1)} fusion(f32[256,16,1024]{0,2,1:T(8,128)} %get-tuple-element.16, f32[256,16]{0,1:T(8,128)S(1)} %broadcast_maximum_fusion, pred[256,1024]{0,1:T(8,128)(4,1)S(1)} %broadcast_compare_fusion, bf16[1024,16,128]{2,1,0:T(8,128)(2,1)S(1)} %copy-done, f32[256,16]{0,1:T(8,128)S(1)} %fusion.4), kind=kOutput, calls=%fused_computation.19 | convolution fusion | flops 1087373312 | bytes 22315008 | tf_op jit(solution)/shard_map/thn,nhd->thd/dot_general | solution.py:89
  102.0 14.6 %fusion.6 = bf16[256,7168]{1,0:T(8,128)(2,1)} fusion(bf16[256,2048]{0,1:T(8,128)(2,1)S(1)} %bitcast.42, bf16[1,2048,7168]{2,1,0:T(8,128)(2,1)} %param.11), kind=kOutput, calls=%fused_computation.8 | convolution fusion | flops 7518027776 | bytes 34078720 | tf_op jit(solution)/shard_map/dot_general | solution.py:100
  116.6 0.0 copy-start.1
  116.6 0.0 reduce-scatter.2.cloned.1.call-update
  116.6 69.5 %reduce-scatter.2.cloned.1.call-done = bf16[64,7168]{1,0:T(8,128)(2,1)} async-done(((bf16[256,7168]{1,0:T(8,128)(2,1)}), bf16[64,7168]{1,0:T(8,128)(2,1)}) %reduce-scatter.2.cloned.1.call-update) | async-done | bytes 917520 | tf_op jit(solution)/shard_map/reduce_scatter | solution.py:99
  186.1 0.0 copy-done.1
  186.1 1.4 fusion.19
  187.5 1.5 collective-permute-start
  189.0 20.7 %collective-permute-done = bf16[64,7168]{1,0:T(8,128)(2,1)S(1)} collective-permute-done((bf16[64,7168]{1,0:T(8,128)(2,1)S(1)}, bf16[64,7168]{1,0:T(8,128)(2,1)S(1)}, u32[]{:S(2)}, u32[]{:S(2)}) %collective-permute-start) | collective-permute-done | bytes 917536 | tf_op jit(solution)/shard_map/ppermute | solution.py:18
  209.7 0.9 copy.58
  (11 shorter events, 0.1 us)
Async XLA Ops:
  6.5 5.6 %copy-start.2 = (s32[1,8]{1,0:T(1,128)S(1)}, s32[1,8]{1,0:T(1,128)}, u32[]{:S(2)}) copy-start(s32[1,8]{1,0:T(1,128)} %param.13) | copy-start | bytes 100
  6.5 42.2 %all-gather.2.cloned.1.call-start = ((), (), s32[]{:S(2)}) async-start(), calls=%async_computation.1 | async-start | bytes 1392640 | tf_op jit(solution)/shard_map/all_gather | solution.py:73
  10.3 175.8 %reduce-scatter.2.cloned.1.call-start = ((), (), s32[]{:S(2)}) async-start(), calls=%async_computation.2 | async-start | bytes 4587520 | tf_op jit(solution)/shard_map/reduce_scatter | solution.py:99
  85.3 8.7 %copy-start = (bf16[1024,16,128]{2,1,0:T(8,128)(2,1)S(1)}, bf16[1024,16,128]{2,1,0:T(8,128)(2,1)}, u32[]{:S(2)}) copy-start(bf16[1024,16,128]{2,1,0:T(8,128)(2,1)} %get-tuple-element.7) | copy-start | bytes 12582916
  116.6 69.5 %copy-start.1 = (bf16[1,64,7168]{2,1,0:T(8,128)(2,1)S(1)}, bf16[1,64,7168]{2,1,0:T(8,128)(2,1)}, u32[]{:S(2)}) copy-start(bf16[1,64,7168]{2,1,0:T(8,128)(2,1)} %param.12) | copy-start | bytes 2752516
  187.5 22.2 %collective-permute-start = (bf16[64,7168]{1,0:T(8,128)(2,1)S(1)}, bf16[64,7168]{1,0:T(8,128)(2,1)S(1)}, u32[]{:S(2)}, u32[]{:S(2)}) collective-permute-start(bf16[64,7168]{1,0:T(8,128)(2,1)S(1)} %fusion.19), channel_id=1, source_target_pairs={{0,1},{1,0},{2,3},{3,2},{4,5},{5,4},{6,7},{7,6},{8,9},{9,8},{10,11... | collective-permute-start | bytes 2752520 | tf_op jit(solution)/shard_map/ppermute | solution.py:18
Sparse Core Ops, SparseCore 0:
  10.4 38.2 all-gather.1
  116.8 69.3 reduce-scatter.1
where the time goes:
time: 219 us; the launch traced here: 217 us
  waiting for transfers between devices  126 us (58%)
  matrix products  44 us (20%)
  local copies, waits for them, and re-layouts  19.6 us (9%)
  between operations  13.5 us (6%)
  other arithmetic  12.9 us (6%)
    reduce_scatter x1, waiting for transfers between devices, local(): lax.psum_scatter(jnp.dot(attention, out_weights, preferred_element_type=j...  69.5 us
    all_gather x1, waiting for transfers between devices, local(): piece = lax.all_gather(own_keys, ('ctx', 'tp'), axis=0, tiled=True)  35.7 us
    ppermute x1, waiting for transfers between devices, passed_along(): return lax.ppermute(value, axis, pairs)  20.7 us
    dot_general x1, matrix products, local(): jnp.dot(attention, out_weights, preferred_element_type=jnp.float32)  14.6 us
    unnamed x10, local copies, waits for them, and re-layouts  13.4 us
    dot_general x1, matrix products, expand(): jnp.dot(latent_part, up_weights, preferred_element_type=jnp.float32)  10.2 us
    dot_general x1, matrix products, local(): jnp.einsum('thr,nr->thn', query_rope, key_rope, preferred_element_type=jn...  8.81 us
    reduce_sum x1, other arithmetic, local(): new_total = jnp.sum(weights, axis=-1)  8.72 us
  transfers between devices with their start and end apart: 3, of which 3 were waited for; matrix products, arithmetic and copies ran while one was open for 1% of the time, Pallas kernels for 0%

commit v1 on v0

v1 whole, which is shorter than its diff:
```python
import functools
import math

import jax
import jax.numpy as jnp
from jax import lax
from jax.experimental import pallas as pl
from jax.experimental.pallas import tpu as pltpu
from jax.sharding import PartitionSpec as P

NOPE = 128
ROPE = 64
VDIM = 128
LATENT = 512
LANES = 128

score_scale = 0.135
SCALE2 = score_scale * math.log2(math.e)

UNIT_PIECES = {0: 2, 1: 2}


def angles_of(places):
    freqs = 10000.0 ** (-(jnp.arange(ROPE // 2).astype(jnp.float32) * 2.0 / ROPE))
    return places.astype(jnp.float32)[:, None] * freqs


def rotate(values, places):
    middle = values.shape[-1] // 2
    angles = angles_of(places)
    first_half = values[..., :middle]
    second_half = values[..., middle:]
    return jnp.concatenate(
        [
            first_half * jnp.cos(angles) - second_half * jnp.sin(angles),
            first_half * jnp.sin(angles) + second_half * jnp.cos(angles),
        ],
        axis=-1,
    )


def place_rows(order_row, first, count, block_len):
    row_ids = first + jnp.arange(count, dtype=jnp.int32)
    owners = row_ids // block_len
    table = jnp.arange(order_row.shape[0], dtype=jnp.int32)
    base = jnp.sum(jnp.where(owners[:, None] == table[None, :], order_row[None, :], 0), axis=1)
    return base * block_len + row_ids % block_len


def gather_keys(own_keys):
    tp_count, ctx_count = lax.axis_size("tp"), lax.axis_size("ctx")
    steps = []
    step = 1
    while step < tp_count:
        steps.append(("tp", step))
        step *= 2
    step = 2
    while step < ctx_count:
        steps.append(("ctx", step))
        step *= 2
    steps.append(("ctx", 1))
    held, masks = own_keys, [(0, 0)]
    for axis, step in steps:
        pairs = [(i, i ^ step) for i in range(lax.axis_size(axis))]
        got = lax.ppermute(held, axis, pairs)
        held = jnp.concatenate([held, got], axis=0)
        masks = masks + [
            (c ^ step, t) if axis == "ctx" else (c, t ^ step) for c, t in masks
        ]
    return held, masks


def attention_kernel(q_ref, lat_ref, w_ref, cos_ref, sin_up_ref, sin_down_ref, qpos_ref, kpos_ref, out_ref, bias_ref):
    @pl.when(pl.program_id(0) == 0)
    def _():
        bias_ref[...] = jnp.where(kpos_ref[...] <= qpos_ref[...], 0.0, -1e30)

    normed = lat_ref[:, :LATENT]
    key_rope = lat_ref[:, LATENT:]
    rows = q_ref.shape[0]
    produced = jnp.dot(normed, w_ref[...], preferred_element_type=jnp.float32).astype(jnp.bfloat16)
    ones = jnp.ones((lat_ref.shape[0], LANES), jnp.bfloat16)
    keys, values = [], []
    for h in range(2):
        base = h * (NOPE + VDIM)
        keys.append(jnp.concatenate([produced[:, base : base + NOPE], key_rope], axis=1))
        values.append(jnp.concatenate([produced[:, base + NOPE : base + NOPE + VDIM], ones], axis=1))
    chunk = min(rows, 128)
    for r in range(rows // chunk):
        span = pl.ds(r * chunk, chunk)
        g0 = q_ref[span, :LANES]
        g1 = q_ref[span, LANES : 2 * LANES].astype(jnp.float32)
        g2 = q_ref[span, 2 * LANES :].astype(jnp.float32)
        r1 = pltpu.roll(g1, ROPE, 1)
        r2 = pltpu.roll(g2, ROPE, 1)
        lane = lax.broadcasted_iota(jnp.int32, (chunk, LANES), 1)
        nope1 = jnp.where(lane < ROPE, r1, r2).astype(jnp.bfloat16)
        cos, sin_up, sin_down = cos_ref[span, :], sin_up_ref[span, :], sin_down_ref[span, :]

        def turned(x):
            return (
                x * cos
                + pltpu.roll(x, ROPE // 2, 1) * sin_up
                + pltpu.roll(x, LANES - ROPE // 2, 1) * sin_down
            ).astype(jnp.bfloat16)

        queries = [
            jnp.concatenate([g0, turned(g1)], axis=1),
            jnp.concatenate([nope1, turned(r2)], axis=1),
        ]
        for h in range(2):
            scores = lax.dot_general(
                queries[h], keys[h], (((1,), (1,)), ((), ())), preferred_element_type=jnp.float32
            )
            scores = scores + bias_ref[span, :]
            top = jnp.max(scores, axis=1, keepdims=True)
            weights = jnp.exp2((scores - top) * SCALE2).astype(jnp.bfloat16)
            summed = jnp.dot(weights, values[h], preferred_element_type=jnp.float32)
            out_ref[span, h * VDIM : (h + 1) * VDIM] = (
                summed[:, :VDIM] / summed[:, VDIM : VDIM + 1]
            ).astype(out_ref.dtype)


def attend(queries, latents, up_weights, query_places, key_places):
    rows, key_count = queries.shape[0], latents.shape[0]
    pairs = queries.shape[1] // (2 * (NOPE + ROPE))
    angles = angles_of(query_places)
    cos, sin = jnp.cos(angles), jnp.sin(angles)
    zero, blank = jnp.zeros_like(cos), jnp.zeros((rows, LANES - ROPE), jnp.float32)
    cos_table = jnp.concatenate([cos, cos, blank], axis=1)
    sin_up = jnp.concatenate([zero, sin, blank], axis=1)
    sin_down = jnp.concatenate([-sin, zero, blank], axis=1)
    whole = lambda shape: pl.BlockSpec(shape, lambda i: (0, 0))
    return pl.pallas_call(
        attention_kernel,
        grid=(pairs,),
        out_shape=jax.ShapeDtypeStruct((rows, pairs * 2 * VDIM), jnp.bfloat16),
        in_specs=[
            pl.BlockSpec((rows, 2 * (NOPE + ROPE)), lambda i: (0, i)),
            whole((key_count, LATENT + LANES)),
            pl.BlockSpec((LATENT, 2 * (NOPE + VDIM)), lambda i: (0, i)),
            whole((rows, LANES)),
            whole((rows, LANES)),
            whole((rows, LANES)),
            whole((rows, 1)),
            whole((1, key_count)),
        ],
        out_specs=pl.BlockSpec((rows, 2 * VDIM), lambda i: (0, i)),
        scratch_shapes=[pltpu.VMEM((rows, key_count), jnp.float32)],
        compiler_params=pltpu.CompilerParams(vmem_limit_bytes=32 * 1024 * 1024),
        cost_estimate=pl.CostEstimate(
            flops=2 * pairs * 2 * key_count * (LATENT * 256 + rows * 512),
            bytes_accessed=2 * (queries.size + latents.size + up_weights.size),
            transcendentals=2 * pairs * rows * key_count,
        ),
    )(queries, latents, up_weights, cos_table, sin_up, sin_down, query_places[:, None], key_places[None, :])


def local(queries, latents, latent_gain, w_ukv, w_o, residual, block_order):
    order_row = block_order[0]
    ctx, tp = lax.axis_index("ctx"), lax.axis_index("tp")
    tp_count = lax.axis_size("tp")
    tok_dev = queries.shape[1]
    block_len = tok_dev // 2
    lat_rows = latents.shape[1]
    width = w_o.shape[2]
    swap = [(0, 1), (1, 0)]

    own_places = place_rows(order_row, (ctx * tp_count + tp) * lat_rows, lat_rows, block_len)
    latent_rows = latents[0].astype(jnp.float32)
    compressed = latent_rows[:, :LATENT]
    scale_rows = lax.rsqrt(jnp.mean(compressed * compressed, axis=-1, keepdims=True) + 1e-06)
    normed = (compressed * scale_rows * latent_gain[0][None, :]).astype(jnp.bfloat16)
    own_rope = rotate(latent_rows[:, LATENT:], own_places).astype(jnp.bfloat16)
    gathered, masks = gather_keys(jnp.concatenate([normed, own_rope], axis=-1))
    gathered = jnp.pad(gathered, ((0, 0), (0, LANES - ROPE)))
    key_places = jnp.concatenate(
        [
            place_rows(order_row, ((ctx ^ c) * tp_count + (tp ^ t)) * lat_rows, lat_rows, block_len)
            for c, t in masks
        ]
    )
    query_places = place_rows(order_row, ctx * tok_dev, tok_dev, block_len)
    attention = attend(queries[0], gathered, w_ukv[0], query_places, key_places)

    last = tp_count - 1
    rows_out = tok_dev // tp_count
    out_weights = w_o[0]

    def row_block(array, dest, lo, size):
        return lax.dynamic_slice(array, (dest * rows_out, lo), (rows_out, size))

    def spans(unit):
        count = UNIT_PIECES.get(unit, 1)
        return [(i * width // count, width // count) for i in range(count)]

    first_dest = jnp.where(tp == 0, last, 0)
    first_rows = lax.dynamic_slice(attention, (first_dest * rows_out, 0), (rows_out, attention.shape[1]))
    got = {}

    def send(hop, value):
        return lax.ppermute(value, "tp", [(hop, hop + 1), (last - hop, last - hop - 1)])

    for lo, size in spans(0):
        part = jnp.dot(first_rows, out_weights[:, lo : lo + size], preferred_element_type=jnp.float32)
        got[0, 0, lo] = send(0, part.astype(jnp.bfloat16))
    terms = jnp.dot(attention, out_weights, preferred_element_type=jnp.float32).astype(jnp.bfloat16)
    ahead = lax.ppermute(
        row_block(terms, jnp.where(tp == 0, 1, last - 1), 0, width), "pp", swap
    )
    for unit in range(1, tp_count - 1):
        for lo, size in spans(unit):
            if unit == tp_count - 2:
                value = ahead[:, lo : lo + size]
            else:
                value = row_block(terms, jnp.where(tp == 0, last - unit, unit), lo, size)
            got[0, unit, lo] = send(0, value)
    for hop in range(1, tp_count - 1):
        for unit in range(0, tp_count - 1 - hop):
            for lo, size in spans(unit):
                value = row_block(terms, jnp.where(tp == hop, last - unit, unit), lo, size)
                got[hop, unit, lo] = send(hop, value + got[hop - 1, unit, lo])

    def ended(hop):
        unit = tp_count - 2 - hop
        here = (tp == hop + 1) | (tp == last - hop - 1)
        whole = jnp.concatenate([got[hop, unit, lo] for lo, _ in spans(unit)], axis=1)
        return jnp.where(here, whole.astype(jnp.float32), 0.0)

    mixed = row_block(terms, tp, 0, width).astype(jnp.float32) + residual[0].astype(jnp.float32)
    for hop in range(1, tp_count - 1):
        mixed = mixed + ended(hop)
    handed = lax.ppermute(mixed.astype(jnp.bfloat16), "pp", swap)
    return (handed.astype(jnp.float32) + ended(0)).astype(jnp.bfloat16)[None]


def solution(mesh):
    in_specs = (
        P("pp", "ctx", "tp"),
        P("pp", ("ctx", "tp"), None),
        P("pp", None),
        P("pp", None, "tp"),
        P("pp", "tp", None),
        P("pp", ("ctx", "tp"), None),
        P("pp", None),
    )
    out_specs = P("pp", ("ctx", "tp"), None)
    return jax.shard_map(local, mesh=mesh, in_specs=in_specs, out_specs=out_specs, check_vma=False)
```

time: 219 us -> 180 us (0.82)
  waiting for transfers between devices: 126 us -> 75.6 us
  starting transfers between devices: 1.55 us -> 30.9 us
  Pallas kernels: 0 us -> 22.1 us
  local copies, waits for them, and re-layouts: 19.6 us -> 5.64 us
  matrix products: 44 us -> 30.3 us
  between operations: 13.5 us -> 0.47 us
    reduce_scatter x1 -> x0, waiting for transfers between devices: 69.5 us -> none  [local(): lax.psum_scatter(jnp.dot(attention, out_weights, preferred_element_type=j...]
    ppermute x1 -> x17, waiting for transfers between devices: 20.7 us -> 75.6 us  [the longest x11 45.7 us: send(): lax.ppermute(value, 'tp', [(hop, hop + 1), (last - hop, last - hop - 1)])]
    all_gather x1 -> x0, waiting for transfers between devices: 35.7 us -> none  [local(): piece = lax.all_gather(own_keys, ('ctx', 'tp'), axis=0, tiled=True)]
    ppermute x1 -> x17, starting transfers between devices: 1.51 us -> 30.9 us  [the longest x11 24.7 us: send(): lax.ppermute(value, 'tp', [(hop, hop + 1), (last - hop, last - hop - 1)])]
    pallas_call x0 -> x1, Pallas kernels: none -> 22.1 us  [attend(): pl.pallas_call(attention_kernel, grid=(pairs,), out_shape=jax.ShapeDtypeS...]
    dot_general x4 -> x2, matrix products: 29.4 us -> 17 us  [local(): jnp.dot(first_rows, out_weights[:, lo:lo + size], preferred_element_type=...]
    unnamed x10 -> x13, local copies, waits for them, and re-layouts: 13.4 us -> 3.45 us
    reduce_sum x1 -> x0, other arithmetic: 8.72 us -> none  [local(): new_total = jnp.sum(weights, axis=-1)]
  transfers between devices with their start and end apart: 3 -> 17, of which waited for: 3 -> 14; matrix products, arithmetic and copies ran while one was open for 1% -> 8% of each run, Pallas kernels for 0% -> 0%
where the time goes in v1:
time: 180 us; the launch traced here: 178 us
  waiting for transfers between devices  75.6 us (42%)
  starting transfers between devices  30.9 us (17%)
  matrix products  30.3 us (17%)
  Pallas kernels  22.1 us (12%)
  other arithmetic  13 us (7%)
  local copies, waits for them, and re-layouts  5.64 us (3%)
    ppermute x11, waiting for transfers between devices, send(): lax.ppermute(value, 'tp', [(hop, hop + 1), (last - hop, last - hop - 1)])  45.7 us
    ppermute x11, starting transfers between devices, send(): lax.ppermute(value, 'tp', [(hop, hop + 1), (last - hop, last - hop - 1)])  24.7 us
    pallas_call x1, Pallas kernels, attend(): pl.pallas_call(attention_kernel, grid=(pairs,), out_shape=jax.ShapeDtypeS...  22.1 us
    dot_general x2, matrix products, local(): jnp.dot(first_rows, out_weights[:, lo:lo + size], preferred_element_type=...  17 us
    ppermute x1, waiting for transfers between devices, local(): handed = lax.ppermute(mixed.astype(jnp.bfloat16), 'pp', swap)  15.2 us
    ppermute x4, waiting for transfers between devices, gather_keys(): got = lax.ppermute(held, axis, pairs)  14.7 us
    dot_general x1, matrix products, local(): jnp.dot(attention, out_weights, preferred_element_type=jnp.float32)  13.4 us
  transfers between devices with their start and end apart: 17, of which 14 were waited for; matrix products, arithmetic and copies ran while one was open for 8% of the time, Pallas kernels for 0%

profile of v1, /device:TPU:16, one launch (start us, length us, event | category | flops | bytes accessed | tf_op | source)
XLA Modules:
  0.0 178.1 jit_solution(27911066323204662)
XLA Ops:
  0.1 0.8 select_reduce_fusion.1
  1.0 0.9 bitcast_convert_fusion
  2.0 0.2 fusion.27
  2.2 0.8 multiply_convert_fusion
  3.1 1.6 collective-permute-start
  4.7 0.7 select_reduce_fusion
  5.8 1.7 collective-permute-done
  7.6 6.3 %collective-permute-done.1 = bf16[128,576]{1,0:T(8,128)(2,1)S(1)} collective-permute-done((bf16[128,576]{1,0:T(8,128)(2,1)S(1)}, bf16[128,576]{1,0:T(8,128)(2,1)S(1)}, u32[]{:S(2)}, u32[]{:S(2)}) %collective-permute-start.1) | collective-permute-done | bytes 147488 | tf_op jit(solution)/shard_map/ppermute | solution.py:65
  14.0 1.4 collective-permute-start.2
  15.5 1.2 fusion.25
  16.7 6.1 %collective-permute-done.2 = bf16[256,576]{1,0:T(8,128)(2,1)S(1)} collective-permute-done((bf16[256,576]{1,0:T(8,128)(2,1)S(1)}, bf16[256,576]{1,0:T(8,128)(2,1)S(1)}, u32[]{:S(2)}, u32[]{:S(2)}) %collective-permute-start.2) | collective-permute-done | bytes 294944 | tf_op jit(solution)/shard_map/ppermute | solution.py:65
  22.9 0.2 copy.16
  23.4 1.2 maximum_maximum_fusion.2
  24.7 0.6 collective-permute-done.3
  25.3 1.4 copy.17
  26.9 1.2 copy-done.1
  28.1 2.2 %copy-done = bf16[1,512,4096]{2,1,0:T(8,128)(2,1)S(1)} copy-done((bf16[1,512,4096]{2,1,0:T(8,128)(2,1)S(1)}, bf16[1,512,4096]{2,1,0:T(8,128)(2,1)}, u32[]{:S(2)}) %copy-start) | copy-done | bytes 4194328
  30.3 22.1 %shard_map.73 = bf16[256,2048]{1,0:T(8,128)(2,1)S(1)} custom-call(bf16[256,3072]{1,0:T(8,128)(2,1)S(1)} %bitcast.20, bf16[1024,640]{1,0:T(8,128)(2,1)S(1)} %pad.4.lat_ref, bf16[512,4096]{1,0:T(8,128)(2,1)S(1)} %bitcast.19, f32[256,128]{1,0:T(8,128)S(1)} %get-tuple-element.41.cos_ref, f32[256,128]{1,0:T(8,128)S(1)} %get-tuple-element.35.sin_up_ref, ...), custom_call_target="tpu_custom_call" | custom-call | flops 8589934592 | bytes 7077888 | tf_op jit(solution)/shard_map/pallas_call | solution.py:134
  52.4 13.4 %convolution_convert_fusion = bf16[256,7168]{1,0:T(8,128)(2,1)S(1)} fusion(bf16[256,2048]{1,0:T(8,128)(2,1)S(1)} %shard_map.73, bf16[1,2048,7168]{2,1,0:T(8,128)(2,1)} %param.11), kind=kOutput, calls=%fused_computation.4 | convolution fusion | flops 7518027776 | bytes 34078720 | tf_op jit(solution)/shard_map/dot_general | solution.py:207
  65.8 9.1 %fusion.4 = bf16[64,3584]{1,0:T(8,128)(2,1)S(1)} fusion(bf16[2048,7168]{1,0:T(8,128)(2,1)} %bitcast.25, bf16[256,2048]{1,0:T(8,128)(2,1)S(1)} %shard_map.73, s32[]{:T(128)S(6)} %select_n.400), kind=kOutput, calls=%fused_computation.5 | convolution fusion | flops 939753472 | bytes 15400964 | tf_op jit(solution)/shard_map/dot_general | solution.py:205
  74.9 1.3 collective-permute-start.8
  76.2 7.8 %fusion.7 = bf16[64,3584]{1,0:T(8,128)(2,1)S(1)} fusion(bf16[2048,7168]{1,0:T(8,128)(2,1)} %bitcast.26, bf16[256,2048]{1,0:T(8,128)(2,1)S(1)} %shard_map.73, s32[]{:T(128)S(6)} %select_n.400), kind=kOutput, calls=%fused_computation.6 | convolution fusion | flops 939753472 | bytes 15400964 | tf_op jit(solution)/shard_map/dot_general | solution.py:205
  84.0 1.3 collective-permute-start.11
  85.3 6.9 %collective-permute-done.8 = bf16[64,3584]{1,0:T(8,128)(2,1)S(1)} collective-permute-done((bf16[64,3584]{1,0:T(8,128)(2,1)S(1)}, bf16[64,3584]{1,0:T(8,128)(2,1)S(1)}, u32[]{:S(2)}, u32[]{:S(2)}) %collective-permute-start.8) | collective-permute-done | bytes 458784 | tf_op jit(solution)/shard_map/ppermute | solution.py:202
  92.3 2.5 %collective-permute-start.9 = (bf16[64,3584]{1,0:T(8,128)(2,1)S(1)}, bf16[64,3584]{1,0:T(8,128)(2,1)S(1)}, u32[]{:S(2)}, u32[]{:S(2)}) collective-permute-start(bf16[64,3584]{1,0:T(8,128)(2,1)S(1)} %dynamic-slice_add_fusion.2), channel_id=1, source_target_pairs={{2,4},{4,2},{3,5},{5,3},{10,12},{12,10},{11,13},{13,11},{18,20},{2... | collective-permute-start | bytes 1376264 | tf_op jit(solution)/shard_map/ppermute | solution.py:202
  94.8 6.7 %collective-permute-done.11 = bf16[64,3584]{1,0:T(8,128)(2,1)S(1)} collective-permute-done((bf16[64,3584]{1,0:T(8,128)(2,1)S(1)}, bf16[64,3584]{1,0:T(8,128)(2,1)S(1)}, u32[]{:S(2)}, u32[]{:S(2)}) %collective-permute-start.11) | collective-permute-done | bytes 458784 | tf_op jit(solution)/shard_map/ppermute | solution.py:202
  101.5 4.2 %collective-permute-done.9 = bf16[64,3584]{1,0:T(8,128)(2,1)S(1)} collective-permute-done((bf16[64,3584]{1,0:T(8,128)(2,1)S(1)}, bf16[64,3584]{1,0:T(8,128)(2,1)S(1)}, u32[]{:S(2)}, u32[]{:S(2)}) %collective-permute-start.9) | collective-permute-done | bytes 458784 | tf_op jit(solution)/shard_map/ppermute | solution.py:202
  105.8 2.4 %dynamic-slice_add_fusion.3 = (bf16[64,3584]{1,0:T(8,128)(2,1)}, bf16[64,3584]{1,0:T(8,128)(2,1)S(1)}, bf16[64,3584]{1,0:T(8,128)(2,1)S(1)}, bf16[64,3584]{1,0:T(8,128)(2,1)S(1)}) fusion(bf16[64,3584]{1,0:T(8,128)(2,1)S(1)} %collective-permute-done.9, bf16[256,7168]{1,0:T(8,128)(2,1)} %copy-done.2, s32[]{:T(128)S(6)} %select_n.396, ...), kind=kLoop, calls=%fused_computation.17 | loop fusion | flops 1835008 | bytes 4587532 | tf_op jit(solution)/shard_map/add | solution.py:222
  108.2 2.2 %collective-permute-start.12 = (bf16[64,3584]{1,0:T(8,128)(2,1)S(1)}, bf16[64,3584]{1,0:T(8,128)(2,1)S(1)}, u32[]{:S(2)}, u32[]{:S(2)}) collective-permute-start(bf16[64,3584]{1,0:T(8,128)(2,1)S(1)} %get-tuple-element.26), channel_id=1, source_target_pairs={{2,4},{4,2},{3,5},{5,3},{10,12},{12,10},{11,13},{13,11},{18,20},{2... | collective-permute-start | bytes 1376264 | tf_op jit(solution)/shard_map/ppermute | solution.py:202
  110.4 1.3 collective-permute-start.6
  111.7 1.3 collective-permute-start.4
  113.1 1.6 collective-permute-start.15
  114.6 5.5 %collective-permute-start.10 = (bf16[64,3584]{1,0:T(8,128)(2,1)}, bf16[64,3584]{1,0:T(8,128)(2,1)}, u32[]{:S(2)}, u32[]{:S(2)}) collective-permute-start(bf16[64,3584]{1,0:T(8,128)(2,1)} %get-tuple-element.25), channel_id=1, source_target_pairs={{4,6},{2,0},{5,7},{3,1},{12,14},{10,8},{13,15},{11,9},{20,22},{18,... | collective-permute-start | bytes 1376264 | tf_op jit(solution)/shard_map/ppermute | solution.py:202
  120.1 0.6 collective-permute-done.12
  120.7 5.0 %collective-permute-done.6 = bf16[64,3584]{1,0:T(8,128)(2,1)S(1)} collective-permute-done((bf16[64,3584]{1,0:T(8,128)(2,1)S(1)}, bf16[64,3584]{1,0:T(8,128)(2,1)S(1)}, u32[]{:S(2)}, u32[]{:S(2)}) %collective-permute-start.6) | collective-permute-done | bytes 458784 | tf_op jit(solution)/shard_map/ppermute | solution.py:202
  125.7 6.7 %collective-permute-done.4 = bf16[64,3584]{1,0:T(8,128)(2,1)S(1)} collective-permute-done((bf16[64,3584]{1,0:T(8,128)(2,1)S(1)}, bf16[64,3584]{1,0:T(8,128)(2,1)S(1)}, u32[]{:S(2)}, u32[]{:S(2)}) %collective-permute-start.4) | collective-permute-done | bytes 458784 | tf_op jit(solution)/shard_map/ppermute | solution.py:202
  132.5 0.3 dynamic-slice_add_fusion.1
  132.8 2.3 %collective-permute-start.13 = (bf16[64,3584]{1,0:T(8,128)(2,1)S(1)}, bf16[64,3584]{1,0:T(8,128)(2,1)}, u32[]{:S(2)}, u32[]{:S(2)}) collective-permute-start(bf16[64,3584]{1,0:T(8,128)(2,1)S(1)} %get-tuple-element.29), channel_id=1, source_target_pairs={{4,6},{2,0},{5,7},{3,1},{12,14},{10,8},{13,15},{11,9},{20,22},{18,... | collective-permute-start | bytes 1376264 | tf_op jit(solution)/shard_map/ppermute | solution.py:202
  135.1 3.6 %collective-permute-start.7 = (bf16[64,3584]{1,0:T(8,128)(2,1)S(1)}, bf16[64,3584]{1,0:T(8,128)(2,1)}, u32[]{:S(2)}, u32[]{:S(2)}) collective-permute-start(bf16[64,3584]{1,0:T(8,128)(2,1)S(1)} %get-tuple-element.30), channel_id=1, source_target_pairs={{2,4},{4,2},{3,5},{5,3},{10,12},{12,10},{11,13},{13,11},{18,20},{2... | collective-permute-start | bytes 1376264 | tf_op jit(solution)/shard_map/ppermute | solution.py:202
  138.7 2.2 %collective-permute-start.5 = (bf16[64,3584]{1,0:T(8,128)(2,1)S(1)}, bf16[64,3584]{1,0:T(8,128)(2,1)}, u32[]{:S(2)}, u32[]{:S(2)}) collective-permute-start(bf16[64,3584]{1,0:T(8,128)(2,1)S(1)} %get-tuple-element.31), channel_id=1, source_target_pairs={{2,4},{4,2},{3,5},{5,3},{10,12},{12,10},{11,13},{13,11},{18,20},{2... | collective-permute-start | bytes 1376264 | tf_op jit(solution)/shard_map/ppermute | solution.py:202
  141.0 1.3 collective-permute-start.16
  142.3 8.3 %collective-permute-done.7 = bf16[64,3584]{1,0:T(8,128)(2,1)} collective-permute-done((bf16[64,3584]{1,0:T(8,128)(2,1)S(1)}, bf16[64,3584]{1,0:T(8,128)(2,1)}, u32[]{:S(2)}, u32[]{:S(2)}) %collective-permute-start.7) | collective-permute-done | bytes 458784 | tf_op jit(solution)/shard_map/ppermute | solution.py:202
  150.5 5.8 %collective-permute-done.5 = bf16[64,3584]{1,0:T(8,128)(2,1)} collective-permute-done((bf16[64,3584]{1,0:T(8,128)(2,1)S(1)}, bf16[64,3584]{1,0:T(8,128)(2,1)}, u32[]{:S(2)}, u32[]{:S(2)}) %collective-permute-start.5) | collective-permute-done | bytes 458784 | tf_op jit(solution)/shard_map/ppermute | solution.py:202
  156.3 2.3 %fusion.12 = bf16[64,7168]{1,0:T(8,128)(2,1)S(1)} fusion(bf16[64,3584]{1,0:T(8,128)(2,1)} %collective-permute-done.7, bf16[64,3584]{1,0:T(8,128)(2,1)} %collective-permute-done.5, bf16[64,3584]{1,0:T(8,128)(2,1)} %collective-permute-done.13, bf16[64,3584]{1,0:T(8,128)(2,1)} %collective-permute-done.10, bf16[1,64,7168]{2,1,0:T(8,128)(2,1)S(1)} %copy-done.4, ...), kind=kLoop, calls=%fused_computation.10 | loop fusion | flops 7340032 | bytes 4587526 | tf_op jit(solution)/shard_map/convert_element_type | solution.py:233
  158.6 1.6 collective-permute-start.14
  160.1 1.6 collective-permute-done.16
  161.7 15.2 %collective-permute-done.14 = bf16[64,7168]{1,0:T(8,128)(2,1)S(1)} collective-permute-done((bf16[64,7168]{1,0:T(8,128)(2,1)S(1)}, bf16[64,7168]{1,0:T(8,128)(2,1)S(1)}, u32[]{:S(2)}, u32[]{:S(2)}) %collective-permute-start.14) | collective-permute-done | bytes 917536 | tf_op jit(solution)/shard_map/ppermute | solution.py:233
  176.9 1.2 fusion.13
  (59 shorter events, 1.7 us)
Async XLA Ops:
  3.1 4.5 %collective-permute-start = (bf16[64,576]{1,0:T(8,128)(2,1)S(1)}, bf16[64,576]{1,0:T(8,128)(2,1)S(1)}, u32[]{:S(2)}, u32[]{:S(2)}) collective-permute-start(bf16[64,576]{1,0:T(8,128)(2,1)S(1)} %get-tuple-element.22), channel_id=1, source_target_pairs={{0,2},{2,0},{4,6},{6,4},{1,3},{3,1},{5,7},{7,5},{8,10},{10,8},{12,... | collective-permute-start | bytes 221192 | tf_op jit(solution)/shard_map/ppermute | solution.py:65
  7.6 6.3 %collective-permute-start.1 = (bf16[128,576]{1,0:T(8,128)(2,1)S(1)}, bf16[128,576]{1,0:T(8,128)(2,1)S(1)}, u32[]{:S(2)}, u32[]{:S(2)}) collective-permute-start(bf16[128,576]{1,0:T(8,128)(2,1)S(1)} %pad_maximum_fusion.2), channel_id=1, source_target_pairs={{0,4},{2,6},{4,0},{6,2},{1,5},{3,7},{5,1},{7,3},{8,12},{10,14},{12... | collective-permute-start | bytes 442376 | tf_op jit(solution)/shard_map/ppermute | solution.py:65
  14.0 8.8 %collective-permute-start.2 = (bf16[256,576]{1,0:T(8,128)(2,1)S(1)}, bf16[256,576]{1,0:T(8,128)(2,1)S(1)}, u32[]{:S(2)}, u32[]{:S(2)}) collective-permute-start(bf16[256,576]{1,0:T(8,128)(2,1)S(1)} %pad_maximum_fusion.1), channel_id=1, source_target_pairs={{0,16},{8,24},{16,0},{24,8},{1,17},{9,25},{17,1},{25,9},{2,18},{10... | collective-permute-start | bytes 884744 | tf_op jit(solution)/shard_map/ppermute | solution.py:65
  23.1 2.2 %collective-permute-start.3 = (bf16[512,576]{0,1:T(8,128)(2,1)S(1)}, bf16[512,576]{0,1:T(8,128)(2,1)}, u32[]{:S(2)}, u32[]{:S(2)}) collective-permute-start(bf16[512,576]{0,1:T(8,128)(2,1)S(1)} %copy.16), channel_id=1, source_target_pairs={{0,8},{8,0},{16,24},{24,16},{1,9},{9,1},{17,25},{25,17},{2,10},{10... | collective-permute-start | bytes 1769480 | tf_op jit(solution)/shard_map/ppermute | solution.py:65
  26.7 1.4 copy-start.1
  28.1 2.2 %copy-start = (bf16[1,512,4096]{2,1,0:T(8,128)(2,1)S(1)}, bf16[1,512,4096]{2,1,0:T(8,128)(2,1)}, u32[]{:S(2)}) copy-start(bf16[1,512,4096]{2,1,0:T(8,128)(2,1)} %param.10) | copy-start | bytes 12582916
  65.7 26.5 %copy-start.2 = (bf16[256,7168]{1,0:T(8,128)(2,1)}, bf16[256,7168]{1,0:T(8,128)(2,1)S(1)}, u32[]{:S(2)}) copy-start(bf16[256,7168]{1,0:T(8,128)(2,1)S(1)} %convolution_convert_fusion) | copy-start | bytes 11010052
  74.9 17.3 %collective-permute-start.8 = (bf16[64,3584]{1,0:T(8,128)(2,1)S(1)}, bf16[64,3584]{1,0:T(8,128)(2,1)S(1)}, u32[]{:S(2)}, u32[]{:S(2)}) collective-permute-start(bf16[64,3584]{1,0:T(8,128)(2,1)S(1)} %fusion.4), channel_id=1, source_target_pairs={{0,2},{6,4},{1,3},{7,5},{8,10},{14,12},{9,11},{15,13},{16,18},{22,... | collective-permute-start | bytes 1376264 | tf_op jit(solution)/shard_map/ppermute | solution.py:202
  84.0 17.5 %collective-permute-start.11 = (bf16[64,3584]{1,0:T(8,128)(2,1)S(1)}, bf16[64,3584]{1,0:T(8,128)(2,1)S(1)}, u32[]{:S(2)}, u32[]{:S(2)}) collective-permute-start(bf16[64,3584]{1,0:T(8,128)(2,1)S(1)} %fusion.7), channel_id=1, source_target_pairs={{0,2},{6,4},{1,3},{7,5},{8,10},{14,12},{9,11},{15,13},{16,18},{22,... | collective-permute-start | bytes 1376264 | tf_op jit(solution)/shard_map/ppermute | solution.py:202
  92.3 13.5 %collective-permute-start.9 = (bf16[64,3584]{1,0:T(8,128)(2,1)S(1)}, bf16[64,3584]{1,0:T(8,128)(2,1)S(1)}, u32[]{:S(2)}, u32[]{:S(2)}) collective-permute-start(bf16[64,3584]{1,0:T(8,128)(2,1)S(1)} %dynamic-slice_add_fusion.2), channel_id=1, source_target_pairs={{2,4},{4,2},{3,5},{5,3},{10,12},{12,10},{11,13},{13,11},{18,20},{2... | collective-permute-start | bytes 1376264 | tf_op jit(solution)/shard_map/ppermute | solution.py:202
  94.8 18.2 %copy-start.3 = (bf16[256,7168]{1,0:T(8,128)(2,1)S(1)}, bf16[256,7168]{1,0:T(8,128)(2,1)}, u32[]{:S(2)}) copy-start(bf16[256,7168]{1,0:T(8,128)(2,1)} %copy-done.2) | copy-start | bytes 11010052
  108.2 12.5 %collective-permute-start.12 = (bf16[64,3584]{1,0:T(8,128)(2,1)S(1)}, bf16[64,3584]{1,0:T(8,128)(2,1)S(1)}, u32[]{:S(2)}, u32[]{:S(2)}) collective-permute-start(bf16[64,3584]{1,0:T(8,128)(2,1)S(1)} %get-tuple-element.26), channel_id=1, source_target_pairs={{2,4},{4,2},{3,5},{5,3},{10,12},{12,10},{11,13},{13,11},{18,20},{2... | collective-permute-start | bytes 1376264 | tf_op jit(solution)/shard_map/ppermute | solution.py:202
  110.4 15.3 %collective-permute-start.6 = (bf16[64,3584]{1,0:T(8,128)(2,1)S(1)}, bf16[64,3584]{1,0:T(8,128)(2,1)S(1)}, u32[]{:S(2)}, u32[]{:S(2)}) collective-permute-start(bf16[64,3584]{1,0:T(8,128)(2,1)S(1)} %get-tuple-element.27), channel_id=1, source_target_pairs={{0,2},{6,4},{1,3},{7,5},{8,10},{14,12},{9,11},{15,13},{16,18},{22,... | collective-permute-start | bytes 1376264 | tf_op jit(solution)/shard_map/ppermute | solution.py:202
  111.7 20.8 %collective-permute-start.4 = (bf16[64,3584]{1,0:T(8,128)(2,1)S(1)}, bf16[64,3584]{1,0:T(8,128)(2,1)S(1)}, u32[]{:S(2)}, u32[]{:S(2)}) collective-permute-start(bf16[64,3584]{1,0:T(8,128)(2,1)S(1)} %get-tuple-element.28), channel_id=1, source_target_pairs={{0,2},{6,4},{1,3},{7,5},{8,10},{14,12},{9,11},{15,13},{16,18},{22,... | collective-permute-start | bytes 1376264 | tf_op jit(solution)/shard_map/ppermute | solution.py:202
  113.1 27.9 %collective-permute-start.15 = (bf16[64,7168]{1,0:T(8,128)(2,1)S(1)}, bf16[64,7168]{1,0:T(8,128)(2,1)}, u32[]{:S(2)}, u32[]{:S(2)}) collective-permute-start(bf16[64,7168]{1,0:T(8,128)(2,1)S(1)} %constant_dynamic-slice_fusion.1), channel_id=1, source_target_pairs={{0,1},{1,0},{2,3},{3,2},{4,5},{5,4},{6,7},{7,6},{8,9},{9,8},{10,11... | collective-permute-start | bytes 2752520 | tf_op jit(solution)/shard_map/ppermute | solution.py:208
  114.6 41.7 %copy-start.4 = (bf16[1,64,7168]{2,1,0:T(8,128)(2,1)S(1)}, bf16[1,64,7168]{2,1,0:T(8,128)(2,1)}, u32[]{:S(2)}) copy-start(bf16[1,64,7168]{2,1,0:T(8,128)(2,1)} %param.12) | copy-start | bytes 2752516
  114.6 27.6 %collective-permute-start.10 = (bf16[64,3584]{1,0:T(8,128)(2,1)}, bf16[64,3584]{1,0:T(8,128)(2,1)}, u32[]{:S(2)}, u32[]{:S(2)}) collective-permute-start(bf16[64,3584]{1,0:T(8,128)(2,1)} %get-tuple-element.25), channel_id=1, source_target_pairs={{4,6},{2,0},{5,7},{3,1},{12,14},{10,8},{13,15},{11,9},{20,22},{18,... | collective-permute-start | bytes 1376264 | tf_op jit(solution)/shard_map/ppermute | solution.py:202
  132.8 9.5 %collective-permute-start.13 = (bf16[64,3584]{1,0:T(8,128)(2,1)S(1)}, bf16[64,3584]{1,0:T(8,128)(2,1)}, u32[]{:S(2)}, u32[]{:S(2)}) collective-permute-start(bf16[64,3584]{1,0:T(8,128)(2,1)S(1)} %get-tuple-element.29), channel_id=1, source_target_pairs={{4,6},{2,0},{5,7},{3,1},{12,14},{10,8},{13,15},{11,9},{20,22},{18,... | collective-permute-start | bytes 1376264 | tf_op jit(solution)/shard_map/ppermute | solution.py:202
  135.1 15.4 %collective-permute-start.7 = (bf16[64,3584]{1,0:T(8,128)(2,1)S(1)}, bf16[64,3584]{1,0:T(8,128)(2,1)}, u32[]{:S(2)}, u32[]{:S(2)}) collective-permute-start(bf16[64,3584]{1,0:T(8,128)(2,1)S(1)} %get-tuple-element.30), channel_id=1, source_target_pairs={{2,4},{4,2},{3,5},{5,3},{10,12},{12,10},{11,13},{13,11},{18,20},{2... | collective-permute-start | bytes 1376264 | tf_op jit(solution)/shard_map/ppermute | solution.py:202
  138.7 17.6 %collective-permute-start.5 = (bf16[64,3584]{1,0:T(8,128)(2,1)S(1)}, bf16[64,3584]{1,0:T(8,128)(2,1)}, u32[]{:S(2)}, u32[]{:S(2)}) collective-permute-start(bf16[64,3584]{1,0:T(8,128)(2,1)S(1)} %get-tuple-element.31), channel_id=1, source_target_pairs={{2,4},{4,2},{3,5},{5,3},{10,12},{12,10},{11,13},{13,11},{18,20},{2... | collective-permute-start | bytes 1376264 | tf_op jit(solution)/shard_map/ppermute | solution.py:202
  141.0 20.8 %collective-permute-start.16 = (bf16[64,7168]{1,0:T(8,128)(2,1)}, bf16[64,7168]{1,0:T(8,128)(2,1)S(1)}, u32[]{:S(2)}, u32[]{:S(2)}) collective-permute-start(bf16[64,7168]{1,0:T(8,128)(2,1)} %collective-permute-done.15), channel_id=1, source_target_pairs={{0,2},{6,4},{1,3},{7,5},{8,10},{14,12},{9,11},{15,13},{16,18},{22,... | collective-permute-start | bytes 2752520 | tf_op jit(solution)/shard_map/ppermute | solution.py:202
  158.6 18.4 %collective-permute-start.14 = (bf16[64,7168]{1,0:T(8,128)(2,1)S(1)}, bf16[64,7168]{1,0:T(8,128)(2,1)S(1)}, u32[]{:S(2)}, u32[]{:S(2)}) collective-permute-start(bf16[64,7168]{1,0:T(8,128)(2,1)S(1)} %fusion.12), channel_id=1, source_target_pairs={{0,1},{1,0},{2,3},{3,2},{4,5},{5,4},{6,7},{7,6},{8,9},{9,8},{10,11... | collective-permute-start | bytes 2752520 | tf_op jit(solution)/shard_map/ppermute | solution.py:233

commit v2 on v0

v2 whole, which is shorter than its diff:
```python
import functools
import math

import jax
import jax.numpy as jnp
from jax import lax
from jax.experimental import pallas as pl
from jax.experimental.pallas import tpu as pltpu
from jax.sharding import PartitionSpec as P

NOPE = 128
ROPE = 64
VDIM = 128
LATENT = 512
LANES = 128

score_scale = 0.135
SCALE2 = score_scale * math.log2(math.e)

HEADS_STEP = 4
PIECES = 2


def angles_of(places):
    freqs = 10000.0 ** (-(jnp.arange(ROPE // 2).astype(jnp.float32) * 2.0 / ROPE))
    return places.astype(jnp.float32)[:, None] * freqs


def rotate(values, places):
    middle = values.shape[-1] // 2
    angles = angles_of(places)
    first_half = values[..., :middle]
    second_half = values[..., middle:]
    return jnp.concatenate(
        [
            first_half * jnp.cos(angles) - second_half * jnp.sin(angles),
            first_half * jnp.sin(angles) + second_half * jnp.cos(angles),
        ],
        axis=-1,
    )


def place_rows(order_row, first, count, block_len):
    row_ids = first + jnp.arange(count, dtype=jnp.int32)
    owners = row_ids // block_len
    table = jnp.arange(order_row.shape[0], dtype=jnp.int32)
    base = jnp.sum(jnp.where(owners[:, None] == table[None, :], order_row[None, :], 0), axis=1)
    return base * block_len + row_ids % block_len


def gather_keys(own_keys):
    tp_count, ctx_count = lax.axis_size("tp"), lax.axis_size("ctx")
    steps = [("tp", 1 << s) for s in range(tp_count.bit_length() - 1)]
    steps += [("ctx", 1 << s) for s in range(1, ctx_count.bit_length() - 1)]
    steps.append(("ctx", 1))
    halves, masks = (own_keys,), [(0, 0)]
    for axis, step in steps:
        held = halves[0] if len(halves) == 1 else jnp.concatenate(halves, axis=0)
        pairs = [(i, i ^ step) for i in range(lax.axis_size(axis))]
        halves = (held, lax.ppermute(held, axis, pairs))
        masks = masks + [
            (c ^ step, t) if axis == "ctx" else (c, t ^ step) for c, t in masks
        ]
    return halves, masks


def attention_kernel(
    slot_ref, q_ref, near_ref, far_ref, w_ref, cos_ref, sin_up_ref, sin_down_ref, qpos_ref, kpos_ref,
    out_ref, bias_ref,
):
    rows, half = q_ref.shape[0], near_ref.shape[0]
    heads = out_ref.shape[1] // VDIM
    blocks = slot_ref.shape[0]
    block = rows // blocks

    @pl.when(pl.program_id(0) == 0)
    def _():
        bias_ref[...] = jnp.where(kpos_ref[...] <= qpos_ref[...], 0.0, -1e30)

    produced, key_rope = [], []
    for part in (near_ref, far_ref):
        produced.append(
            jnp.dot(part[:, :LATENT], w_ref[...], preferred_element_type=jnp.float32).astype(jnp.bfloat16)
        )
        key_rope.append(
            jnp.concatenate([part[:, LATENT:], jnp.zeros((half, LANES - ROPE), jnp.bfloat16)], axis=1)
        )
    ones = jnp.ones((half, LANES), jnp.bfloat16)
    lane = lax.broadcasted_iota(jnp.int32, (rows, LANES), 1)

    def turned(x):
        return (
            x * cos_ref[...]
            + pltpu.roll(x, ROPE // 2, 1) * sin_up_ref[...]
            + pltpu.roll(x, LANES - ROPE // 2, 1) * sin_down_ref[...]
        ).astype(jnp.bfloat16)

    def query(h):
        base = (h // 2) * 2 * (NOPE + ROPE)
        middle = q_ref[:, base + LANES : base + 2 * LANES].astype(jnp.float32)
        if h % 2 == 0:
            return jnp.concatenate([q_ref[:, base : base + LANES], turned(middle)], axis=1)
        middle = pltpu.roll(middle, ROPE, 1)
        final = pltpu.roll(q_ref[:, base + 2 * LANES : base + 3 * LANES].astype(jnp.float32), ROPE, 1)
        nope = jnp.where(lane < ROPE, middle, final).astype(jnp.bfloat16)
        return jnp.concatenate([nope, turned(final)], axis=1)

    def scores(h):
        base = h * (NOPE + VDIM)
        q = query(h)
        return [
            lax.dot_general(
                q,
                jnp.concatenate([made[:, base : base + NOPE], rope], axis=1),
                (((1,), (1,)), ((), ())),
                preferred_element_type=jnp.float32,
            )
            for made, rope in zip(produced, key_rope)
        ]

    def weigh(found):
        found = [found[0] + bias_ref[:, :half], found[1] + bias_ref[:, half:]]
        top = jnp.max(jnp.maximum(found[0], found[1]), axis=1, keepdims=True)
        return [jnp.exp2((part - top) * SCALE2).astype(jnp.bfloat16) for part in found]

    def finish(h, weights):
        base = h * (NOPE + VDIM) + NOPE
        summed = sum(
            jnp.dot(
                part,
                jnp.concatenate([made[:, base : base + VDIM], ones], axis=1),
                preferred_element_type=jnp.float32,
            )
            for part, made in zip(weights, produced)
        )
        result = (summed[:, :VDIM] / summed[:, VDIM : VDIM + 1]).astype(out_ref.dtype)
        for dest in range(blocks):
            at = pl.multiple_of(slot_ref[dest] * block, block)
            out_ref[pl.ds(at, block), h * VDIM : (h + 1) * VDIM] = result[dest * block : (dest + 1) * block]

    found, weights = scores(0), None
    for h in range(heads):
        following = scores(h + 1) if h + 1 < heads else None
        now = weigh(found)
        if h > 0:
            finish(h - 1, weights)
        found, weights = following, now
    finish(heads - 1, weights)


def attend(queries, halves, up_weights, query_places, key_places, slots):
    rows, half = queries.shape[0], halves[0].shape[0]
    heads = queries.shape[1] // (NOPE + ROPE)
    angles = angles_of(query_places)
    cos, sin = jnp.cos(angles), jnp.sin(angles)
    zero, blank = jnp.zeros_like(cos), jnp.zeros((rows, LANES - ROPE), jnp.float32)
    cos_table = jnp.concatenate([cos, cos, blank], axis=1)
    sin_up = jnp.concatenate([zero, sin, blank], axis=1)
    sin_down = jnp.concatenate([-sin, zero, blank], axis=1)
    whole = lambda shape: pl.BlockSpec(shape, lambda i, s: (0, 0))
    along = lambda height, width: pl.BlockSpec((height, width), lambda i, s: (0, i))
    return pl.pallas_call(
        attention_kernel,
        out_shape=jax.ShapeDtypeStruct((rows, heads * VDIM), jnp.bfloat16),
        grid_spec=pltpu.PrefetchScalarGridSpec(
            num_scalar_prefetch=1,
            grid=(heads // HEADS_STEP,),
            in_specs=[
                along(rows, HEADS_STEP * (NOPE + ROPE)),
                whole(halves[0].shape),
                whole(halves[1].shape),
                along(LATENT, HEADS_STEP * (NOPE + VDIM)),
                whole((rows, LANES)),
                whole((rows, LANES)),
                whole((rows, LANES)),
                whole((rows, 1)),
                whole((1, 2 * half)),
            ],
            out_specs=along(rows, HEADS_STEP * VDIM),
            scratch_shapes=[pltpu.VMEM((rows, 2 * half), jnp.float32)],
        ),
        compiler_params=pltpu.CompilerParams(vmem_limit_bytes=56 * 1024 * 1024),
        cost_estimate=pl.CostEstimate(
            flops=4 * heads * half * (LATENT * 256 + rows * 512),
            bytes_accessed=2 * (queries.size + up_weights.size),
            transcendentals=2 * heads * rows * half,
        ),
    )(
        slots, queries, *halves, up_weights, cos_table, sin_up, sin_down,
        query_places[:, None], key_places[None, :],
    )


def project_kernel(x_ref, w_ref, *out_refs):
    block = out_refs[0].shape[0]
    made = jnp.dot(x_ref[...], w_ref[...], preferred_element_type=jnp.float32)
    for i, out in enumerate(out_refs):
        out[...] = made[i * block : (i + 1) * block].astype(out.dtype)


def project(rows, weights, lo, size, blocks):
    count, depth = rows.shape
    tile = max(t for t in range(LANES, 1024 + 1, LANES) if size % t == 0 and lo % t == 0)
    block = count // blocks
    return pl.pallas_call(
        project_kernel,
        grid=(size // tile,),
        out_shape=[jax.ShapeDtypeStruct((block, size), jnp.bfloat16)] * blocks,
        in_specs=[
            pl.BlockSpec((count, depth), lambda i: (0, 0)),
            pl.BlockSpec((depth, tile), lambda i: (0, i + lo // tile)),
        ],
        out_specs=[pl.BlockSpec((block, tile), lambda i: (0, i))] * blocks,
        compiler_params=pltpu.CompilerParams(vmem_limit_bytes=48 * 1024 * 1024),
        cost_estimate=pl.CostEstimate(
            flops=2 * count * depth * size, bytes_accessed=2 * depth * size, transcendentals=0
        ),
    )(rows, weights)


def add_kernel(always, count, flag_ref, *refs):
    total = refs[0][...].astype(jnp.float32)
    for ref in refs[1:always]:
        total = total + ref[...].astype(jnp.float32)
    for i, ref in enumerate(refs[always:count]):
        total = total + jnp.where(flag_ref[i] > 0, ref[...].astype(jnp.float32), 0.0)
    refs[-1][...] = total.astype(refs[-1].dtype)


def add_where(flags, values, flagged, earlier):
    count = len(values) + len(flagged)
    return pl.pallas_call(
        functools.partial(add_kernel, len(values), count),
        out_shape=jax.ShapeDtypeStruct(values[0].shape, jnp.bfloat16),
        in_specs=[pl.BlockSpec(memory_space=pltpu.SMEM)]
        + [pl.BlockSpec(memory_space=pltpu.VMEM)] * count
        + [pl.BlockSpec(memory_space=pl.ANY)] * len(earlier),
        out_specs=pl.BlockSpec(memory_space=pltpu.VMEM),
        compiler_params=pltpu.CompilerParams(vmem_limit_bytes=16 * 1024 * 1024),
    )(flags, *values, *flagged, *earlier)


def add_after(values, earlier):
    return add_where(jnp.ones((1,), jnp.int32), values, [], earlier)


def local(queries, latents, latent_gain, w_ukv, w_o, residual, block_order):
    order_row = block_order[0]
    ctx, tp = lax.axis_index("ctx"), lax.axis_index("tp")
    tp_count = lax.axis_size("tp")
    last = tp_count - 1
    tok_dev = queries.shape[1]
    block_len = tok_dev // 2
    lat_rows = latents.shape[1]
    width = w_o.shape[2]
    swap = [(0, 1), (1, 0)]

    own_places = place_rows(order_row, (ctx * tp_count + tp) * lat_rows, lat_rows, block_len)
    latent_rows = latents[0].astype(jnp.float32)
    compressed = latent_rows[:, :LATENT]
    scale_rows = lax.rsqrt(jnp.mean(compressed * compressed, axis=-1, keepdims=True) + 1e-06)
    normed = (compressed * scale_rows * latent_gain[0][None, :]).astype(jnp.bfloat16)
    own_rope = rotate(latent_rows[:, LATENT:], own_places).astype(jnp.bfloat16)
    halves, masks = gather_keys(jnp.concatenate([normed, own_rope], axis=-1))
    key_places = jnp.concatenate(
        [
            place_rows(order_row, ((ctx ^ c) * tp_count + (tp ^ t)) * lat_rows, lat_rows, block_len)
            for c, t in masks
        ]
    )
    query_places = place_rows(order_row, ctx * tok_dev, tok_dev, block_len)

    dests = jnp.arange(tp_count, dtype=jnp.int32)
    right_first = tp < tp_count // 2
    slots = jnp.where(
        dests == tp,
        last,
        jnp.where(
            right_first,
            jnp.where(dests > tp, last - dests, last - tp + dests),
            jnp.where(dests < tp, dests, tp + last - dests),
        ),
    )
    attention = attend(queries[0], halves, w_ukv[0], query_places, key_places, slots)

    def slot_of(hop, unit):
        return unit if 2 * hop < last else hop + unit

    def send(hop, value):
        return lax.ppermute(value, "tp", [(hop, hop + 1), (last - hop, last - hop - 1)])

    size = width // PIECES
    terms = [project(attention, w_o[0], i * size, size, tp_count) for i in range(PIECES)]
    got, ahead, sums = {}, {}, {}
    for i in range(PIECES):
        ahead[i] = lax.ppermute(terms[i][slot_of(0, last - 1)], "pp", swap)
        for unit in range(last):
            got[0, unit, i] = send(0, ahead[i] if unit == last - 1 else terms[i][slot_of(0, unit)])
    before = []
    for stage in range(1, last):
        for i in range(PIECES):
            sends = [(hop, stage - hop) for hop in range(1, stage + 1) if stage - hop < last - hop]
            arrived = [got[hop - 1, unit, i] for hop, unit in sends]
            if stage == 1:
                arrived.append(ahead[i])
            made = []
            for hop, unit in sends:
                own = terms[i][slot_of(hop, unit)]
                sums[hop, unit, i] = add_after([own, got[hop - 1, unit, i]], arrived + before)
                made.append(sums[hop, unit, i])
            for hop, unit in sends:
                got[hop, unit, i] = send(hop, sums[hop, unit, i])
            before = made

    outs = []
    for i in range(PIECES):
        kept = [terms[i][last], residual[0][:, i * size : (i + 1) * size]]
        ends = [(hop, last - 1 - hop) for hop in range(1, last)]
        flags = jnp.stack([(tp == hop + 1) | (tp == last - hop - 1) for hop, _ in ends]).astype(jnp.int32)
        arrived = [got[hop, unit, i] for hop, unit in ends]
        earlier = before + ([got[0, last - 1, i - 1]] if i > 0 else [])
        mixed = add_where(flags, kept, arrived, earlier)
        before = [mixed]
        handed = lax.ppermute(mixed, "pp", swap).astype(jnp.float32)
        here = (tp == 1) | (tp == last - 1)
        outs.append(handed + jnp.where(here, got[0, last - 1, i].astype(jnp.float32), 0.0))
    return jnp.concatenate(outs, axis=1).astype(jnp.bfloat16)[None]


def solution(mesh):
    in_specs = (
        P("pp", "ctx", "tp"),
        P("pp", ("ctx", "tp"), None),
        P("pp", None),
        P("pp", None, "tp"),
        P("pp", "tp", None),
        P("pp", ("ctx", "tp"), None),
        P("pp", None),
    )
    out_specs = P("pp", ("ctx", "tp"), None)
    return jax.shard_map(local, mesh=mesh, in_specs=in_specs, out_specs=out_specs, check_vma=False)
```

time: 219 us -> 134 us (0.61)
  waiting for transfers between devices: 126 us -> 51.4 us
  matrix products: 44 us -> 0 us
  Pallas kernels: 0 us -> 36.8 us
  starting transfers between devices: 1.55 us -> 29.1 us
  local copies, waits for them, and re-layouts: 19.6 us -> 6 us
  between operations: 13.5 us -> 0.58 us
  other arithmetic: 12.9 us -> 8.26 us
    reduce_scatter x1 -> x0, waiting for transfers between devices: 69.5 us -> none  [local(): lax.psum_scatter(jnp.dot(attention, out_weights, preferred_element_type=j...]
    dot_general x5 -> x0, matrix products: 44 us -> none  [the longest x1 14.6 us: local(): jnp.dot(attention, out_weights, preferred_element_type=jnp.float32)]
    pallas_call x0 -> x11, Pallas kernels: none -> 36.8 us  [the longest x2 17 us: project(): pl.pallas_call(project_kernel, grid=(size // tile,), out_shape=[jax.Shape...]
    all_gather x1 -> x0, waiting for transfers between devices: 35.7 us -> none  [local(): piece = lax.all_gather(own_keys, ('ctx', 'tp'), axis=0, tiled=True)]
    ppermute x1 -> x20, waiting for transfers between devices: 20.7 us -> 51.4 us  [the longest x12 28.6 us: send(): lax.ppermute(value, 'tp', [(hop, hop + 1), (last - hop, last - hop - 1)])]
    ppermute x1 -> x20, starting transfers between devices: 1.51 us -> 29.1 us  [the longest x12 22.7 us: send(): lax.ppermute(value, 'tp', [(hop, hop + 1), (last - hop, last - hop - 1)])]
    unnamed x10 -> x24, local copies, waits for them, and re-layouts: 13.4 us -> 3.71 us
    reduce_sum x1 -> x0, other arithmetic: 8.72 us -> none  [local(): new_total = jnp.sum(weights, axis=-1)]
  transfers between devices with their start and end apart: 3 -> 20, of which waited for: 3 -> 12; matrix products, arithmetic and copies ran while one was open for 1% -> 4% of each run, Pallas kernels for 0% -> 10%
where the time goes in v2:
time: 134 us; the launch traced here: 132 us
  waiting for transfers between devices  51.4 us (38%)
  Pallas kernels  36.8 us (27%)
  starting transfers between devices  29.1 us (22%)
  other arithmetic  8.26 us (6%)
  local copies, waits for them, and re-layouts  6 us (4%)
    ppermute x12, waiting for transfers between devices, send(): lax.ppermute(value, 'tp', [(hop, hop + 1), (last - hop, last - hop - 1)])  28.6 us
    ppermute x12, starting transfers between devices, send(): lax.ppermute(value, 'tp', [(hop, hop + 1), (last - hop, last - hop - 1)])  22.7 us
    pallas_call x2, Pallas kernels, project(): pl.pallas_call(project_kernel, grid=(size // tile,), out_shape=[jax.Shape...  17 us
    pallas_call x1, Pallas kernels, attend(): pl.pallas_call(attention_kernel, out_shape=jax.ShapeDtypeStruct((rows, he...  15.8 us
    ppermute x4, waiting for transfers between devices, gather_keys(): halves = (held, lax.ppermute(held, axis, pairs))  14.8 us
    ppermute x2, waiting for transfers between devices, local(): handed = lax.ppermute(mixed, 'pp', swap).astype(jnp.float32)  8.03 us
    pallas_call x8, Pallas kernels, add_where(): pl.pallas_call(functools.partial(add_kernel, len(values), count), out_sha...  4.02 us
    unnamed x24, local copies, waits for them, and re-layouts  3.71 us
  transfers between devices with their start and end apart: 20, of which 12 were waited for; matrix products, arithmetic and copies ran while one was open for 4% of the time, Pallas kernels for 10%

profile of v2, /device:TPU:16, one launch (start us, length us, event | category | flops | bytes accessed | tf_op | source)
XLA Modules:
  0.0 132.1 jit_solution(4096451019153219291)
XLA Ops:
  0.3 0.9 bitcast_convert_fusion
  1.4 0.8 select_reduce_fusion.1
  2.4 0.8 multiply_convert_fusion
  3.2 1.6 %collective-permute-start = (bf16[64,576]{1,0:T(8,128)(2,1)S(1)}, bf16[64,576]{1,0:T(8,128)(2,1)S(1)}, u32[]{:S(2)}, u32[]{:S(2)}) collective-permute-start(bf16[64,576]{1,0:T(8,128)(2,1)S(1)} %pad_maximum_fusion.4), channel_id=1, source_target_pairs={{0,2},{2,0},{4,6},{6,4},{1,3},{3,1},{5,7},{7,5},{8,10},{10,8},{12,... | collective-permute-start | bytes 221192 | tf_op jit(solution)/shard_map/ppermute | solution.py:60
  4.8 0.7 select_reduce_fusion
  5.7 2.0 %collective-permute-done = bf16[64,576]{1,0:T(8,128)(2,1)S(1)} collective-permute-done((bf16[64,576]{1,0:T(8,128)(2,1)S(1)}, bf16[64,576]{1,0:T(8,128)(2,1)S(1)}, u32[]{:S(2)}, u32[]{:S(2)}) %collective-permute-start) | collective-permute-done | bytes 73760 | tf_op jit(solution)/shard_map/ppermute | solution.py:60
  7.8 6.3 %collective-permute-done.1 = bf16[128,576]{1,0:T(8,128)(2,1)S(1)} collective-permute-done((bf16[128,576]{1,0:T(8,128)(2,1)S(1)}, bf16[128,576]{1,0:T(8,128)(2,1)S(1)}, u32[]{:S(2)}, u32[]{:S(2)}) %collective-permute-start.1) | collective-permute-done | bytes 147488 | tf_op jit(solution)/shard_map/ppermute | solution.py:60
  14.2 1.4 %collective-permute-start.2 = (bf16[256,576]{1,0:T(8,128)(2,1)S(1)}, bf16[256,576]{1,0:T(8,128)(2,1)S(1)}, u32[]{:S(2)}, u32[]{:S(2)}) collective-permute-start(bf16[256,576]{1,0:T(8,128)(2,1)S(1)} %pad_maximum_fusion.2), channel_id=1, source_target_pairs={{0,16},{8,24},{16,0},{24,8},{1,17},{9,25},{17,1},{25,9},{2,18},{10... | collective-permute-start | bytes 884744 | tf_op jit(solution)/shard_map/ppermute | solution.py:60
  15.8 0.7 fusion.3.qpos_ref
  16.5 6.4 %collective-permute-done.2 = bf16[256,576]{1,0:T(8,128)(2,1)S(1)} collective-permute-done((bf16[256,576]{1,0:T(8,128)(2,1)S(1)}, bf16[256,576]{1,0:T(8,128)(2,1)S(1)}, u32[]{:S(2)}, u32[]{:S(2)}) %collective-permute-start.2) | collective-permute-done | bytes 294944 | tf_op jit(solution)/shard_map/ppermute | solution.py:60
  23.5 0.7 concatenate.51
  25.3 0.9 maximum_maximum_fusion.2
  26.2 1.1 copy.18.far_ref
  27.3 15.8 %shard_map.73.x_ref = bf16[256,2048]{1,0:T(8,128)(2,1)} custom-call(s32[4]{0:T(128)} %compare_select_fusion.2.slot_ref, bf16[256,3072]{1,0:T(8,128)(2,1)} %bitcast.26, bf16[512,576]{1,0:T(8,128)(2,1)} %copy-done.10, bf16[512,576]{1,0:T(8,128)(2,1)} %copy.18.far_ref, bf16[512,4096]{1,0:T(8,128)(2,1)} %bitcast.25, f32[256,128]{1,0:T(8,128)} %get-tuple-element.50.cos_ref, ...), custom_call_target="tpu_custom_call" | custom-call | flops 8589934592 | bytes 5767168 | tf_op jit(solution)/shard_map/pallas_call | solution.py:162
  43.1 1.2 copy-done
  44.3 8.2 %shard_map.74 = (bf16[64,3584]{1,0:T(8,128)(2,1)S(1)}, bf16[64,3584]{1,0:T(8,128)(2,1)S(1)}, bf16[64,3584]{1,0:T(8,128)(2,1)S(1)}, bf16[64,3584]{1,0:T(8,128)(2,1)S(1)}) custom-call(bf16[256,2048]{1,0:T(8,128)(2,1)S(1)} %copy-done, bf16[2048,7168]{1,0:T(8,128)(2,1)} %bitcast.17), custom_call_target="tpu_custom_call" | custom-call | flops 3758096384 | bytes 14680064 | tf_op jit(solution)/shard_map/pallas_call | solution.py:205
  52.5 0.8 copy-done.6
  53.3 1.3 collective-permute-start.5
  54.6 1.1 collective-permute-start.6
  55.7 8.8 %shard_map.76 = (bf16[64,3584]{1,0:T(8,128)(2,1)S(1)}, bf16[64,3584]{1,0:T(8,128)(2,1)}, bf16[64,3584]{1,0:T(8,128)(2,1)S(1)}, bf16[64,3584]{1,0:T(8,128)(2,1)S(1)}) custom-call(bf16[256,2048]{1,0:T(8,128)(2,1)S(1)} %copy-done, bf16[2048,7168]{1,0:T(8,128)(2,1)} %bitcast.18), custom_call_target="tpu_custom_call" | custom-call | flops 3758096384 | bytes 14680064 | tf_op jit(solution)/shard_map/pallas_call | solution.py:205
  64.5 1.3 collective-permute-start.8
  65.7 1.1 collective-permute-start.9
  66.8 1.3 collective-permute-start.4
  68.1 2.4 %collective-permute-done.5.refs_1_.refs_2_ = bf16[64,3584]{1,0:T(8,128)(2,1)S(1)} collective-permute-done((bf16[64,3584]{1,0:T(8,128)(2,1)S(1)}, bf16[64,3584]{1,0:T(8,128)(2,1)S(1)}, u32[]{:S(2)}, u32[]{:S(2)}) %collective-permute-start.5) | collective-permute-done | bytes 458784 | tf_op jit(solution)/shard_map/ppermute | solution.py:290
  70.6 2.4 %collective-permute-start.7 = (bf16[64,3584]{1,0:T(8,128)(2,1)S(1)}, bf16[64,3584]{1,0:T(8,128)(2,1)S(1)}, u32[]{:S(2)}, u32[]{:S(2)}) collective-permute-start(bf16[64,3584]{1,0:T(8,128)(2,1)S(1)} %shard_map.75.refs_4_), channel_id=1, source_target_pairs={{2,4},{4,2},{3,5},{5,3},{10,12},{12,10},{11,13},{13,11},{18,20},{2... | collective-permute-start | bytes 1376264 | tf_op jit(solution)/shard_map/ppermute | solution.py:290
  73.0 1.3 collective-permute-start.12
  74.3 8.0 %collective-permute-done.8.refs_1_.refs_2_ = bf16[64,3584]{1,0:T(8,128)(2,1)S(1)} collective-permute-done((bf16[64,3584]{1,0:T(8,128)(2,1)S(1)}, bf16[64,3584]{1,0:T(8,128)(2,1)S(1)}, u32[]{:S(2)}, u32[]{:S(2)}) %collective-permute-start.8) | collective-permute-done | bytes 458784 | tf_op jit(solution)/shard_map/ppermute | solution.py:290
  82.4 0.7 copy-done.2
  83.1 2.7 %collective-permute-start.13 = (bf16[64,3584]{1,0:T(8,128)(2,1)S(1)}, bf16[64,3584]{1,0:T(8,128)(2,1)S(1)}, u32[]{:S(2)}, u32[]{:S(2)}) collective-permute-start(bf16[64,3584]{1,0:T(8,128)(2,1)S(1)} %shard_map.77.refs_4_), channel_id=1, source_target_pairs={{2,4},{4,2},{3,5},{5,3},{10,12},{12,10},{11,13},{13,11},{18,20},{2... | collective-permute-start | bytes 1376264 | tf_op jit(solution)/shard_map/ppermute | solution.py:290
  85.8 6.3 %collective-permute-done.4.refs_1_.refs_2_ = bf16[64,3584]{1,0:T(8,128)(2,1)S(1)} collective-permute-done((bf16[64,3584]{1,0:T(8,128)(2,1)S(1)}, bf16[64,3584]{1,0:T(8,128)(2,1)S(1)}, u32[]{:S(2)}, u32[]{:S(2)}) %collective-permute-start.4) | collective-permute-done | bytes 458784 | tf_op jit(solution)/shard_map/ppermute | solution.py:290
  92.2 2.4 %collective-permute-start.11 = (bf16[64,3584]{1,0:T(8,128)(2,1)S(1)}, bf16[64,3584]{1,0:T(8,128)(2,1)}, u32[]{:S(2)}, u32[]{:S(2)}) collective-permute-start(bf16[64,3584]{1,0:T(8,128)(2,1)S(1)} %shard_map.79.refs_5_), channel_id=1, source_target_pairs={{4,6},{2,0},{5,7},{3,1},{12,14},{10,8},{13,15},{11,9},{20,22},{18,... | collective-permute-start | bytes 1376264 | tf_op jit(solution)/shard_map/ppermute | solution.py:290
  94.7 2.7 %collective-permute-start.10 = (bf16[64,3584]{1,0:T(8,128)(2,1)S(1)}, bf16[64,3584]{1,0:T(8,128)(2,1)}, u32[]{:S(2)}, u32[]{:S(2)}) collective-permute-start(bf16[64,3584]{1,0:T(8,128)(2,1)S(1)} %shard_map.78.refs_4_), channel_id=1, source_target_pairs={{2,4},{4,2},{3,5},{5,3},{10,12},{12,10},{11,13},{13,11},{18,20},{2... | collective-permute-start | bytes 1376264 | tf_op jit(solution)/shard_map/ppermute | solution.py:290
  97.6 1.3 collective-permute-start.15
  98.9 3.1 %collective-permute-done.12.refs_1_.refs_2_ = bf16[64,3584]{1,0:T(8,128)(2,1)S(1)} collective-permute-done((bf16[64,3584]{1,0:T(8,128)(2,1)}, bf16[64,3584]{1,0:T(8,128)(2,1)S(1)}, u32[]{:S(2)}, u32[]{:S(2)}) %collective-permute-start.12) | collective-permute-done | bytes 458784 | tf_op jit(solution)/shard_map/ppermute | solution.py:290
  101.9 1.0 copy-done.9
  103.1 1.7 %collective-permute-start.17 = (bf16[64,3584]{1,0:T(8,128)(2,1)S(1)}, bf16[64,3584]{1,0:T(8,128)(2,1)S(1)}, u32[]{:S(2)}, u32[]{:S(2)}) collective-permute-start(bf16[64,3584]{1,0:T(8,128)(2,1)S(1)} %shard_map.81.refs_5_), channel_id=1, source_target_pairs={{4,6},{2,0},{5,7},{3,1},{12,14},{10,8},{13,15},{11,9},{20,22},{18,... | collective-permute-start | bytes 1376264 | tf_op jit(solution)/shard_map/ppermute | solution.py:290
  104.8 1.1 shard_map.80.refs_4_
  105.9 3.1 %collective-permute-start.16 = (bf16[64,3584]{1,0:T(8,128)(2,1)S(1)}, bf16[64,3584]{1,0:T(8,128)(2,1)S(1)}, u32[]{:S(2)}, u32[]{:S(2)}) collective-permute-start(bf16[64,3584]{1,0:T(8,128)(2,1)S(1)} %shard_map.80.refs_4_), channel_id=1, source_target_pairs={{2,4},{4,2},{3,5},{5,3},{10,12},{12,10},{11,13},{13,11},{18,20},{2... | collective-permute-start | bytes 1376264 | tf_op jit(solution)/shard_map/ppermute | solution.py:290
  109.1 1.5 %shard_map.82.refs_4_ = bf16[64,3584]{1,0:T(8,128)(2,1)S(1)} custom-call(s32[2]{0:T(128)S(1)} %add_convert_fusion.2.flag_ref, bf16[64,3584]{1,0:T(8,128)(2,1)S(1)} %copy-done.7, bf16[64,3584]{1,0:T(8,128)(2,1)S(1)} %get-tuple-element.39.refs_1_, bf16[64,3584]{1,0:T(8,128)(2,1)} %collective-permute-done.10.refs_2_, ...), custom_call_target="tpu_custom_call" | custom-call | tf_op jit(solution)/shard_map/pallas_call | solution.py:232
  110.6 0.6 collective-permute-start.14
  111.3 1.3 collective-permute-start.19
  112.6 1.6 %collective-permute-done.17.refs_3_ = bf16[64,3584]{1,0:T(8,128)(2,1)S(1)} collective-permute-done((bf16[64,3584]{1,0:T(8,128)(2,1)S(1)}, bf16[64,3584]{1,0:T(8,128)(2,1)S(1)}, u32[]{:S(2)}, u32[]{:S(2)}) %collective-permute-start.17) | collective-permute-done | bytes 458784 | tf_op jit(solution)/shard_map/ppermute | solution.py:290
  114.1 5.3 %collective-permute-done.16.refs_2_ = bf16[64,3584]{1,0:T(8,128)(2,1)S(1)} collective-permute-done((bf16[64,3584]{1,0:T(8,128)(2,1)S(1)}, bf16[64,3584]{1,0:T(8,128)(2,1)S(1)}, u32[]{:S(2)}, u32[]{:S(2)}) %collective-permute-start.16) | collective-permute-done | bytes 458784 | tf_op jit(solution)/shard_map/ppermute | solution.py:290
  119.4 0.8 shard_map.83
  120.2 0.6 collective-permute-start.18
  121.3 2.0 %collective-permute-done.19 = bf16[64,3584]{1,0:T(8,128)(2,1)S(1)} collective-permute-done((bf16[64,3584]{1,0:T(8,128)(2,1)S(1)}, bf16[64,3584]{1,0:T(8,128)(2,1)S(1)}, u32[]{:S(2)}, u32[]{:S(2)}) %collective-permute-start.19) | collective-permute-done | bytes 458784 | tf_op jit(solution)/shard_map/ppermute | solution.py:290
  123.3 7.7 %collective-permute-done.18 = bf16[64,3584]{1,0:T(8,128)(2,1)S(1)} collective-permute-done((bf16[64,3584]{1,0:T(8,128)(2,1)S(1)}, bf16[64,3584]{1,0:T(8,128)(2,1)S(1)}, u32[]{:S(2)}, u32[]{:S(2)}) %collective-permute-start.18) | collective-permute-done | bytes 458784 | tf_op jit(solution)/shard_map/ppermute | solution.py:324
  131.1 1.0 pad_maximum_fusion
  (81 shorter events, 4.0 us)
Async XLA Ops:
  3.2 4.4 %collective-permute-start = (bf16[64,576]{1,0:T(8,128)(2,1)S(1)}, bf16[64,576]{1,0:T(8,128)(2,1)S(1)}, u32[]{:S(2)}, u32[]{:S(2)}) collective-permute-start(bf16[64,576]{1,0:T(8,128)(2,1)S(1)} %pad_maximum_fusion.4), channel_id=1, source_target_pairs={{0,2},{2,0},{4,6},{6,4},{1,3},{3,1},{5,7},{7,5},{8,10},{10,8},{12,... | collective-permute-start | bytes 221192 | tf_op jit(solution)/shard_map/ppermute | solution.py:60
  7.8 6.3 %collective-permute-start.1 = (bf16[128,576]{1,0:T(8,128)(2,1)S(1)}, bf16[128,576]{1,0:T(8,128)(2,1)S(1)}, u32[]{:S(2)}, u32[]{:S(2)}) collective-permute-start(bf16[128,576]{1,0:T(8,128)(2,1)S(1)} %pad_maximum_fusion.3), channel_id=1, source_target_pairs={{0,4},{2,6},{4,0},{6,2},{1,5},{3,7},{5,1},{7,3},{8,12},{10,14},{12... | collective-permute-start | bytes 442376 | tf_op jit(solution)/shard_map/ppermute | solution.py:60
  14.2 8.8 %collective-permute-start.2 = (bf16[256,576]{1,0:T(8,128)(2,1)S(1)}, bf16[256,576]{1,0:T(8,128)(2,1)S(1)}, u32[]{:S(2)}, u32[]{:S(2)}) collective-permute-start(bf16[256,576]{1,0:T(8,128)(2,1)S(1)} %pad_maximum_fusion.2), channel_id=1, source_target_pairs={{0,16},{8,24},{16,0},{24,8},{1,17},{9,25},{17,1},{25,9},{2,18},{10... | collective-permute-start | bytes 884744 | tf_op jit(solution)/shard_map/ppermute | solution.py:60
  23.1 3.2 %copy-start.10 = (bf16[512,576]{1,0:T(8,128)(2,1)}, bf16[512,576]{1,0:T(8,128)(2,1)S(1)}, u32[]{:S(2)}) copy-start(bf16[512,576]{1,0:T(8,128)(2,1)S(1)} %pad_maximum_fusion.1.near_ref) | copy-start | bytes 1769476
  23.3 2.9 %collective-permute-start.3 = (bf16[512,576]{0,1:T(8,128)(2,1)S(1)}, bf16[512,576]{0,1:T(8,128)(2,1)S(1)}, u32[]{:S(2)}, u32[]{:S(2)}) collective-permute-start(bf16[512,576]{0,1:T(8,128)(2,1)S(1)} %copy.16), channel_id=1, source_target_pairs={{0,8},{8,0},{16,24},{24,16},{1,9},{9,1},{17,25},{25,17},{2,10},{10... | collective-permute-start | bytes 1769480 | tf_op jit(solution)/shard_map/ppermute | solution.py:60
  43.1 1.2 copy-start
  52.5 0.8 copy-start.6
  53.3 17.2 %collective-permute-start.5 = (bf16[64,3584]{1,0:T(8,128)(2,1)S(1)}, bf16[64,3584]{1,0:T(8,128)(2,1)S(1)}, u32[]{:S(2)}, u32[]{:S(2)}) collective-permute-start(bf16[64,3584]{1,0:T(8,128)(2,1)S(1)} %get-tuple-element.15.refs_0_), channel_id=1, source_target_pairs={{0,2},{6,4},{1,3},{7,5},{8,10},{14,12},{9,11},{15,13},{16,18},{22,... | collective-permute-start | bytes 1376264 | tf_op jit(solution)/shard_map/ppermute | solution.py:290
  54.6 15.9 %collective-permute-start.6 = (bf16[64,3584]{1,0:T(8,128)(2,1)S(1)}, bf16[64,3584]{1,0:T(8,128)(2,1)S(1)}, u32[]{:S(2)}, u32[]{:S(2)}) collective-permute-start(bf16[64,3584]{1,0:T(8,128)(2,1)S(1)} %get-tuple-element.16.refs_0_), channel_id=1, source_target_pairs={{0,1},{1,0},{2,3},{3,2},{4,5},{5,4},{6,7},{7,6},{8,9},{9,8},{10,11... | collective-permute-start | bytes 1376264 | tf_op jit(solution)/shard_map/ppermute | solution.py:296
  64.4 17.9 %copy-start.4 = (bf16[64,3584]{1,0:T(8,128)(2,1)}, bf16[64,3584]{1,0:T(8,128)(2,1)S(1)}, u32[]{:S(2)}) copy-start(bf16[64,3584]{1,0:T(8,128)(2,1)S(1)} %get-tuple-element.20.refs_0_) | copy-start | bytes 1376260
  64.4 17.9 %copy-start.8 = (bf16[64,3584]{1,0:T(8,128)(2,1)}, bf16[64,3584]{1,0:T(8,128)(2,1)S(1)}, u32[]{:S(2)}) copy-start(bf16[64,3584]{1,0:T(8,128)(2,1)S(1)} %get-tuple-element.18.refs_0_) | copy-start | bytes 1376260
  64.5 17.8 %collective-permute-start.8 = (bf16[64,3584]{1,0:T(8,128)(2,1)S(1)}, bf16[64,3584]{1,0:T(8,128)(2,1)S(1)}, u32[]{:S(2)}, u32[]{:S(2)}) collective-permute-start(bf16[64,3584]{1,0:T(8,128)(2,1)S(1)} %get-tuple-element.17.refs_0_), channel_id=1, source_target_pairs={{0,2},{6,4},{1,3},{7,5},{8,10},{14,12},{9,11},{15,13},{16,18},{22,... | collective-permute-start | bytes 1376264 | tf_op jit(solution)/shard_map/ppermute | solution.py:290
  65.7 16.5 %collective-permute-start.9 = (bf16[64,3584]{1,0:T(8,128)(2,1)S(1)}, bf16[64,3584]{1,0:T(8,128)(2,1)S(1)}, u32[]{:S(2)}, u32[]{:S(2)}) collective-permute-start(bf16[64,3584]{1,0:T(8,128)(2,1)S(1)} %get-tuple-element.18.refs_0_), channel_id=1, source_target_pairs={{0,1},{1,0},{2,3},{3,2},{4,5},{5,4},{6,7},{7,6},{8,9},{9,8},{10,11... | collective-permute-start | bytes 1376264 | tf_op jit(solution)/shard_map/ppermute | solution.py:296
  66.8 25.3 %collective-permute-start.4 = (bf16[64,3584]{1,0:T(8,128)(2,1)S(1)}, bf16[64,3584]{1,0:T(8,128)(2,1)S(1)}, u32[]{:S(2)}, u32[]{:S(2)}) collective-permute-start(bf16[64,3584]{1,0:T(8,128)(2,1)S(1)} %get-tuple-element.14.refs_0_), channel_id=1, source_target_pairs={{0,2},{6,4},{1,3},{7,5},{8,10},{14,12},{9,11},{15,13},{16,18},{22,... | collective-permute-start | bytes 1376264 | tf_op jit(solution)/shard_map/ppermute | solution.py:290
  70.5 11.9 %copy-start.1 = (bf16[64,3584]{1,0:T(8,128)(2,1)}, bf16[64,3584]{1,0:T(8,128)(2,1)S(1)}, u32[]{:S(2)}) copy-start(bf16[64,3584]{1,0:T(8,128)(2,1)S(1)} %collective-permute-done.6.refs_3_) | copy-start | bytes 1376260
  70.6 21.5 %collective-permute-start.7 = (bf16[64,3584]{1,0:T(8,128)(2,1)S(1)}, bf16[64,3584]{1,0:T(8,128)(2,1)S(1)}, u32[]{:S(2)}, u32[]{:S(2)}) collective-permute-start(bf16[64,3584]{1,0:T(8,128)(2,1)S(1)} %shard_map.75.refs_4_), channel_id=1, source_target_pairs={{2,4},{4,2},{3,5},{5,3},{10,12},{12,10},{11,13},{13,11},{18,20},{2... | collective-permute-start | bytes 1376264 | tf_op jit(solution)/shard_map/ppermute | solution.py:290
  73.0 28.9 %collective-permute-start.12 = (bf16[64,3584]{1,0:T(8,128)(2,1)}, bf16[64,3584]{1,0:T(8,128)(2,1)S(1)}, u32[]{:S(2)}, u32[]{:S(2)}) collective-permute-start(bf16[64,3584]{1,0:T(8,128)(2,1)} %get-tuple-element.19.refs_0_), channel_id=1, source_target_pairs={{0,2},{6,4},{1,3},{7,5},{8,10},{14,12},{9,11},{15,13},{16,18},{22,... | collective-permute-start | bytes 1376264 | tf_op jit(solution)/shard_map/ppermute | solution.py:290
  82.3 0.8 copy-start.2
  83.1 18.9 %collective-permute-start.13 = (bf16[64,3584]{1,0:T(8,128)(2,1)S(1)}, bf16[64,3584]{1,0:T(8,128)(2,1)S(1)}, u32[]{:S(2)}, u32[]{:S(2)}) collective-permute-start(bf16[64,3584]{1,0:T(8,128)(2,1)S(1)} %shard_map.77.refs_4_), channel_id=1, source_target_pairs={{2,4},{4,2},{3,5},{5,3},{10,12},{12,10},{11,13},{13,11},{18,20},{2... | collective-permute-start | bytes 1376264 | tf_op jit(solution)/shard_map/ppermute | solution.py:290
  92.2 5.2 %copy-start.11 = (bf16[1,64,7168]{2,1,0:T(8,128)(2,1)S(1)}, bf16[1,64,7168]{2,1,0:T(8,128)(2,1)}, u32[]{:S(2)}) copy-start(bf16[1,64,7168]{2,1,0:T(8,128)(2,1)} %param.12) | copy-start | bytes 2752516
  92.2 16.8 %collective-permute-start.11 = (bf16[64,3584]{1,0:T(8,128)(2,1)S(1)}, bf16[64,3584]{1,0:T(8,128)(2,1)}, u32[]{:S(2)}, u32[]{:S(2)}) collective-permute-start(bf16[64,3584]{1,0:T(8,128)(2,1)S(1)} %shard_map.79.refs_5_), channel_id=1, source_target_pairs={{4,6},{2,0},{5,7},{3,1},{12,14},{10,8},{13,15},{11,9},{20,22},{18,... | collective-permute-start | bytes 1376264 | tf_op jit(solution)/shard_map/ppermute | solution.py:290
  94.7 14.4 %collective-permute-start.10 = (bf16[64,3584]{1,0:T(8,128)(2,1)S(1)}, bf16[64,3584]{1,0:T(8,128)(2,1)}, u32[]{:S(2)}, u32[]{:S(2)}) collective-permute-start(bf16[64,3584]{1,0:T(8,128)(2,1)S(1)} %shard_map.78.refs_4_), channel_id=1, source_target_pairs={{2,4},{4,2},{3,5},{5,3},{10,12},{12,10},{11,13},{13,11},{18,20},{2... | collective-permute-start | bytes 1376264 | tf_op jit(solution)/shard_map/ppermute | solution.py:290
  97.6 15.0 %collective-permute-start.15 = (bf16[64,3584]{1,0:T(8,128)(2,1)}, bf16[64,3584]{1,0:T(8,128)(2,1)S(1)}, u32[]{:S(2)}, u32[]{:S(2)}) collective-permute-start(bf16[64,3584]{1,0:T(8,128)(2,1)} %copy-done.1), channel_id=1, source_target_pairs={{0,2},{6,4},{1,3},{7,5},{8,10},{14,12},{9,11},{15,13},{16,18},{22,... | collective-permute-start | bytes 1376264 | tf_op jit(solution)/shard_map/ppermute | solution.py:290
  101.9 1.0 copy-start.9
  103.1 6.0 %copy-start.7 = (bf16[64,3584]{1,0:T(8,128)(2,1)S(1)}, bf16[64,3584]{1,0:T(8,128)(2,1)}, u32[]{:S(2)}) copy-start(bf16[64,3584]{1,0:T(8,128)(2,1)} %copy-done.6) | copy-start | bytes 1376260
  103.1 11.0 %collective-permute-start.17 = (bf16[64,3584]{1,0:T(8,128)(2,1)S(1)}, bf16[64,3584]{1,0:T(8,128)(2,1)S(1)}, u32[]{:S(2)}, u32[]{:S(2)}) collective-permute-start(bf16[64,3584]{1,0:T(8,128)(2,1)S(1)} %shard_map.81.refs_5_), channel_id=1, source_target_pairs={{4,6},{2,0},{5,7},{3,1},{12,14},{10,8},{13,15},{11,9},{20,22},{18,... | collective-permute-start | bytes 1376264 | tf_op jit(solution)/shard_map/ppermute | solution.py:290
  105.9 13.5 %collective-permute-start.16 = (bf16[64,3584]{1,0:T(8,128)(2,1)S(1)}, bf16[64,3584]{1,0:T(8,128)(2,1)S(1)}, u32[]{:S(2)}, u32[]{:S(2)}) collective-permute-start(bf16[64,3584]{1,0:T(8,128)(2,1)S(1)} %shard_map.80.refs_4_), channel_id=1, source_target_pairs={{2,4},{4,2},{3,5},{5,3},{10,12},{12,10},{11,13},{13,11},{18,20},{2... | collective-permute-start | bytes 1376264 | tf_op jit(solution)/shard_map/ppermute | solution.py:290
  109.1 2.2 %copy-start.3 = (bf16[64,3584]{1,0:T(8,128)(2,1)S(1)}, bf16[64,3584]{1,0:T(8,128)(2,1)}, u32[]{:S(2)}) copy-start(bf16[64,3584]{1,0:T(8,128)(2,1)} %copy-done.2) | copy-start | bytes 1376260
  109.1 10.3 %copy-start.5 = (bf16[64,3584]{1,0:T(8,128)(2,1)S(1)}, bf16[64,3584]{1,0:T(8,128)(2,1)}, u32[]{:S(2)}) copy-start(bf16[64,3584]{1,0:T(8,128)(2,1)} %copy-done.4) | copy-start | bytes 1376260
  110.6 10.5 %collective-permute-start.14 = (bf16[64,3584]{1,0:T(8,128)(2,1)S(1)}, bf16[64,3584]{1,0:T(8,128)(2,1)S(1)}, u32[]{:S(2)}, u32[]{:S(2)}) collective-permute-start(bf16[64,3584]{1,0:T(8,128)(2,1)S(1)} %shard_map.82.refs_4_), channel_id=1, source_target_pairs={{0,1},{1,0},{2,3},{3,2},{4,5},{5,4},{6,7},{7,6},{8,9},{9,8},{10,11... | collective-permute-start | bytes 1376264 | tf_op jit(solution)/shard_map/ppermute | solution.py:324
  111.3 12.1 %collective-permute-start.19 = (bf16[64,3584]{1,0:T(8,128)(2,1)S(1)}, bf16[64,3584]{1,0:T(8,128)(2,1)S(1)}, u32[]{:S(2)}, u32[]{:S(2)}) collective-permute-start(bf16[64,3584]{1,0:T(8,128)(2,1)S(1)} %copy-done.3), channel_id=1, source_target_pairs={{0,2},{6,4},{1,3},{7,5},{8,10},{14,12},{9,11},{15,13},{16,18},{22,... | collective-permute-start | bytes 1376264 | tf_op jit(solution)/shard_map/ppermute | solution.py:290
  120.2 10.8 %collective-permute-start.18 = (bf16[64,3584]{1,0:T(8,128)(2,1)S(1)}, bf16[64,3584]{1,0:T(8,128)(2,1)S(1)}, u32[]{:S(2)}, u32[]{:S(2)}) collective-permute-start(bf16[64,3584]{1,0:T(8,128)(2,1)S(1)} %shard_map.83), channel_id=1, source_target_pairs={{0,1},{1,0},{2,3},{3,2},{4,5},{5,4},{6,7},{7,6},{8,9},{9,8},{10,11... | collective-permute-start | bytes 1376264 | tf_op jit(solution)/shard_map/ppermute | solution.py:324

commit v3 on v0

v3 whole, which is shorter than its diff:
```python
import functools
import math

import jax
import jax.numpy as jnp
import numpy as np
from jax import lax
from jax.experimental import pallas as pl
from jax.experimental.pallas import tpu as pltpu
from jax.sharding import PartitionSpec as P

NOPE = 128
ROPE = 64
VDIM = 128
LATENT = 512
LANES = 128

score_scale = 0.135
SCALE2 = score_scale * math.log2(math.e)

HEADS_STEP = 4
MIB = 1024 * 1024
PREPARE_VMEM = 16 * MIB
PROJECT_VMEM = 24 * MIB
ATTEND_VMEM = 48 * MIB
ADD_VMEM = 8 * MIB
FINAL_FLOPS = 2 * 10**10
PIECES = 2


def row_places(order_ref, first, count, block_len):
    return order_ref[first // block_len] * block_len + first % block_len


def rope_tables(places):
    lane = lax.broadcasted_iota(jnp.int32, (places.shape[0], LANES), 1)
    angles = places.astype(jnp.float32) * lane_freqs()
    cos, sin = jnp.cos(angles), jnp.sin(angles)
    half = ROPE // 2
    return (
        jnp.where(lane < ROPE, cos, 0.0),
        jnp.where((lane >= half) & (lane < ROPE), sin, 0.0),
        jnp.where(lane < half, -sin, 0.0),
    )


def turned(x, cos, sin_up, sin_down):
    half = ROPE // 2
    return (
        x * cos + pltpu.roll(x, half, 1) * sin_up + pltpu.roll(x, LANES - half, 1) * sin_down
    ).astype(jnp.bfloat16)


def lane_freqs():
    half = ROPE // 2
    lane = lax.broadcasted_iota(jnp.int32, (1, LANES), 1) % half
    freqs = jnp.zeros((1, LANES), jnp.float32)
    for j in range(half):
        freqs = jnp.where(lane == j, np.float32(10000.0 ** (-2.0 * j / ROPE)), freqs)
    return freqs


def own_keys_kernel(block_len, order_ref, latent_ref, gain_ref, out_ref):
    rows = latent_ref.shape[0]
    first = (lax.axis_index("ctx") * lax.axis_size("tp") + lax.axis_index("tp")) * rows
    places = row_places(order_ref, first, rows, block_len) + lax.broadcasted_iota(jnp.int32, (rows, 1), 0)
    compressed = latent_ref[:, :LATENT].astype(jnp.float32)
    scale_rows = lax.rsqrt(jnp.mean(compressed * compressed, axis=-1, keepdims=True) + 1e-06)
    out_ref[:, :LATENT] = (compressed * scale_rows * gain_ref[...]).astype(jnp.bfloat16)
    rope = jnp.concatenate(
        [latent_ref[:, LATENT:].astype(jnp.float32), jnp.zeros((rows, LANES - ROPE), jnp.float32)], axis=1
    )
    out_ref[:, LATENT:] = turned(rope, *rope_tables(places))


def own_keys(order_row, latents, gain, block_len):
    return pl.pallas_call(
        functools.partial(own_keys_kernel, block_len),
        out_shape=jax.ShapeDtypeStruct((latents.shape[0], LATENT + LANES), jnp.bfloat16),
        in_specs=[pl.BlockSpec(memory_space=pltpu.SMEM)] + [pl.BlockSpec(memory_space=pltpu.VMEM)] * 2,
        out_specs=pl.BlockSpec(memory_space=pltpu.VMEM),
        compiler_params=pltpu.CompilerParams(vmem_limit_bytes=60 * MIB),
    )(order_row, latents, gain)


def join_kernel(count, *refs):
    at = 0
    for ref in refs[:count]:
        refs[-1][at : at + ref.shape[0], :] = ref[...]
        at += ref.shape[0]


def join_after(arrays, earlier):
    rows = sum(array.shape[0] for array in arrays)
    return pl.pallas_call(
        functools.partial(join_kernel, len(arrays)),
        out_shape=jax.ShapeDtypeStruct((rows, arrays[0].shape[1]), arrays[0].dtype),
        in_specs=[pl.BlockSpec(memory_space=pltpu.VMEM)] * len(arrays)
        + [pl.BlockSpec(memory_space=pl.ANY)] * len(earlier),
        out_specs=pl.BlockSpec(memory_space=pltpu.VMEM),
        compiler_params=pltpu.CompilerParams(vmem_limit_bytes=16 * 1024 * 1024),
    )(*arrays, *earlier)


def gather_masks():
    masks = [(0, 0)]
    for s in range(lax.axis_size("tp").bit_length() - 1):
        masks = masks + [(c, t ^ (1 << s)) for c, t in masks]
    for s in list(range(1, lax.axis_size("ctx").bit_length() - 1)) + [0]:
        masks = masks + [(c ^ (1 << s), t) for c, t in masks]
    return masks


def gather_keys(own, earlier):
    tp_count, ctx_count = lax.axis_size("tp"), lax.axis_size("ctx")

    def traded(value, axis, step):
        return lax.ppermute(value, axis, [(i, i ^ step) for i in range(lax.axis_size(axis))])

    pieces = [own]
    for s in range(tp_count.bit_length() - 1):
        held = own if s == 0 else join_after(pieces, [])
        pieces = [held, traded(held, "tp", 1 << s)]
    pieces[-1] = join_after(pieces[-1:], earlier)
    for s in list(range(1, ctx_count.bit_length() - 1)) + [0]:
        pieces = pieces + [traded(piece, "ctx", 1 << s) for piece in pieces]
    return pieces


def prepare_kernel(block_len, key_rows, masks, order_ref, q_hbm, out_ref, bias_ref, q_ref, semaphore):
    rows = q_ref.shape[0]
    fetch = pltpu.make_async_copy(q_hbm, q_ref, semaphore)
    fetch.start()
    tp_count = lax.axis_size("tp")
    ctx, tp = lax.axis_index("ctx"), lax.axis_index("tp")
    row = lax.broadcasted_iota(jnp.int32, (rows, 1), 0)
    places = jnp.zeros((rows, 1), jnp.int32)
    for b in range(rows // block_len):
        base = row_places(order_ref, ctx * rows + b * block_len, block_len, block_len)
        places = jnp.where(row // block_len == b, base + row % block_len, places)
    lane = lax.broadcasted_iota(jnp.int32, (1, LANES), 1)
    group = LANES // key_rows
    for g in range(len(masks) // group):
        keys = jnp.zeros((1, LANES), jnp.int32)
        for j in range(group):
            c, t = masks[g * group + j]
            base = row_places(order_ref, ((ctx ^ c) * tp_count + (tp ^ t)) * key_rows, key_rows, block_len)
            keys = jnp.where(lane // key_rows == j, base + lane % key_rows, keys)
        bias_ref[:, g * LANES : (g + 1) * LANES] = jnp.where(keys <= places, 0.0, -1e30)
    tables = rope_tables(places)
    lane = lax.broadcasted_iota(jnp.int32, (rows, LANES), 1)
    fetch.wait()
    per_step = HEADS_STEP // 2
    for pair in range(q_ref.shape[1] // (3 * LANES)):
        step, base, to = pair // per_step, pair * 3 * LANES, pair % per_step * 4 * LANES
        middle = q_ref[:, base + LANES : base + 2 * LANES].astype(jnp.float32)
        out_ref[step, :, to : to + LANES] = q_ref[:, base : base + LANES]
        out_ref[step, :, to + LANES : to + 2 * LANES] = turned(middle, *tables)
        middle = pltpu.roll(middle, ROPE, 1)
        final = pltpu.roll(q_ref[:, base + 2 * LANES : base + 3 * LANES].astype(jnp.float32), ROPE, 1)
        nope = jnp.where(lane < ROPE, middle, final).astype(jnp.bfloat16)
        out_ref[step, :, to + 2 * LANES : to + 3 * LANES] = nope
        out_ref[step, :, to + 3 * LANES : to + 4 * LANES] = turned(final, *tables)


def prepare(order_row, queries, key_rows, masks, block_len):
    rows = queries.shape[0]
    heads = queries.shape[1] // (NOPE + ROPE)
    key_count = key_rows * len(masks)
    return pl.pallas_call(
        functools.partial(prepare_kernel, block_len, key_rows, masks),
        out_shape=[
            jax.ShapeDtypeStruct((heads // HEADS_STEP, rows, HEADS_STEP * 2 * LANES), jnp.bfloat16),
            jax.ShapeDtypeStruct((rows, key_count), jnp.float32),
        ],
        in_specs=[
            pl.BlockSpec(memory_space=pltpu.SMEM),
            pl.BlockSpec(memory_space=pltpu.HBM),
        ],
        out_specs=[pl.BlockSpec(memory_space=pltpu.VMEM)] * 2,
        scratch_shapes=[pltpu.VMEM(queries.shape, queries.dtype), pltpu.SemaphoreType.DMA],
        compiler_params=pltpu.CompilerParams(vmem_limit_bytes=PREPARE_VMEM),
        cost_estimate=pl.CostEstimate(flops=20 * queries.size, bytes_accessed=6 * queries.size, transcendentals=0),
    )(order_row, queries)


def slot_of_dest(dest):
    tp, last = lax.axis_index("tp"), lax.axis_size("tp") - 1
    right_first = jnp.where(dest > tp, last - dest, last - tp + dest)
    left_first = jnp.where(dest < tp, dest, tp + last - dest)
    return jnp.where(dest == tp, last, jnp.where(2 * tp <= last, right_first, left_first))


def attention_kernel(piece_count, steps, *refs):
    q_ref, bias_ref, w_ref, out_w_ref = refs[:4]
    piece_refs = refs[4 : 4 + piece_count]
    rest_refs = refs[4 + piece_count :]
    attention_ref, term_refs = rest_refs[0], rest_refs[1:-4]
    keys_ref, held_ref, columns_ref, semaphores = rest_refs[-4:]
    step = pl.program_id(0)
    block = q_ref.shape[1] // len(term_refs)
    tiles, _, tile = columns_ref.shape

    def column_copy(i):
        return pltpu.make_async_copy(
            out_w_ref.at[:, pl.ds(i * tile, tile)], columns_ref.at[i], semaphores.at[i]
        )

    @pl.when(step == 0)
    def _():
        for i in range(tiles):
            column_copy(i).start()
        at = 0
        for ref in piece_refs:
            keys_ref[at : at + ref.shape[0], :] = ref[...]
            at += ref.shape[0]

    @pl.when(step < steps)
    def _():
        attend_heads(step, q_ref, bias_ref, w_ref, keys_ref, held_ref, len(term_refs))

    @pl.when(step == steps)
    def _():
        wide = held_ref.shape[2]
        for i in range(steps):
            attention_ref[:, i * wide : (i + 1) * wide] = held_ref[i]
        for i in range(tiles):
            column_copy(i).wait()

    @pl.when(step >= steps)
    def _():
        made = jnp.dot(attention_ref[...], columns_ref[step - steps], preferred_element_type=jnp.float32)
        for i, out in enumerate(term_refs):
            out[...] = made[i * block : (i + 1) * block].astype(out.dtype)


def attend_heads(step, q_ref, bias_ref, w_ref, keys_ref, held_ref, blocks):
    half = keys_ref.shape[0] // 2
    block = q_ref.shape[1] // blocks
    produced = [
        jnp.dot(
            keys_ref[part * half : (part + 1) * half, :LATENT], w_ref[...], preferred_element_type=jnp.float32
        ).astype(jnp.bfloat16)
        for part in range(2)
    ]
    key_rope = [keys_ref[part * half : (part + 1) * half, LATENT:] for part in range(2)]
    ones = jnp.ones((half, LANES), jnp.bfloat16)

    def scores(h):
        base = h * (NOPE + VDIM)
        return [
            lax.dot_general(
                q_ref[step, :, h * 2 * LANES : (h + 1) * 2 * LANES],
                jnp.concatenate([made[:, base : base + NOPE], rope], axis=1),
                (((1,), (1,)), ((), ())),
                preferred_element_type=jnp.float32,
            )
            for made, rope in zip(produced, key_rope)
        ]

    def weigh(found):
        found = [found[0] + bias_ref[:, :half], found[1] + bias_ref[:, half:]]
        top = jnp.max(jnp.maximum(found[0], found[1]), axis=1, keepdims=True)
        return [jnp.exp2((part - top) * SCALE2).astype(jnp.bfloat16) for part in found]

    def finish(h, weights):
        base = h * (NOPE + VDIM) + NOPE
        summed = sum(
            jnp.dot(
                part,
                jnp.concatenate([made[:, base : base + VDIM], ones], axis=1),
                preferred_element_type=jnp.float32,
            )
            for part, made in zip(weights, produced)
        )
        result = (summed[:, :VDIM] / summed[:, VDIM : VDIM + 1]).astype(held_ref.dtype)
        for dest in range(blocks):
            at = pl.multiple_of(slot_of_dest(dest) * block, block)
            held_ref[step, pl.ds(at, block), h * VDIM : (h + 1) * VDIM] = result[dest * block : (dest + 1) * block]

    found, weights = scores(0), None
    for h in range(HEADS_STEP):
        following = scores(h + 1) if h + 1 < HEADS_STEP else None
        now = weigh(found)
        if h > 0:
            finish(h - 1, weights)
        found, weights = following, now
    finish(HEADS_STEP - 1, weights)


def column_tile(lo, size, most):
    return max(t for t in range(LANES, most + 1, LANES) if size % t == 0 and lo % t == 0)


def attend(queries, bias, pieces, up_weights, out_weights, size, blocks):
    rows, key_count = bias.shape
    steps = queries.shape[0]
    heads = steps * HEADS_STEP
    depth = heads * VDIM
    tile = column_tile(0, size, 1024)
    head_step = lambda i: jnp.minimum(i, steps - 1)
    column_step = lambda i: jnp.maximum(i - steps, 0)
    whole = lambda shape: pl.BlockSpec(shape, lambda i: (0, 0))
    return pl.pallas_call(
        functools.partial(attention_kernel, len(pieces), steps),
        grid=(steps + size // tile,),
        out_shape=[
            jax.ShapeDtypeStruct((rows, depth), jnp.bfloat16),
        ]
        + [jax.ShapeDtypeStruct((rows // blocks, size), jnp.bfloat16)] * blocks,
        in_specs=[
            pl.BlockSpec(memory_space=pltpu.VMEM),
            pl.BlockSpec(memory_space=pltpu.VMEM),
            pl.BlockSpec((LATENT, HEADS_STEP * (NOPE + VDIM)), lambda i: (0, head_step(i))),
            pl.BlockSpec(memory_space=pltpu.HBM),
        ]
        + [pl.BlockSpec(memory_space=pltpu.VMEM)] * len(pieces),
        out_specs=[pl.BlockSpec(memory_space=pltpu.VMEM)]
        + [pl.BlockSpec((rows // blocks, tile), lambda i: (0, column_step(i)))] * blocks,
        scratch_shapes=[
            pltpu.VMEM((key_count, LATENT + LANES), jnp.bfloat16),
            pltpu.VMEM((steps, rows, HEADS_STEP * VDIM), jnp.bfloat16),
            pltpu.VMEM((size // tile, depth, tile), jnp.bfloat16),
            pltpu.SemaphoreType.DMA((size // tile,)),
        ],
        compiler_params=pltpu.CompilerParams(vmem_limit_bytes=ATTEND_VMEM),
        cost_estimate=pl.CostEstimate(
            flops=2 * heads * key_count * (LATENT * 256 + rows * 512) + 2 * rows * depth * size,
            bytes_accessed=2 * (queries.size + up_weights.size + depth * size),
            transcendentals=heads * rows * key_count,
        ),
    )(queries, bias, up_weights, out_weights, *pieces)


def project_kernel(x_ref, upper_ref, lower_ref, *out_refs):
    block, half = out_refs[0].shape[0], upper_ref.shape[0]
    made = jnp.dot(x_ref[:, :half], upper_ref[...], preferred_element_type=jnp.float32)
    made = made + jnp.dot(x_ref[:, half:], lower_ref[...], preferred_element_type=jnp.float32)
    for i, out in enumerate(out_refs):
        out[...] = made[i * block : (i + 1) * block].astype(out.dtype)


def project(rows, weights, lo, size, blocks):
    count, depth = rows.shape
    tile = column_tile(lo, size, 1024)
    block = count // blocks
    return pl.pallas_call(
        project_kernel,
        grid=(size // tile,),
        out_shape=[jax.ShapeDtypeStruct((block, size), jnp.bfloat16)] * blocks,
        in_specs=[
            pl.BlockSpec((count, depth), lambda i: (0, 0)),
            pl.BlockSpec((depth // 2, tile), lambda i: (0, i + lo // tile)),
            pl.BlockSpec((depth // 2, tile), lambda i: (1, i + lo // tile)),
        ],
        out_specs=[pl.BlockSpec((block, tile), lambda i: (0, i))] * blocks,
        compiler_params=pltpu.CompilerParams(vmem_limit_bytes=PROJECT_VMEM),
        cost_estimate=pl.CostEstimate(
            flops=2 * count * depth * size, bytes_accessed=2 * depth * size, transcendentals=0
        ),
    )(rows, weights, weights)


def total_of(refs, flag_ref, always):
    total = jnp.zeros(refs[0].shape, jnp.float32)
    for i, ref in enumerate(refs):
        value = ref[...].astype(jnp.float32)
        total = total + (value if i < always else jnp.where(flag_ref[i - always] > 0, value, 0.0))
    return total.astype(jnp.bfloat16)


def add_kernel(count, *refs):
    refs[-1][...] = total_of(refs[:count], None, count)


def add_after(values, earlier):
    return pl.pallas_call(
        functools.partial(add_kernel, len(values)),
        out_shape=jax.ShapeDtypeStruct(values[0].shape, jnp.bfloat16),
        in_specs=[pl.BlockSpec(memory_space=pltpu.VMEM)] * len(values)
        + [pl.BlockSpec(memory_space=pl.ANY)] * len(earlier),
        out_specs=pl.BlockSpec(memory_space=pltpu.VMEM),
        compiler_params=pltpu.CompilerParams(vmem_limit_bytes=ADD_VMEM),
    )(*values, *earlier)


def pair_kernel(own_ref, rest_ref, unit_ref, out_ref):
    rows = own_ref.shape[0]
    out_ref[:rows, :] = total_of([own_ref, rest_ref], None, 2)
    out_ref[rows:, :] = unit_ref[...]


def pair_up(own, rest, unit):
    rows, size = own.shape
    return pl.pallas_call(
        pair_kernel,
        out_shape=jax.ShapeDtypeStruct((2 * rows, size), jnp.bfloat16),
        in_specs=[pl.BlockSpec(memory_space=pltpu.VMEM)] * 3,
        out_specs=pl.BlockSpec(memory_space=pltpu.VMEM),
        compiler_params=pltpu.CompilerParams(vmem_limit_bytes=ADD_VMEM),
    )(own, rest, unit)


def finish_kernel(count, flag_ref, pair_ref, *refs):
    rows = refs[-1].shape[0]
    refs[-1][...] = total_of([pair_ref.at[:rows, :], *refs[:count]], flag_ref, 1)


def finish(flags, pair, flagged, piece, pieces, before):
    rows, size = flagged[0].shape
    operands = [flags, pair, *flagged] + before
    return pl.pallas_call(
        functools.partial(finish_kernel, len(flagged)),
        grid=(1,),
        out_shape=jax.ShapeDtypeStruct((rows, size * pieces), jnp.bfloat16),
        in_specs=[pl.BlockSpec(memory_space=pltpu.SMEM)]
        + [pl.BlockSpec(memory_space=pltpu.VMEM)] * (1 + len(flagged))
        + [pl.BlockSpec(memory_space=pl.ANY)] * len(before),
        out_specs=pl.BlockSpec((rows, size), lambda i: (0, piece)),
        input_output_aliases={len(operands) - 1: 0} if before else {},
        compiler_params=pltpu.CompilerParams(vmem_limit_bytes=ADD_VMEM),
        cost_estimate=pl.CostEstimate(flops=FINAL_FLOPS, bytes_accessed=0, transcendentals=0),
    )(*operands)


def local(queries, latents, latent_gain, w_ukv, w_o, residual, block_order):
    tp = lax.axis_index("tp")
    tp_count = lax.axis_size("tp")
    last = tp_count - 1
    tok_dev, lat_rows, width = queries.shape[1], latents.shape[1], w_o.shape[2]
    order_row = block_order[0]
    block_len = tok_dev * lax.axis_size("ctx") // order_row.shape[0]
    size = width // PIECES

    turned_queries, bias = prepare(order_row, queries[0], lat_rows, gather_masks(), block_len)
    pieces = gather_keys(own_keys(order_row, latents[0], latent_gain, block_len), [turned_queries, bias])
    attention, *first_terms = attend(turned_queries, bias, pieces, w_ukv[0], w_o[0], size, tp_count)

    def slot_of(hop, unit):
        return unit if 2 * hop < last else hop + unit

    def send(hop, value, across):
        steps = [(hop, hop + 1), (last - hop, last - hop - 1)]
        if not across:
            return lax.ppermute(value, "tp", steps)
        return lax.ppermute(
            value, ("tp", "pp"), [(2 * i + p, 2 * j + 1 - p) for i, j in steps for p in range(2)]
        )

    def flags_of(*conditions):
        return jnp.stack(conditions).astype(jnp.int32)

    terms = [first_terms] + [project(attention, w_o[0], i * size, size, tp_count) for i in range(1, PIECES)]
    got, ahead = {}, {}
    for i in range(PIECES):
        for unit in range(last - 1):
            got[0, unit, i] = send(0, terms[i][slot_of(0, unit)], False)
        rest = residual[0][:, i * size : (i + 1) * size]
        both = pair_up(terms[i][last], rest, terms[i][slot_of(0, last - 1)])
        ahead[i] = lax.ppermute(both, "pp", [(0, 1), (1, 0)])
        got[0, last - 1, i] = send(0, ahead[i][rest.shape[0] :], False)
    before = []
    for stage in range(1, last):
        for i in range(PIECES):
            for hop in range(stage, 0, -1):
                unit = stage - hop
                if unit >= last - hop:
                    continue
                if (stage, hop, i) == (2, 1, 0):
                    before = before + [ahead[0]]
                summed = add_after([terms[i][slot_of(hop, unit)], got[hop - 1, unit, i]], before)
                before = [summed]
                got[hop, unit, i] = send(hop, summed, unit == last - 1 - hop)

    flags = flags_of(*[(tp == hop + 1) | (tp == last - hop - 1) for hop in range(last)])
    out = []
    for i in range(PIECES):
        ended = [got[hop, last - 1 - hop, i] for hop in range(last)]
        out = [finish(flags, ahead[i], ended, i, PIECES, out)]
    return out[0][None]


def solution(mesh):
    in_specs = (
        P("pp", "ctx", "tp"),
        P("pp", ("ctx", "tp"), None),
        P("pp", None),
        P("pp", None, "tp"),
        P("pp", "tp", None),
        P("pp", ("ctx", "tp"), None),
        P("pp", None),
    )
    out_specs = P("pp", ("ctx", "tp"), None)
    return jax.shard_map(local, mesh=mesh, in_specs=in_specs, out_specs=out_specs, check_vma=False)
```

time: 219 us -> 117 us (0.53)
  waiting for transfers between devices: 126 us -> 31.2 us
  matrix products: 44 us -> 0 us
  Pallas kernels: 0 us -> 39.7 us
  starting transfers between devices: 1.55 us -> 38.4 us
  between operations: 13.5 us -> 0.28 us
  local copies, waits for them, and re-layouts: 19.6 us -> 6.67 us
  other arithmetic: 12.9 us -> 0.08 us
    reduce_scatter x1 -> x0, waiting for transfers between devices: 69.5 us -> none  [local(): lax.psum_scatter(jnp.dot(attention, out_weights, preferred_element_type=j...]
    dot_general x5 -> x0, matrix products: 44 us -> none  [the longest x1 14.6 us: local(): jnp.dot(attention, out_weights, preferred_element_type=jnp.float32)]
    pallas_call x0 -> x16, Pallas kernels: none -> 39.7 us  [the longest x1 19.7 us: attend(): pl.pallas_call(functools.partial(attention_kernel, len(pieces), steps), g...]
    ppermute x1 -> x22, starting transfers between devices: 1.51 us -> 38.4 us  [the longest x8 16.2 us: send(): return lax.ppermute(value, 'tp', steps)]
    all_gather x1 -> x0, waiting for transfers between devices: 35.7 us -> none  [local(): piece = lax.all_gather(own_keys, ('ctx', 'tp'), axis=0, tiled=True)]
    ppermute x1 -> x22, waiting for transfers between devices: 20.7 us -> 31.2 us  [the longest x8 16.2 us: send(): return lax.ppermute(value, 'tp', steps)]
    reduce_sum x5 -> x0, other arithmetic: 9.74 us -> none  [the longest x1 8.72 us: local(): new_total = jnp.sum(weights, axis=-1)]
    unnamed x10 -> x14, local copies, waits for them, and re-layouts: 13.4 us -> 4.75 us
  transfers between devices with their start and end apart: 3 -> 22, of which waited for: 3 -> 11; matrix products, arithmetic and copies ran while one was open for 1% -> 2% of each run, Pallas kernels for 0% -> 14%
where the time goes in v3:
time: 117 us; the launch traced here: 116 us
  Pallas kernels  39.7 us (34%)
  starting transfers between devices  38.4 us (33%)
  waiting for transfers between devices  31.2 us (27%)
  local copies, waits for them, and re-layouts  6.67 us (6%)
    pallas_call x1, Pallas kernels, attend(): pl.pallas_call(functools.partial(attention_kernel, len(pieces), steps), g...  19.7 us
    ppermute x8, starting transfers between devices, send(): return lax.ppermute(value, 'tp', steps)  16.2 us
    ppermute x8, waiting for transfers between devices, send(): return lax.ppermute(value, 'tp', steps)  16.2 us
    ppermute x4, starting transfers between devices, send(): lax.ppermute(value, ('tp', 'pp'), [(2 * i + p, 2 * j + 1 - p) for i, j in...  15 us
    ppermute x8, waiting for transfers between devices, traded(): lax.ppermute(value, axis, [(i, i ^ step) for i in range(lax.axis_size(axi...  9.49 us
    pallas_call x1, Pallas kernels, project(): pl.pallas_call(project_kernel, grid=(size // tile,), out_shape=[jax.Shape...  8.85 us
    ppermute x4, waiting for transfers between devices, send(): lax.ppermute(value, ('tp', 'pp'), [(2 * i + p, 2 * j + 1 - p) for i, j in...  5.51 us
    ppermute x8, starting transfers between devices, traded(): lax.ppermute(value, axis, [(i, i ^ step) for i in range(lax.axis_size(axi...  5.09 us
  transfers between devices with their start and end apart: 22, of which 11 were waited for; matrix products, arithmetic and copies ran while one was open for 2% of the time, Pallas kernels for 14%

profile of v3, /device:TPU:16, one launch (start us, length us, event | category | flops | bytes accessed | tf_op | source)
XLA Modules:
  0.0 116.3 jit_solution(13338992814693135668)
XLA Ops:
  0.0 1.7 %shard_map.74.refs_0_ = bf16[64,640]{1,0:T(8,128)(2,1)} custom-call(s32[8]{0:T(128)} %bitcast.10, bf16[64,576]{1,0:T(8,128)(2,1)} %bitcast.16, f32[1,512]{1,0:T(1,128)} %gain_ref.1), custom_call_target="tpu_custom_call" | custom-call | tf_op jit(solution)/shard_map/pallas_call | solution.py:77
  1.7 1.6 %collective-permute-start = (bf16[64,640]{1,0:T(8,128)(2,1)}, bf16[64,640]{1,0:T(8,128)(2,1)S(1)}, u32[]{:S(2)}, u32[]{:S(2)}) collective-permute-start(bf16[64,640]{1,0:T(8,128)(2,1)} %shard_map.74.refs_0_), channel_id=1, source_target_pairs={{0,2},{2,0},{4,6},{6,4},{1,3},{3,1},{5,7},{7,5},{8,10},{10,8},{12,... | collective-permute-start | bytes 245768 | tf_op jit(solution)/shard_map/ppermute | solution.py:118
  3.3 3.1 %collective-permute-done.refs_1_ = bf16[64,640]{1,0:T(8,128)(2,1)S(1)} collective-permute-done((bf16[64,640]{1,0:T(8,128)(2,1)}, bf16[64,640]{1,0:T(8,128)(2,1)S(1)}, u32[]{:S(2)}, u32[]{:S(2)}) %collective-permute-start) | collective-permute-done | bytes 81952 | tf_op jit(solution)/shard_map/ppermute | solution.py:118
  6.4 0.9 copy-done.4
  7.4 1.4 %copy-done.1 = bf16[1,256,3072]{2,1,0:T(8,128)(2,1)S(1)} copy-done((bf16[1,256,3072]{2,1,0:T(8,128)(2,1)S(1)}, bf16[1,256,3072]{2,1,0:T(8,128)(2,1)}, u32[]{:S(2)}) %copy-start.1) | copy-done | bytes 1572888
  8.8 0.7 copy-done.5
  9.4 2.8 %shard_map.73 = (bf16[4,256,1024]{2,1,0:T(8,128)(2,1)S(1)}, f32[256,1024]{1,0:T(8,128)S(1)}) custom-call(s32[8]{0:T(128)S(1)} %bitcast.11, bf16[256,3072]{1,0:T(8,128)(2,1)S(1)} %bitcast.9), custom_call_target="tpu_custom_call" | custom-call | flops 15728640 | bytes 4718592 | tf_op jit(solution)/shard_map/pallas_call | solution.py:170
  12.2 1.9 %collective-permute-start.2 = (bf16[128,640]{1,0:T(8,128)(2,1)S(1)}, bf16[128,640]{1,0:T(8,128)(2,1)S(1)}, u32[]{:S(2)}, u32[]{:S(2)}) collective-permute-start(bf16[128,640]{1,0:T(8,128)(2,1)S(1)} %shard_map.75.refs_4_), channel_id=1, source_target_pairs={{0,16},{8,24},{16,0},{24,8},{1,17},{9,25},{17,1},{25,9},{2,18},{10... | collective-permute-start | bytes 491528 | tf_op jit(solution)/shard_map/ppermute | solution.py:118
  14.2 1.0 collective-permute-start.3
  15.2 0.5 collective-permute-start.5
  15.7 3.4 %collective-permute-done.2.refs_6_ = bf16[128,640]{1,0:T(8,128)(2,1)S(1)} collective-permute-done((bf16[128,640]{1,0:T(8,128)(2,1)S(1)}, bf16[128,640]{1,0:T(8,128)(2,1)S(1)}, u32[]{:S(2)}, u32[]{:S(2)}) %collective-permute-start.2) | collective-permute-done | bytes 163872 | tf_op jit(solution)/shard_map/ppermute | solution.py:118
  19.1 1.8 %collective-permute-done.3.refs_7_ = bf16[128,640]{1,0:T(8,128)(2,1)S(1)} collective-permute-done((bf16[128,640]{1,0:T(8,128)(2,1)S(1)}, bf16[128,640]{1,0:T(8,128)(2,1)S(1)}, u32[]{:S(2)}, u32[]{:S(2)}) %collective-permute-start.3) | collective-permute-done | bytes 163872 | tf_op jit(solution)/shard_map/ppermute | solution.py:118
  20.9 1.3 %collective-permute-done.7.refs_11_ = bf16[128,640]{1,0:T(8,128)(2,1)S(1)} collective-permute-done((bf16[128,640]{1,0:T(8,128)(2,1)S(1)}, bf16[128,640]{1,0:T(8,128)(2,1)S(1)}, u32[]{:S(2)}, u32[]{:S(2)}) %collective-permute-start.7) | collective-permute-done | bytes 163872 | tf_op jit(solution)/shard_map/ppermute | solution.py:118
  22.2 19.7 %shard_map.77 = (bf16[256,2048]{1,0:T(8,128)(2,1)S(1)}, bf16[64,3584]{1,0:T(8,128)(2,1)S(1)}, bf16[64,3584]{1,0:T(8,128)(2,1)S(1)}, bf16[64,3584]{1,0:T(8,128)(2,1)S(1)}, bf16[64,3584]{1,0:T(8,128)(2,1)S(1)}) custom-call(bf16[4,256,1024]{2,1,0:T(8,128)(2,1)} %copy-done, f32[256,1024]{1,0:T(8,128)S(1)} %get-tuple-element.17.refs_2_.refs_1_, ...), custom_call_target="tpu_custom_call" | custom-call | flops 12348030976 | bytes 20971520 | tf_op jit(solution)/shard_map/pallas_call | solution.py:304
  41.9 0.1 shard_map.83
  42.0 1.4 %collective-permute-start.16 = (bf16[128,3584]{1,0:T(8,128)(2,1)S(1)}, bf16[128,3584]{1,0:T(8,128)(2,1)S(1)}, u32[]{:S(2)}, u32[]{:S(2)}) collective-permute-start(bf16[128,3584]{1,0:T(8,128)(2,1)S(1)} %shard_map.83), channel_id=1, source_target_pairs={{0,1},{1,0},{2,3},{3,2},{4,5},{5,4},{6,7},{7,6},{8,9},{9,8},{10,11... | collective-permute-start | bytes 2752520 | tf_op jit(solution)/shard_map/ppermute | solution.py:460
  43.4 1.3 %collective-permute-start.12 = (bf16[64,3584]{1,0:T(8,128)(2,1)S(1)}, bf16[64,3584]{1,0:T(8,128)(2,1)S(1)}, u32[]{:S(2)}, u32[]{:S(2)}) collective-permute-start(bf16[64,3584]{1,0:T(8,128)(2,1)S(1)} %get-tuple-element.23.refs_0_), channel_id=1, source_target_pairs={{0,2},{6,4},{1,3},{7,5},{8,10},{14,12},{9,11},{15,13},{16,18},{22,... | collective-permute-start | bytes 1376264 | tf_op jit(solution)/shard_map/ppermute | solution.py:445
  44.7 8.8 %shard_map.78 = (bf16[64,3584]{1,0:T(8,128)(2,1)S(1)}, bf16[64,3584]{1,0:T(8,128)(2,1)}, bf16[64,3584]{1,0:T(8,128)(2,1)S(1)}, bf16[64,3584]{1,0:T(8,128)(2,1)S(1)}) custom-call(bf16[256,2048]{1,0:T(8,128)(2,1)S(1)} %get-tuple-element.18.x_ref, bf16[2048,7168]{1,0:T(8,128)(2,1)} %bitcast.13, bf16[2048,7168]{1,0:T(8,128)(2,1)} %bitcast.14), custom_call_target="tpu_custom_call" | custom-call | flops 3758096384 | bytes 14680064 | tf_op jit(solution)/shard_map/pallas_call | solution.py:347
  53.5 1.3 %collective-permute-start.11 = (bf16[64,3584]{1,0:T(8,128)(2,1)S(1)}, bf16[64,3584]{1,0:T(8,128)(2,1)S(1)}, u32[]{:S(2)}, u32[]{:S(2)}) collective-permute-start(bf16[64,3584]{1,0:T(8,128)(2,1)S(1)} %get-tuple-element.22.refs_0_), channel_id=1, source_target_pairs={{0,2},{6,4},{1,3},{7,5},{8,10},{14,12},{9,11},{15,13},{16,18},{22,... | collective-permute-start | bytes 1376264 | tf_op jit(solution)/shard_map/ppermute | solution.py:445
  54.8 1.3 %collective-permute-start.14 = (bf16[64,3584]{1,0:T(8,128)(2,1)S(1)}, bf16[64,3584]{1,0:T(8,128)(2,1)S(1)}, u32[]{:S(2)}, u32[]{:S(2)}) collective-permute-start(bf16[64,3584]{1,0:T(8,128)(2,1)S(1)} %get-tuple-element.24.refs_0_), channel_id=1, source_target_pairs={{0,2},{6,4},{1,3},{7,5},{8,10},{14,12},{9,11},{15,13},{16,18},{22,... | collective-permute-start | bytes 1376264 | tf_op jit(solution)/shard_map/ppermute | solution.py:445
  56.1 2.2 %collective-permute-done.12.refs_1_ = bf16[64,3584]{1,0:T(8,128)(2,1)S(1)} collective-permute-done((bf16[64,3584]{1,0:T(8,128)(2,1)S(1)}, bf16[64,3584]{1,0:T(8,128)(2,1)S(1)}, u32[]{:S(2)}, u32[]{:S(2)}) %collective-permute-start.12) | collective-permute-done | bytes 458784 | tf_op jit(solution)/shard_map/ppermute | solution.py:445
  58.3 0.1 shard_map.80.refs_2_
  58.4 4.1 %collective-permute-start.15 = (bf16[64,3584]{1,0:T(8,128)(2,1)S(1)}, bf16[64,3584]{1,0:T(8,128)(2,1)S(1)}, u32[]{:S(2)}, u32[]{:S(2)}) collective-permute-start(bf16[64,3584]{1,0:T(8,128)(2,1)S(1)} %shard_map.80.refs_2_), channel_id=1, source_target_pairs={{2,4},{4,2},{3,5},{5,3},{10,12},{12,10},{11,13},{13,11},{18,20},{2... | collective-permute-start | bytes 1376264 | tf_op jit(solution)/shard_map/ppermute | solution.py:445
  62.5 0.1 shard_map.79
  62.6 0.6 collective-permute-start.8
  63.2 6.0 %collective-permute-done.11.refs_1_ = bf16[64,3584]{1,0:T(8,128)(2,1)S(1)} collective-permute-done((bf16[64,3584]{1,0:T(8,128)(2,1)S(1)}, bf16[64,3584]{1,0:T(8,128)(2,1)S(1)}, u32[]{:S(2)}, u32[]{:S(2)}) %collective-permute-start.11) | collective-permute-done | bytes 458784 | tf_op jit(solution)/shard_map/ppermute | solution.py:445
  69.4 4.4 %collective-permute-start.13 = (bf16[64,3584]{1,0:T(8,128)(2,1)S(1)}, bf16[64,3584]{1,0:T(8,128)(2,1)S(1)}, u32[]{:S(2)}, u32[]{:S(2)}) collective-permute-start(bf16[64,3584]{1,0:T(8,128)(2,1)S(1)} %shard_map.81.refs_2_), channel_id=1, source_target_pairs={{2,4},{4,2},{3,5},{5,3},{10,12},{12,10},{11,13},{13,11},{18,20},{2... | collective-permute-start | bytes 1376264 | tf_op jit(solution)/shard_map/ppermute | solution.py:445
  73.8 1.3 %collective-permute-start.10 = (bf16[64,3584]{1,0:T(8,128)(2,1)}, bf16[64,3584]{1,0:T(8,128)(2,1)}, u32[]{:S(2)}, u32[]{:S(2)}) collective-permute-start(bf16[64,3584]{1,0:T(8,128)(2,1)} %get-tuple-element.21.refs_0_), channel_id=1, source_target_pairs={{0,2},{6,4},{1,3},{7,5},{8,10},{14,12},{9,11},{15,13},{16,18},{22,... | collective-permute-start | bytes 1376264 | tf_op jit(solution)/shard_map/ppermute | solution.py:445
  75.1 0.1 shard_map.82.refs_2_
  75.2 3.9 %collective-permute-done.14.refs_1_ = bf16[64,3584]{1,0:T(8,128)(2,1)S(1)} collective-permute-done((bf16[64,3584]{1,0:T(8,128)(2,1)S(1)}, bf16[64,3584]{1,0:T(8,128)(2,1)S(1)}, u32[]{:S(2)}, u32[]{:S(2)}) %collective-permute-start.14) | collective-permute-done | bytes 458784 | tf_op jit(solution)/shard_map/ppermute | solution.py:445
  79.1 0.1 shard_map.84.refs_2_
  79.2 4.4 %collective-permute-start.20 = (bf16[64,3584]{1,0:T(8,128)(2,1)S(1)}, bf16[64,3584]{1,0:T(8,128)(2,1)}, u32[]{:S(2)}, u32[]{:S(2)}) collective-permute-start(bf16[64,3584]{1,0:T(8,128)(2,1)S(1)} %shard_map.84.refs_2_), channel_id=1, source_target_pairs={{2,5},{3,4},{4,3},{5,2},{10,13},{11,12},{12,11},{13,10},{18,21},{1... | collective-permute-start | bytes 1376264 | tf_op jit(solution)/shard_map/ppermute | solution.py:446
  83.6 0.8 slice.19
  84.4 1.3 %collective-permute-start.19 = (bf16[64,3584]{1,0:T(8,128)(2,1)}, bf16[64,3584]{1,0:T(8,128)(2,1)}, u32[]{:S(2)}, u32[]{:S(2)}) collective-permute-start(bf16[64,3584]{1,0:T(8,128)(2,1)} %slice.19), channel_id=1, source_target_pairs={{0,2},{6,4},{1,3},{7,5},{8,10},{14,12},{9,11},{15,13},{16,18},{22,... | collective-permute-start | bytes 1376264 | tf_op jit(solution)/shard_map/ppermute | solution.py:445
  85.7 0.8 copy-done.2
  86.5 7.0 %collective-permute-start.21 = (bf16[64,3584]{1,0:T(8,128)(2,1)S(1)}, bf16[64,3584]{1,0:T(8,128)(2,1)}, u32[]{:S(2)}, u32[]{:S(2)}) collective-permute-start(bf16[64,3584]{1,0:T(8,128)(2,1)S(1)} %shard_map.82.refs_2_), channel_id=1, source_target_pairs={{4,7},{5,6},{2,1},{3,0},{12,15},{13,14},{10,9},{11,8},{20,23},{21,... | collective-permute-start | bytes 1376264 | tf_op jit(solution)/shard_map/ppermute | solution.py:446
  93.6 1.0 copy-done.3
  94.7 1.3 %collective-permute-start.18 = (bf16[64,3584]{1,0:T(8,128)(2,1)S(1)}, bf16[64,3584]{1,0:T(8,128)(2,1)S(1)}, u32[]{:S(2)}, u32[]{:S(2)}) collective-permute-start(bf16[64,3584]{1,0:T(8,128)(2,1)S(1)} %shard_map.85.refs_2_), channel_id=1, source_target_pairs={{4,7},{5,6},{2,1},{3,0},{12,15},{13,14},{10,9},{11,8},{20,23},{21,... | collective-permute-start | bytes 1376264 | tf_op jit(solution)/shard_map/ppermute | solution.py:446
  96.0 1.3 %shard_map.86 = bf16[64,3584]{1,0:T(8,128)(2,1)S(1)} custom-call(bf16[64,3584]{1,0:T(8,128)(2,1)} %get-tuple-element.21.refs_0_, bf16[64,3584]{1,0:T(8,128)(2,1)} %collective-permute-done.10.refs_1_, bf16[64,3584]{1,0:T(8,128)(2,1)S(1)} %shard_map.85.refs_2_), custom_call_target="tpu_custom_call" | custom-call | tf_op jit(solution)/shard_map/pallas_call | solution.py:377
  97.3 2.3 %collective-permute-start.17 = (bf16[64,3584]{1,0:T(8,128)(2,1)S(1)}, bf16[64,3584]{1,0:T(8,128)(2,1)S(1)}, u32[]{:S(2)}, u32[]{:S(2)}) collective-permute-start(bf16[64,3584]{1,0:T(8,128)(2,1)S(1)} %shard_map.86), channel_id=1, source_target_pairs={{2,5},{3,4},{4,3},{5,2},{10,13},{11,12},{12,11},{13,10},{18,21},{1... | collective-permute-start | bytes 1376264 | tf_op jit(solution)/shard_map/ppermute | solution.py:446
  99.7 1.1 slice.17
  100.7 1.3 %collective-permute-start.9 = (bf16[64,3584]{1,0:T(8,128)(2,1)S(1)}, bf16[64,3584]{1,0:T(8,128)(2,1)S(1)}, u32[]{:S(2)}, u32[]{:S(2)}) collective-permute-start(bf16[64,3584]{1,0:T(8,128)(2,1)S(1)} %slice.17), channel_id=1, source_target_pairs={{0,2},{6,4},{1,3},{7,5},{8,10},{14,12},{9,11},{15,13},{16,18},{22,... | collective-permute-start | bytes 1376264 | tf_op jit(solution)/shard_map/ppermute | solution.py:445
  102.0 1.7 %collective-permute-done.21.refs_2_ = bf16[64,3584]{1,0:T(8,128)(2,1)} collective-permute-done((bf16[64,3584]{1,0:T(8,128)(2,1)S(1)}, bf16[64,3584]{1,0:T(8,128)(2,1)}, u32[]{:S(2)}, u32[]{:S(2)}) %collective-permute-start.21) | collective-permute-done | bytes 458784 | tf_op jit(solution)/shard_map/ppermute | solution.py:446
  103.7 2.4 %shard_map.87.refs_3_ = bf16[64,7168]{1,0:T(8,128)(2,1)} custom-call(s32[3]{0:T(128)S(1)} %add_convert_fusion.flag_ref, bf16[128,3584]{1,0:T(8,128)(2,1)S(1)} %collective-permute-done.16.refs_3_.pair_ref, bf16[64,3584]{1,0:T(8,128)(2,1)} %collective-permute-done.19.refs_0_, bf16[64,3584]{1,0:T(8,128)(2,1)} %collective-permute-done.20.refs_1_, ...), custom_call_target="tpu_custom_call" | custom-call | flops 20000000000 | tf_op jit(solution)/shard_map/pallas_call | solution.py:412
  106.1 3.6 %collective-permute-done.17.refs_1_ = bf16[64,3584]{1,0:T(8,128)(2,1)S(1)} collective-permute-done((bf16[64,3584]{1,0:T(8,128)(2,1)S(1)}, bf16[64,3584]{1,0:T(8,128)(2,1)S(1)}, u32[]{:S(2)}, u32[]{:S(2)}) %collective-permute-start.17) | collective-permute-done | bytes 458784 | tf_op jit(solution)/shard_map/ppermute | solution.py:446
  109.7 0.2 collective-permute-done.18.refs_2_
  109.9 4.1 %collective-permute-done.9.refs_0_ = bf16[64,3584]{1,0:T(8,128)(2,1)S(1)} collective-permute-done((bf16[64,3584]{1,0:T(8,128)(2,1)S(1)}, bf16[64,3584]{1,0:T(8,128)(2,1)S(1)}, u32[]{:S(2)}, u32[]{:S(2)}) %collective-permute-start.9) | collective-permute-done | bytes 458784 | tf_op jit(solution)/shard_map/ppermute | solution.py:445
  114.1 2.3 %shard_map.88 = bf16[64,7168]{1,0:T(8,128)(2,1)} custom-call(s32[3]{0:T(128)S(1)} %add_convert_fusion.flag_ref, bf16[128,3584]{1,0:T(8,128)(2,1)} %collective-permute-done.8.pair_ref, bf16[64,3584]{1,0:T(8,128)(2,1)S(1)} %collective-permute-done.9.refs_0_, bf16[64,3584]{1,0:T(8,128)(2,1)S(1)} %collective-permute-done.17.refs_1_, ...), custom_call_target="tpu_custom_call", output_to_operand_aliasing={{}: (5, {})} | custom-call | flops 20000000000 | tf_op jit(solution)/shard_map/pallas_call | solution.py:412
  (30 shorter events, 0.5 us)
Async XLA Ops:
  1.7 4.7 %collective-permute-start = (bf16[64,640]{1,0:T(8,128)(2,1)}, bf16[64,640]{1,0:T(8,128)(2,1)S(1)}, u32[]{:S(2)}, u32[]{:S(2)}) collective-permute-start(bf16[64,640]{1,0:T(8,128)(2,1)} %shard_map.74.refs_0_), channel_id=1, source_target_pairs={{0,2},{2,0},{4,6},{6,4},{1,3},{3,1},{5,7},{7,5},{8,10},{10,8},{12,... | collective-permute-start | bytes 245768 | tf_op jit(solution)/shard_map/ppermute | solution.py:118
  6.4 0.9 copy-start.4
  7.3 6.8 %collective-permute-start.1 = (bf16[128,640]{1,0:T(8,128)(2,1)S(1)}, bf16[128,640]{1,0:T(8,128)(2,1)S(1)}, u32[]{:S(2)}, u32[]{:S(2)}) collective-permute-start(bf16[128,640]{1,0:T(8,128)(2,1)S(1)} %shard_map.75.refs_4_), channel_id=1, source_target_pairs={{0,4},{2,6},{4,0},{6,2},{1,5},{3,7},{5,1},{7,3},{8,12},{10,14},{12... | collective-permute-start | bytes 491528 | tf_op jit(solution)/shard_map/ppermute | solution.py:118
  7.4 1.4 %copy-start.1 = (bf16[1,256,3072]{2,1,0:T(8,128)(2,1)S(1)}, bf16[1,256,3072]{2,1,0:T(8,128)(2,1)}, u32[]{:S(2)}) copy-start(bf16[1,256,3072]{2,1,0:T(8,128)(2,1)} %param.7) | copy-start | bytes 4718596
  8.8 0.7 copy-start.5
  9.4 11.4 %copy-start.6 = (bf16[1,64,7168]{2,1,0:T(8,128)(2,1)S(1)}, bf16[1,64,7168]{2,1,0:T(8,128)(2,1)}, u32[]{:S(2)}) copy-start(bf16[1,64,7168]{2,1,0:T(8,128)(2,1)} %param.12) | copy-start | bytes 2752516
  12.2 10.0 %copy-start = (bf16[4,256,1024]{2,1,0:T(8,128)(2,1)}, bf16[4,256,1024]{2,1,0:T(8,128)(2,1)S(1)}, u32[]{:S(2)}) copy-start(bf16[4,256,1024]{2,1,0:T(8,128)(2,1)S(1)} %get-tuple-element.16.refs_1_.refs_0_) | copy-start | bytes 6291460
  12.2 6.8 %collective-permute-start.2 = (bf16[128,640]{1,0:T(8,128)(2,1)S(1)}, bf16[128,640]{1,0:T(8,128)(2,1)S(1)}, u32[]{:S(2)}, u32[]{:S(2)}) collective-permute-start(bf16[128,640]{1,0:T(8,128)(2,1)S(1)} %shard_map.75.refs_4_), channel_id=1, source_target_pairs={{0,16},{8,24},{16,0},{24,8},{1,17},{9,25},{17,1},{25,9},{2,18},{10... | collective-permute-start | bytes 491528 | tf_op jit(solution)/shard_map/ppermute | solution.py:118
  14.2 6.7 %collective-permute-start.3 = (bf16[128,640]{1,0:T(8,128)(2,1)S(1)}, bf16[128,640]{1,0:T(8,128)(2,1)S(1)}, u32[]{:S(2)}, u32[]{:S(2)}) collective-permute-start(bf16[128,640]{1,0:T(8,128)(2,1)S(1)} %shard_map.76.refs_5_), channel_id=1, source_target_pairs={{0,16},{8,24},{16,0},{24,8},{1,17},{9,25},{17,1},{25,9},{2,18},{10... | collective-permute-start | bytes 491528 | tf_op jit(solution)/shard_map/ppermute | solution.py:118
  15.2 5.7 %collective-permute-start.4 = (bf16[128,640]{1,0:T(8,128)(2,1)S(1)}, bf16[128,640]{1,0:T(8,128)(2,1)S(1)}, u32[]{:S(2)}, u32[]{:S(2)}) collective-permute-start(bf16[128,640]{1,0:T(8,128)(2,1)S(1)} %shard_map.75.refs_4_), channel_id=1, source_target_pairs={{0,8},{8,0},{16,24},{24,16},{1,9},{9,1},{17,25},{25,17},{2,10},{10... | collective-permute-start | bytes 491528 | tf_op jit(solution)/shard_map/ppermute | solution.py:118
  15.2 5.7 %collective-permute-start.5 = (bf16[128,640]{1,0:T(8,128)(2,1)S(1)}, bf16[128,640]{1,0:T(8,128)(2,1)S(1)}, u32[]{:S(2)}, u32[]{:S(2)}) collective-permute-start(bf16[128,640]{1,0:T(8,128)(2,1)S(1)} %shard_map.76.refs_5_), channel_id=1, source_target_pairs={{0,8},{8,0},{16,24},{24,16},{1,9},{9,1},{17,25},{25,17},{2,10},{10... | collective-permute-start | bytes 491528 | tf_op jit(solution)/shard_map/ppermute | solution.py:118
  19.1 1.9 %collective-permute-start.6 = (bf16[128,640]{1,0:T(8,128)(2,1)S(1)}, bf16[128,640]{1,0:T(8,128)(2,1)S(1)}, u32[]{:S(2)}, u32[]{:S(2)}) collective-permute-start(bf16[128,640]{1,0:T(8,128)(2,1)S(1)} %collective-permute-done.2.refs_6_), channel_id=1, source_target_pairs={{0,8},{8,0},{16,24},{24,16},{1,9},{9,1},{17,25},{25,17},{2,10},{10... | collective-permute-start | bytes 491528 | tf_op jit(solution)/shard_map/ppermute | solution.py:118
  20.8 1.4 %collective-permute-start.7 = (bf16[128,640]{1,0:T(8,128)(2,1)S(1)}, bf16[128,640]{1,0:T(8,128)(2,1)S(1)}, u32[]{:S(2)}, u32[]{:S(2)}) collective-permute-start(bf16[128,640]{1,0:T(8,128)(2,1)S(1)} %collective-permute-done.3.refs_7_), channel_id=1, source_target_pairs={{0,8},{8,0},{16,24},{24,16},{1,9},{9,1},{17,25},{25,17},{2,10},{10... | collective-permute-start | bytes 491528 | tf_op jit(solution)/shard_map/ppermute | solution.py:118
  42.0 37.1 %collective-permute-start.16 = (bf16[128,3584]{1,0:T(8,128)(2,1)S(1)}, bf16[128,3584]{1,0:T(8,128)(2,1)S(1)}, u32[]{:S(2)}, u32[]{:S(2)}) collective-permute-start(bf16[128,3584]{1,0:T(8,128)(2,1)S(1)} %shard_map.83), channel_id=1, source_target_pairs={{0,1},{1,0},{2,3},{3,2},{4,5},{5,4},{6,7},{7,6},{8,9},{9,8},{10,11... | collective-permute-start | bytes 2752520 | tf_op jit(solution)/shard_map/ppermute | solution.py:460
  43.4 14.9 %collective-permute-start.12 = (bf16[64,3584]{1,0:T(8,128)(2,1)S(1)}, bf16[64,3584]{1,0:T(8,128)(2,1)S(1)}, u32[]{:S(2)}, u32[]{:S(2)}) collective-permute-start(bf16[64,3584]{1,0:T(8,128)(2,1)S(1)} %get-tuple-element.23.refs_0_), channel_id=1, source_target_pairs={{0,2},{6,4},{1,3},{7,5},{8,10},{14,12},{9,11},{15,13},{16,18},{22,... | collective-permute-start | bytes 1376264 | tf_op jit(solution)/shard_map/ppermute | solution.py:445
  53.5 15.7 %collective-permute-start.11 = (bf16[64,3584]{1,0:T(8,128)(2,1)S(1)}, bf16[64,3584]{1,0:T(8,128)(2,1)S(1)}, u32[]{:S(2)}, u32[]{:S(2)}) collective-permute-start(bf16[64,3584]{1,0:T(8,128)(2,1)S(1)} %get-tuple-element.22.refs_0_), channel_id=1, source_target_pairs={{0,2},{6,4},{1,3},{7,5},{8,10},{14,12},{9,11},{15,13},{16,18},{22,... | collective-permute-start | bytes 1376264 | tf_op jit(solution)/shard_map/ppermute | solution.py:445
  54.8 24.3 %collective-permute-start.14 = (bf16[64,3584]{1,0:T(8,128)(2,1)S(1)}, bf16[64,3584]{1,0:T(8,128)(2,1)S(1)}, u32[]{:S(2)}, u32[]{:S(2)}) collective-permute-start(bf16[64,3584]{1,0:T(8,128)(2,1)S(1)} %get-tuple-element.24.refs_0_), channel_id=1, source_target_pairs={{0,2},{6,4},{1,3},{7,5},{8,10},{14,12},{9,11},{15,13},{16,18},{22,... | collective-permute-start | bytes 1376264 | tf_op jit(solution)/shard_map/ppermute | solution.py:445
  58.4 15.4 %collective-permute-start.15 = (bf16[64,3584]{1,0:T(8,128)(2,1)S(1)}, bf16[64,3584]{1,0:T(8,128)(2,1)S(1)}, u32[]{:S(2)}, u32[]{:S(2)}) collective-permute-start(bf16[64,3584]{1,0:T(8,128)(2,1)S(1)} %shard_map.80.refs_2_), channel_id=1, source_target_pairs={{2,4},{4,2},{3,5},{5,3},{10,12},{12,10},{11,13},{13,11},{18,20},{2... | collective-permute-start | bytes 1376264 | tf_op jit(solution)/shard_map/ppermute | solution.py:445
  62.6 34.7 %collective-permute-start.8 = (bf16[128,3584]{1,0:T(8,128)(2,1)S(1)}, bf16[128,3584]{1,0:T(8,128)(2,1)}, u32[]{:S(2)}, u32[]{:S(2)}) collective-permute-start(bf16[128,3584]{1,0:T(8,128)(2,1)S(1)} %shard_map.79), channel_id=1, source_target_pairs={{0,1},{1,0},{2,3},{3,2},{4,5},{5,4},{6,7},{7,6},{8,9},{9,8},{10,11... | collective-permute-start | bytes 2752520 | tf_op jit(solution)/shard_map/ppermute | solution.py:460
  69.4 16.3 %collective-permute-start.13 = (bf16[64,3584]{1,0:T(8,128)(2,1)S(1)}, bf16[64,3584]{1,0:T(8,128)(2,1)S(1)}, u32[]{:S(2)}, u32[]{:S(2)}) collective-permute-start(bf16[64,3584]{1,0:T(8,128)(2,1)S(1)} %shard_map.81.refs_2_), channel_id=1, source_target_pairs={{2,4},{4,2},{3,5},{5,3},{10,12},{12,10},{11,13},{13,11},{18,20},{2... | collective-permute-start | bytes 1376264 | tf_op jit(solution)/shard_map/ppermute | solution.py:445
  73.8 20.9 %collective-permute-start.10 = (bf16[64,3584]{1,0:T(8,128)(2,1)}, bf16[64,3584]{1,0:T(8,128)(2,1)}, u32[]{:S(2)}, u32[]{:S(2)}) collective-permute-start(bf16[64,3584]{1,0:T(8,128)(2,1)} %get-tuple-element.21.refs_0_), channel_id=1, source_target_pairs={{0,2},{6,4},{1,3},{7,5},{8,10},{14,12},{9,11},{15,13},{16,18},{22,... | collective-permute-start | bytes 1376264 | tf_op jit(solution)/shard_map/ppermute | solution.py:445
  79.2 21.5 %collective-permute-start.20 = (bf16[64,3584]{1,0:T(8,128)(2,1)S(1)}, bf16[64,3584]{1,0:T(8,128)(2,1)}, u32[]{:S(2)}, u32[]{:S(2)}) collective-permute-start(bf16[64,3584]{1,0:T(8,128)(2,1)S(1)} %shard_map.84.refs_2_), channel_id=1, source_target_pairs={{2,5},{3,4},{4,3},{5,2},{10,13},{11,12},{12,11},{13,10},{18,21},{1... | collective-permute-start | bytes 1376264 | tf_op jit(solution)/shard_map/ppermute | solution.py:446
  84.4 17.6 %collective-permute-start.19 = (bf16[64,3584]{1,0:T(8,128)(2,1)}, bf16[64,3584]{1,0:T(8,128)(2,1)}, u32[]{:S(2)}, u32[]{:S(2)}) collective-permute-start(bf16[64,3584]{1,0:T(8,128)(2,1)} %slice.19), channel_id=1, source_target_pairs={{0,2},{6,4},{1,3},{7,5},{8,10},{14,12},{9,11},{15,13},{16,18},{22,... | collective-permute-start | bytes 1376264 | tf_op jit(solution)/shard_map/ppermute | solution.py:445
  85.7 0.8 copy-start.2
  86.5 17.2 %collective-permute-start.21 = (bf16[64,3584]{1,0:T(8,128)(2,1)S(1)}, bf16[64,3584]{1,0:T(8,128)(2,1)}, u32[]{:S(2)}, u32[]{:S(2)}) collective-permute-start(bf16[64,3584]{1,0:T(8,128)(2,1)S(1)} %shard_map.82.refs_2_), channel_id=1, source_target_pairs={{4,7},{5,6},{2,1},{3,0},{12,15},{13,14},{10,9},{11,8},{20,23},{21,... | collective-permute-start | bytes 1376264 | tf_op jit(solution)/shard_map/ppermute | solution.py:446
  93.6 1.0 copy-start.3
  94.7 15.2 %collective-permute-start.18 = (bf16[64,3584]{1,0:T(8,128)(2,1)S(1)}, bf16[64,3584]{1,0:T(8,128)(2,1)S(1)}, u32[]{:S(2)}, u32[]{:S(2)}) collective-permute-start(bf16[64,3584]{1,0:T(8,128)(2,1)S(1)} %shard_map.85.refs_2_), channel_id=1, source_target_pairs={{4,7},{5,6},{2,1},{3,0},{12,15},{13,14},{10,9},{11,8},{20,23},{21,... | collective-permute-start | bytes 1376264 | tf_op jit(solution)/shard_map/ppermute | solution.py:446
  97.3 12.4 %collective-permute-start.17 = (bf16[64,3584]{1,0:T(8,128)(2,1)S(1)}, bf16[64,3584]{1,0:T(8,128)(2,1)S(1)}, u32[]{:S(2)}, u32[]{:S(2)}) collective-permute-start(bf16[64,3584]{1,0:T(8,128)(2,1)S(1)} %shard_map.86), channel_id=1, source_target_pairs={{2,5},{3,4},{4,3},{5,2},{10,13},{11,12},{12,11},{13,10},{18,21},{1... | collective-permute-start | bytes 1376264 | tf_op jit(solution)/shard_map/ppermute | solution.py:446
  100.7 13.4 %collective-permute-start.9 = (bf16[64,3584]{1,0:T(8,128)(2,1)S(1)}, bf16[64,3584]{1,0:T(8,128)(2,1)S(1)}, u32[]{:S(2)}, u32[]{:S(2)}) collective-permute-start(bf16[64,3584]{1,0:T(8,128)(2,1)S(1)} %slice.17), channel_id=1, source_target_pairs={{0,2},{6,4},{1,3},{7,5},{8,10},{14,12},{9,11},{15,13},{16,18},{22,... | collective-permute-start | bytes 1376264 | tf_op jit(solution)/shard_map/ppermute | solution.py:445

commit v4 on v3

--- a/solution.py
+++ b/solution.py
@@ -18,14 +18,16 @@
 score_scale = 0.135
 SCALE2 = score_scale * math.log2(math.e)
 
-HEADS_STEP = 4
+HEADS_STEP = 8
 MIB = 1024 * 1024
 PREPARE_VMEM = 16 * MIB
 PROJECT_VMEM = 24 * MIB
 ATTEND_VMEM = 48 * MIB
 ADD_VMEM = 8 * MIB
-FINAL_FLOPS = 2 * 10**10
+FINAL_FLOPS = 10**10
+FIRST_SHARE = 50
 PIECES = 2
+TILE = 896
 
 
 def row_places(order_ref, first, count, block_len):
@@ -76,7 +78,7 @@
 def own_keys(order_row, latents, gain, block_len):
     return pl.pallas_call(
         functools.partial(own_keys_kernel, block_len),
-        out_shape=jax.ShapeDtypeStruct((latents.shape[0], LATENT + LANES), jnp.bfloat16),
+        out_shape=pltpu.VMEM((latents.shape[0], LATENT + LANES), jnp.bfloat16),
         in_specs=[pl.BlockSpec(memory_space=pltpu.SMEM)] + [pl.BlockSpec(memory_space=pltpu.VMEM)] * 2,
         out_specs=pl.BlockSpec(memory_space=pltpu.VMEM),
         compiler_params=pltpu.CompilerParams(vmem_limit_bytes=60 * MIB),
@@ -297,7 +299,7 @@
     steps = queries.shape[0]
     heads = steps * HEADS_STEP
     depth = heads * VDIM
-    tile = column_tile(0, size, 1024)
+    tile = column_tile(0, size, TILE)
     head_step = lambda i: jnp.minimum(i, steps - 1)
     column_step = lambda i: jnp.maximum(i - steps, 0)
     whole = lambda shape: pl.BlockSpec(shape, lambda i: (0, 0))
@@ -342,7 +344,7 @@
 
 def project(rows, weights, lo, size, blocks):
     count, depth = rows.shape
-    tile = column_tile(lo, size, 1024)
+    tile = column_tile(lo, size, TILE)
     block = count // blocks
     return pl.pallas_call(
         project_kernel,
@@ -401,22 +403,26 @@
     )(own, rest, unit)
 
 
-def finish_kernel(count, flag_ref, pair_ref, *refs):
-    rows = refs[-1].shape[0]
-    refs[-1][...] = total_of([pair_ref.at[:rows, :], *refs[:count]], flag_ref, 1)
-
-
-def finish(flags, pair, flagged, piece, pieces, before):
+def finish_kernel(lo, count, flag_ref, pair_ref, *refs):
+    out_hbm, held_ref, semaphore = refs[-3:]
+    rows, size = held_ref.shape
+    held_ref[...] = total_of([pair_ref.at[:rows, :], *refs[:count]], flag_ref, 1)
+    copy = pltpu.make_async_copy(held_ref, out_hbm.at[:, pl.ds(lo, size)], semaphore)
+    copy.start()
+    copy.wait()
+
+
+def finish(flags, pair, flagged, lo, width, before):
     rows, size = flagged[0].shape
     operands = [flags, pair, *flagged] + before
     return pl.pallas_call(
-        functools.partial(finish_kernel, len(flagged)),
-        grid=(1,),
-        out_shape=jax.ShapeDtypeStruct((rows, size * pieces), jnp.bfloat16),
+        functools.partial(finish_kernel, lo, len(flagged)),
+        out_shape=jax.ShapeDtypeStruct((rows, width), jnp.bfloat16),
         in_specs=[pl.BlockSpec(memory_space=pltpu.SMEM)]
         + [pl.BlockSpec(memory_space=pltpu.VMEM)] * (1 + len(flagged))
         + [pl.BlockSpec(memory_space=pl.ANY)] * len(before),
-        out_specs=pl.BlockSpec((rows, size), lambda i: (0, piece)),
+        out_specs=pl.BlockSpec(memory_space=pl.ANY),
+        scratch_shapes=[pltpu.VMEM((rows, size), jnp.bfloat16), pltpu.SemaphoreType.DMA],
         input_output_aliases={len(operands) - 1: 0} if before else {},
         compiler_params=pltpu.CompilerParams(vmem_limit_bytes=ADD_VMEM),
         cost_estimate=pl.CostEstimate(flops=FINAL_FLOPS, bytes_accessed=0, transcendentals=0),
@@ -430,11 +436,13 @@
     tok_dev, lat_rows, width = queries.shape[1], latents.shape[1], w_o.shape[2]
     order_row = block_order[0]
     block_len = tok_dev * lax.axis_size("ctx") // order_row.shape[0]
-    size = width // PIECES
+    tile = column_tile(0, width, TILE)
+    first_size = -(-width * FIRST_SHARE // (100 * tile)) * tile
+    spans = [(0, first_size), (first_size, width - first_size)]
 
     turned_queries, bias = prepare(order_row, queries[0], lat_rows, gather_masks(), block_len)
     pieces = gather_keys(own_keys(order_row, latents[0], latent_gain, block_len), [turned_queries, bias])
-    attention, *first_terms = attend(turned_queries, bias, pieces, w_ukv[0], w_o[0], size, tp_count)
+    attention, *first_terms = attend(turned_queries, bias, pieces, w_ukv[0], w_o[0], first_size, tp_count)
 
     def slot_of(hop, unit):
         return unit if 2 * hop < last else hop + unit
@@ -450,12 +458,13 @@
     def flags_of(*conditions):
         return jnp.stack(conditions).astype(jnp.int32)
 
-    terms = [first_terms] + [project(attention, w_o[0], i * size, size, tp_count) for i in range(1, PIECES)]
+    terms = [first_terms] + [project(attention, w_o[0], *span, tp_count) for span in spans[1:]]
     got, ahead = {}, {}
     for i in range(PIECES):
         for unit in range(last - 1):
             got[0, unit, i] = send(0, terms[i][slot_of(0, unit)], False)
-        rest = residual[0][:, i * size : (i + 1) * size]
+        lo, size = spans[i]
+        rest = residual[0][:, lo : lo + size]
         both = pair_up(terms[i][last], rest, terms[i][slot_of(0, last - 1)])
         ahead[i] = lax.ppermute(both, "pp", [(0, 1), (1, 0)])
         got[0, last - 1, i] = send(0, ahead[i][rest.shape[0] :], False)
@@ -476,7 +485,7 @@
     out = []
     for i in range(PIECES):
         ended = [got[hop, last - 1 - hop, i] for hop in range(last)]
-        out = [finish(flags, ahead[i], ended, i, PIECES, out)]
+        out = [finish(flags, ahead[i], ended, spans[i][0], width, out)]
     return out[0][None]
 
 

time: 117 us -> 115 us (0.983)
  Pallas kernels: 39.7 us -> 38.4 us
    unnamed x14 -> x12, local copies, waits for them, and re-layouts: 4.75 us -> 3.87 us
where the time goes in v4:
time: 115 us; the launch traced here: 114 us
  Pallas kernels  38.4 us (33%)
  starting transfers between devices  38.4 us (33%)
  waiting for transfers between devices  31 us (27%)
  local copies, waits for them, and re-layouts  5.79 us (5%)
    pallas_call x1, Pallas kernels, attend(): pl.pallas_call(functools.partial(attention_kernel, len(pieces), steps), g...  19 us
    ppermute x8, starting transfers between devices, send(): return lax.ppermute(value, 'tp', steps)  16.3 us
    ppermute x8, waiting for transfers between devices, send(): return lax.ppermute(value, 'tp', steps)  16.2 us
    ppermute x4, starting transfers between devices, send(): lax.ppermute(value, ('tp', 'pp'), [(2 * i + p, 2 * j + 1 - p) for i, j in...  15.1 us
    ppermute x8, waiting for transfers between devices, traded(): lax.ppermute(value, axis, [(i, i ^ step) for i in range(lax.axis_size(axi...  9.3 us
    pallas_call x1, Pallas kernels, project(): pl.pallas_call(project_kernel, grid=(size // tile,), out_shape=[jax.Shape...  8.85 us
    ppermute x4, waiting for transfers between devices, send(): lax.ppermute(value, ('tp', 'pp'), [(2 * i + p, 2 * j + 1 - p) for i, j in...  5.5 us
    ppermute x8, starting transfers between devices, traded(): lax.ppermute(value, axis, [(i, i ^ step) for i in range(lax.axis_size(axi...  5.14 us
  transfers between devices with their start and end apart: 22, of which 11 were waited for; matrix products, arithmetic and copies ran while one was open for 2% of the time, Pallas kernels for 14%

profile of v4, /device:TPU:16, one launch (start us, length us, event | category | flops | bytes accessed | tf_op | source)
XLA Modules:
  0.0 114.0 jit_solution(8342388605536639750)
XLA Ops:
  0.0 1.1 shard_map.74.refs_0_
  1.1 1.6 %collective-permute-start = (bf16[64,640]{1,0:T(8,128)(2,1)S(1)}, bf16[64,640]{1,0:T(8,128)(2,1)S(1)}, u32[]{:S(2)}, u32[]{:S(2)}) collective-permute-start(bf16[64,640]{1,0:T(8,128)(2,1)S(1)} %shard_map.74.refs_0_), channel_id=1, source_target_pairs={{0,2},{2,0},{4,6},{6,4},{1,3},{3,1},{5,7},{7,5},{8,10},{10,8},{12,... | collective-permute-start | bytes 245768 | tf_op jit(solution)/shard_map/ppermute | solution.py:120
  2.7 2.9 %collective-permute-done.refs_1_ = bf16[64,640]{1,0:T(8,128)(2,1)S(1)} collective-permute-done((bf16[64,640]{1,0:T(8,128)(2,1)S(1)}, bf16[64,640]{1,0:T(8,128)(2,1)S(1)}, u32[]{:S(2)}, u32[]{:S(2)}) %collective-permute-start) | collective-permute-done | bytes 81952 | tf_op jit(solution)/shard_map/ppermute | solution.py:120
  5.7 1.4 %copy-done.1 = bf16[1,256,3072]{2,1,0:T(8,128)(2,1)S(1)} copy-done((bf16[1,256,3072]{2,1,0:T(8,128)(2,1)S(1)}, bf16[1,256,3072]{2,1,0:T(8,128)(2,1)}, u32[]{:S(2)}) %copy-start.1) | copy-done | bytes 1572888
  7.1 0.7 copy-done.4
  7.8 2.8 %shard_map.73 = (bf16[2,256,2048]{2,1,0:T(8,128)(2,1)S(1)}, f32[256,1024]{1,0:T(8,128)S(1)}) custom-call(s32[8]{0:T(128)S(1)} %bitcast.11, bf16[256,3072]{1,0:T(8,128)(2,1)S(1)} %bitcast.9), custom_call_target="tpu_custom_call" | custom-call | flops 15728640 | bytes 4718592 | tf_op jit(solution)/shard_map/pallas_call | solution.py:172
  10.6 1.9 %collective-permute-start.2 = (bf16[128,640]{1,0:T(8,128)(2,1)S(1)}, bf16[128,640]{1,0:T(8,128)(2,1)S(1)}, u32[]{:S(2)}, u32[]{:S(2)}) collective-permute-start(bf16[128,640]{1,0:T(8,128)(2,1)S(1)} %shard_map.75.refs_4_), channel_id=1, source_target_pairs={{0,16},{8,24},{16,0},{24,8},{1,17},{9,25},{17,1},{25,9},{2,18},{10... | collective-permute-start | bytes 491528 | tf_op jit(solution)/shard_map/ppermute | solution.py:120
  12.5 1.0 collective-permute-start.3
  13.5 0.5 collective-permute-start.5
  14.0 3.4 %collective-permute-done.2.refs_6_ = bf16[128,640]{1,0:T(8,128)(2,1)S(1)} collective-permute-done((bf16[128,640]{1,0:T(8,128)(2,1)S(1)}, bf16[128,640]{1,0:T(8,128)(2,1)S(1)}, u32[]{:S(2)}, u32[]{:S(2)}) %collective-permute-start.2) | collective-permute-done | bytes 163872 | tf_op jit(solution)/shard_map/ppermute | solution.py:120
  17.4 1.8 %collective-permute-done.3.refs_7_ = bf16[128,640]{1,0:T(8,128)(2,1)S(1)} collective-permute-done((bf16[128,640]{1,0:T(8,128)(2,1)S(1)}, bf16[128,640]{1,0:T(8,128)(2,1)S(1)}, u32[]{:S(2)}, u32[]{:S(2)}) %collective-permute-start.3) | collective-permute-done | bytes 163872 | tf_op jit(solution)/shard_map/ppermute | solution.py:120
  19.3 1.3 %collective-permute-done.7.refs_11_ = bf16[128,640]{1,0:T(8,128)(2,1)S(1)} collective-permute-done((bf16[128,640]{1,0:T(8,128)(2,1)S(1)}, bf16[128,640]{1,0:T(8,128)(2,1)S(1)}, u32[]{:S(2)}, u32[]{:S(2)}) %collective-permute-start.7) | collective-permute-done | bytes 163872 | tf_op jit(solution)/shard_map/ppermute | solution.py:120
  20.6 19.0 %shard_map.77 = (bf16[256,2048]{1,0:T(8,128)(2,1)S(1)}, bf16[64,3584]{1,0:T(8,128)(2,1)S(1)}, bf16[64,3584]{1,0:T(8,128)(2,1)S(1)}, bf16[64,3584]{1,0:T(8,128)(2,1)S(1)}, bf16[64,3584]{1,0:T(8,128)(2,1)S(1)}) custom-call(bf16[2,256,2048]{2,1,0:T(8,128)(2,1)} %copy-done, f32[256,1024]{1,0:T(8,128)S(1)} %get-tuple-element.17.refs_2_.refs_1_, ...), custom_call_target="tpu_custom_call" | custom-call | flops 12348030976 | bytes 20971520 | tf_op jit(solution)/shard_map/pallas_call | solution.py:306
  39.5 0.1 shard_map.83
  39.7 1.4 %collective-permute-start.16 = (bf16[128,3584]{1,0:T(8,128)(2,1)S(1)}, bf16[128,3584]{1,0:T(8,128)(2,1)S(1)}, u32[]{:S(2)}, u32[]{:S(2)}) collective-permute-start(bf16[128,3584]{1,0:T(8,128)(2,1)S(1)} %shard_map.83), channel_id=1, source_target_pairs={{0,1},{1,0},{2,3},{3,2},{4,5},{5,4},{6,7},{7,6},{8,9},{9,8},{10,11... | collective-permute-start | bytes 2752520 | tf_op jit(solution)/shard_map/ppermute | solution.py:469
  41.0 1.3 %collective-permute-start.12 = (bf16[64,3584]{1,0:T(8,128)(2,1)S(1)}, bf16[64,3584]{1,0:T(8,128)(2,1)S(1)}, u32[]{:S(2)}, u32[]{:S(2)}) collective-permute-start(bf16[64,3584]{1,0:T(8,128)(2,1)S(1)} %get-tuple-element.23.refs_0_), channel_id=1, source_target_pairs={{0,2},{6,4},{1,3},{7,5},{8,10},{14,12},{9,11},{15,13},{16,18},{22,... | collective-permute-start | bytes 1376264 | tf_op jit(solution)/shard_map/ppermute | solution.py:453
  42.3 8.9 %shard_map.78 = (bf16[64,3584]{1,0:T(8,128)(2,1)S(1)}, bf16[64,3584]{1,0:T(8,128)(2,1)}, bf16[64,3584]{1,0:T(8,128)(2,1)S(1)}, bf16[64,3584]{1,0:T(8,128)(2,1)S(1)}) custom-call(bf16[256,2048]{1,0:T(8,128)(2,1)S(1)} %get-tuple-element.18.x_ref, bf16[2048,7168]{1,0:T(8,128)(2,1)} %bitcast.13, bf16[2048,7168]{1,0:T(8,128)(2,1)} %bitcast.14), custom_call_target="tpu_custom_call" | custom-call | flops 3758096384 | bytes 14680064 | tf_op jit(solution)/shard_map/pallas_call | solution.py:349
  51.2 1.3 %collective-permute-start.11 = (bf16[64,3584]{1,0:T(8,128)(2,1)S(1)}, bf16[64,3584]{1,0:T(8,128)(2,1)S(1)}, u32[]{:S(2)}, u32[]{:S(2)}) collective-permute-start(bf16[64,3584]{1,0:T(8,128)(2,1)S(1)} %get-tuple-element.22.refs_0_), channel_id=1, source_target_pairs={{0,2},{6,4},{1,3},{7,5},{8,10},{14,12},{9,11},{15,13},{16,18},{22,... | collective-permute-start | bytes 1376264 | tf_op jit(solution)/shard_map/ppermute | solution.py:453
  52.5 1.3 %collective-permute-start.14 = (bf16[64,3584]{1,0:T(8,128)(2,1)S(1)}, bf16[64,3584]{1,0:T(8,128)(2,1)S(1)}, u32[]{:S(2)}, u32[]{:S(2)}) collective-permute-start(bf16[64,3584]{1,0:T(8,128)(2,1)S(1)} %get-tuple-element.24.refs_0_), channel_id=1, source_target_pairs={{0,2},{6,4},{1,3},{7,5},{8,10},{14,12},{9,11},{15,13},{16,18},{22,... | collective-permute-start | bytes 1376264 | tf_op jit(solution)/shard_map/ppermute | solution.py:453
  53.8 2.2 %collective-permute-done.12.refs_1_ = bf16[64,3584]{1,0:T(8,128)(2,1)S(1)} collective-permute-done((bf16[64,3584]{1,0:T(8,128)(2,1)S(1)}, bf16[64,3584]{1,0:T(8,128)(2,1)S(1)}, u32[]{:S(2)}, u32[]{:S(2)}) %collective-permute-start.12) | collective-permute-done | bytes 458784 | tf_op jit(solution)/shard_map/ppermute | solution.py:453
  55.9 0.1 shard_map.80.refs_2_
  56.0 4.1 %collective-permute-start.15 = (bf16[64,3584]{1,0:T(8,128)(2,1)S(1)}, bf16[64,3584]{1,0:T(8,128)(2,1)S(1)}, u32[]{:S(2)}, u32[]{:S(2)}) collective-permute-start(bf16[64,3584]{1,0:T(8,128)(2,1)S(1)} %shard_map.80.refs_2_), channel_id=1, source_target_pairs={{2,4},{4,2},{3,5},{5,3},{10,12},{12,10},{11,13},{13,11},{18,20},{2... | collective-permute-start | bytes 1376264 | tf_op jit(solution)/shard_map/ppermute | solution.py:453
  60.2 0.1 shard_map.79
  60.3 0.6 collective-permute-start.8
  60.9 6.0 %collective-permute-done.11.refs_1_ = bf16[64,3584]{1,0:T(8,128)(2,1)S(1)} collective-permute-done((bf16[64,3584]{1,0:T(8,128)(2,1)S(1)}, bf16[64,3584]{1,0:T(8,128)(2,1)S(1)}, u32[]{:S(2)}, u32[]{:S(2)}) %collective-permute-start.11) | collective-permute-done | bytes 458784 | tf_op jit(solution)/shard_map/ppermute | solution.py:453
  66.9 0.1 shard_map.81.refs_2_
  67.0 4.4 %collective-permute-start.13 = (bf16[64,3584]{1,0:T(8,128)(2,1)S(1)}, bf16[64,3584]{1,0:T(8,128)(2,1)S(1)}, u32[]{:S(2)}, u32[]{:S(2)}) collective-permute-start(bf16[64,3584]{1,0:T(8,128)(2,1)S(1)} %shard_map.81.refs_2_), channel_id=1, source_target_pairs={{2,4},{4,2},{3,5},{5,3},{10,12},{12,10},{11,13},{13,11},{18,20},{2... | collective-permute-start | bytes 1376264 | tf_op jit(solution)/shard_map/ppermute | solution.py:453
  71.4 1.3 %collective-permute-start.10 = (bf16[64,3584]{1,0:T(8,128)(2,1)}, bf16[64,3584]{1,0:T(8,128)(2,1)}, u32[]{:S(2)}, u32[]{:S(2)}) collective-permute-start(bf16[64,3584]{1,0:T(8,128)(2,1)} %get-tuple-element.21.refs_0_), channel_id=1, source_target_pairs={{0,2},{6,4},{1,3},{7,5},{8,10},{14,12},{9,11},{15,13},{16,18},{22,... | collective-permute-start | bytes 1376264 | tf_op jit(solution)/shard_map/ppermute | solution.py:453
  72.7 0.1 shard_map.82.refs_2_
  72.8 3.9 %collective-permute-done.14.refs_1_ = bf16[64,3584]{1,0:T(8,128)(2,1)S(1)} collective-permute-done((bf16[64,3584]{1,0:T(8,128)(2,1)S(1)}, bf16[64,3584]{1,0:T(8,128)(2,1)S(1)}, u32[]{:S(2)}, u32[]{:S(2)}) %collective-permute-start.14) | collective-permute-done | bytes 458784 | tf_op jit(solution)/shard_map/ppermute | solution.py:453
  76.7 0.1 shard_map.84.refs_2_
  76.8 4.4 %collective-permute-start.20 = (bf16[64,3584]{1,0:T(8,128)(2,1)S(1)}, bf16[64,3584]{1,0:T(8,128)(2,1)}, u32[]{:S(2)}, u32[]{:S(2)}) collective-permute-start(bf16[64,3584]{1,0:T(8,128)(2,1)S(1)} %shard_map.84.refs_2_), channel_id=1, source_target_pairs={{2,5},{3,4},{4,3},{5,2},{10,13},{11,12},{12,11},{13,10},{18,21},{1... | collective-permute-start | bytes 1376264 | tf_op jit(solution)/shard_map/ppermute | solution.py:454
  81.2 0.8 slice.19
  82.0 1.3 %collective-permute-start.19 = (bf16[64,3584]{1,0:T(8,128)(2,1)}, bf16[64,3584]{1,0:T(8,128)(2,1)}, u32[]{:S(2)}, u32[]{:S(2)}) collective-permute-start(bf16[64,3584]{1,0:T(8,128)(2,1)} %slice.19), channel_id=1, source_target_pairs={{0,2},{6,4},{1,3},{7,5},{8,10},{14,12},{9,11},{15,13},{16,18},{22,... | collective-permute-start | bytes 1376264 | tf_op jit(solution)/shard_map/ppermute | solution.py:453
  83.4 0.8 copy-done.2
  84.1 7.0 %collective-permute-start.21 = (bf16[64,3584]{1,0:T(8,128)(2,1)S(1)}, bf16[64,3584]{1,0:T(8,128)(2,1)}, u32[]{:S(2)}, u32[]{:S(2)}) collective-permute-start(bf16[64,3584]{1,0:T(8,128)(2,1)S(1)} %shard_map.82.refs_2_), channel_id=1, source_target_pairs={{4,7},{5,6},{2,1},{3,0},{12,15},{13,14},{10,9},{11,8},{20,23},{21,... | collective-permute-start | bytes 1376264 | tf_op jit(solution)/shard_map/ppermute | solution.py:454
  91.2 1.0 copy-done.3
  92.3 1.3 %collective-permute-start.18 = (bf16[64,3584]{1,0:T(8,128)(2,1)S(1)}, bf16[64,3584]{1,0:T(8,128)(2,1)S(1)}, u32[]{:S(2)}, u32[]{:S(2)}) collective-permute-start(bf16[64,3584]{1,0:T(8,128)(2,1)S(1)} %shard_map.85.refs_2_), channel_id=1, source_target_pairs={{4,7},{5,6},{2,1},{3,0},{12,15},{13,14},{10,9},{11,8},{20,23},{21,... | collective-permute-start | bytes 1376264 | tf_op jit(solution)/shard_map/ppermute | solution.py:454
  93.7 1.3 %shard_map.86 = bf16[64,3584]{1,0:T(8,128)(2,1)S(1)} custom-call(bf16[64,3584]{1,0:T(8,128)(2,1)} %get-tuple-element.21.refs_0_, bf16[64,3584]{1,0:T(8,128)(2,1)} %collective-permute-done.10.refs_1_, bf16[64,3584]{1,0:T(8,128)(2,1)S(1)} %shard_map.85.refs_2_), custom_call_target="tpu_custom_call" | custom-call | tf_op jit(solution)/shard_map/pallas_call | solution.py:379
  95.0 2.3 %collective-permute-start.17 = (bf16[64,3584]{1,0:T(8,128)(2,1)S(1)}, bf16[64,3584]{1,0:T(8,128)(2,1)S(1)}, u32[]{:S(2)}, u32[]{:S(2)}) collective-permute-start(bf16[64,3584]{1,0:T(8,128)(2,1)S(1)} %shard_map.86), channel_id=1, source_target_pairs={{2,5},{3,4},{4,3},{5,2},{10,13},{11,12},{12,11},{13,10},{18,21},{1... | collective-permute-start | bytes 1376264 | tf_op jit(solution)/shard_map/ppermute | solution.py:454
  97.3 1.1 slice.17
  98.4 1.3 %collective-permute-start.9 = (bf16[64,3584]{1,0:T(8,128)(2,1)S(1)}, bf16[64,3584]{1,0:T(8,128)(2,1)S(1)}, u32[]{:S(2)}, u32[]{:S(2)}) collective-permute-start(bf16[64,3584]{1,0:T(8,128)(2,1)S(1)} %slice.17), channel_id=1, source_target_pairs={{0,2},{6,4},{1,3},{7,5},{8,10},{14,12},{9,11},{15,13},{16,18},{22,... | collective-permute-start | bytes 1376264 | tf_op jit(solution)/shard_map/ppermute | solution.py:453
  99.7 1.7 %collective-permute-done.21.refs_2_ = bf16[64,3584]{1,0:T(8,128)(2,1)} collective-permute-done((bf16[64,3584]{1,0:T(8,128)(2,1)S(1)}, bf16[64,3584]{1,0:T(8,128)(2,1)}, u32[]{:S(2)}, u32[]{:S(2)}) %collective-permute-start.21) | collective-permute-done | bytes 458784 | tf_op jit(solution)/shard_map/ppermute | solution.py:454
  101.3 2.4 %shard_map.87.refs_3_ = bf16[64,7168]{1,0:T(8,128)(2,1)} custom-call(s32[3]{0:T(128)S(1)} %add_convert_fusion.flag_ref, bf16[128,3584]{1,0:T(8,128)(2,1)S(1)} %collective-permute-done.16.refs_3_.pair_ref, bf16[64,3584]{1,0:T(8,128)(2,1)} %collective-permute-done.19.refs_0_, bf16[64,3584]{1,0:T(8,128)(2,1)} %collective-permute-done.20.refs_1_, ...), custom_call_target="tpu_custom_call" | custom-call | flops 10000000000 | tf_op jit(solution)/shard_map/pallas_call | solution.py:418
  103.7 3.6 %collective-permute-done.17.refs_1_ = bf16[64,3584]{1,0:T(8,128)(2,1)S(1)} collective-permute-done((bf16[64,3584]{1,0:T(8,128)(2,1)S(1)}, bf16[64,3584]{1,0:T(8,128)(2,1)S(1)}, u32[]{:S(2)}, u32[]{:S(2)}) %collective-permute-start.17) | collective-permute-done | bytes 458784 | tf_op jit(solution)/shard_map/ppermute | solution.py:454
  107.3 0.2 collective-permute-done.18.refs_2_
  107.6 4.2 %collective-permute-done.9.refs_0_ = bf16[64,3584]{1,0:T(8,128)(2,1)S(1)} collective-permute-done((bf16[64,3584]{1,0:T(8,128)(2,1)S(1)}, bf16[64,3584]{1,0:T(8,128)(2,1)S(1)}, u32[]{:S(2)}, u32[]{:S(2)}) %collective-permute-start.9) | collective-permute-done | bytes 458784 | tf_op jit(solution)/shard_map/ppermute | solution.py:453
  111.7 2.3 %shard_map.88 = bf16[64,7168]{1,0:T(8,128)(2,1)} custom-call(s32[3]{0:T(128)S(1)} %add_convert_fusion.flag_ref, bf16[128,3584]{1,0:T(8,128)(2,1)} %collective-permute-done.8.pair_ref, bf16[64,3584]{1,0:T(8,128)(2,1)S(1)} %collective-permute-done.9.refs_0_, bf16[64,3584]{1,0:T(8,128)(2,1)S(1)} %collective-permute-done.17.refs_1_, ...), custom_call_target="tpu_custom_call", output_to_operand_aliasing={{}: (5, {})} | custom-call | flops 10000000000 | tf_op jit(solution)/shard_map/pallas_call | solution.py:418
  (28 shorter events, 0.4 us)
Async XLA Ops:
  1.1 4.5 %collective-permute-start = (bf16[64,640]{1,0:T(8,128)(2,1)S(1)}, bf16[64,640]{1,0:T(8,128)(2,1)S(1)}, u32[]{:S(2)}, u32[]{:S(2)}) collective-permute-start(bf16[64,640]{1,0:T(8,128)(2,1)S(1)} %shard_map.74.refs_0_), channel_id=1, source_target_pairs={{0,2},{2,0},{4,6},{6,4},{1,3},{3,1},{5,7},{7,5},{8,10},{10,8},{12,... | collective-permute-start | bytes 245768 | tf_op jit(solution)/shard_map/ppermute | solution.py:120
  5.6 6.9 %collective-permute-start.1 = (bf16[128,640]{1,0:T(8,128)(2,1)S(1)}, bf16[128,640]{1,0:T(8,128)(2,1)S(1)}, u32[]{:S(2)}, u32[]{:S(2)}) collective-permute-start(bf16[128,640]{1,0:T(8,128)(2,1)S(1)} %shard_map.75.refs_4_), channel_id=1, source_target_pairs={{0,4},{2,6},{4,0},{6,2},{1,5},{3,7},{5,1},{7,3},{8,12},{10,14},{12... | collective-permute-start | bytes 491528 | tf_op jit(solution)/shard_map/ppermute | solution.py:120
  5.7 1.4 %copy-start.1 = (bf16[1,256,3072]{2,1,0:T(8,128)(2,1)S(1)}, bf16[1,256,3072]{2,1,0:T(8,128)(2,1)}, u32[]{:S(2)}) copy-start(bf16[1,256,3072]{2,1,0:T(8,128)(2,1)} %param.7) | copy-start | bytes 4718596
  7.1 0.7 copy-start.4
  7.8 11.4 %copy-start.5 = (bf16[1,64,7168]{2,1,0:T(8,128)(2,1)S(1)}, bf16[1,64,7168]{2,1,0:T(8,128)(2,1)}, u32[]{:S(2)}) copy-start(bf16[1,64,7168]{2,1,0:T(8,128)(2,1)} %param.12) | copy-start | bytes 2752516
  10.6 10.0 %copy-start = (bf16[2,256,2048]{2,1,0:T(8,128)(2,1)}, bf16[2,256,2048]{2,1,0:T(8,128)(2,1)S(1)}, u32[]{:S(2)}) copy-start(bf16[2,256,2048]{2,1,0:T(8,128)(2,1)S(1)} %get-tuple-element.16.refs_1_.refs_0_) | copy-start | bytes 6291460
  10.6 6.8 %collective-permute-start.2 = (bf16[128,640]{1,0:T(8,128)(2,1)S(1)}, bf16[128,640]{1,0:T(8,128)(2,1)S(1)}, u32[]{:S(2)}, u32[]{:S(2)}) collective-permute-start(bf16[128,640]{1,0:T(8,128)(2,1)S(1)} %shard_map.75.refs_4_), channel_id=1, source_target_pairs={{0,16},{8,24},{16,0},{24,8},{1,17},{9,25},{17,1},{25,9},{2,18},{10... | collective-permute-start | bytes 491528 | tf_op jit(solution)/shard_map/ppermute | solution.py:120
  12.5 6.7 %collective-permute-start.3 = (bf16[128,640]{1,0:T(8,128)(2,1)S(1)}, bf16[128,640]{1,0:T(8,128)(2,1)S(1)}, u32[]{:S(2)}, u32[]{:S(2)}) collective-permute-start(bf16[128,640]{1,0:T(8,128)(2,1)S(1)} %shard_map.76.refs_5_), channel_id=1, source_target_pairs={{0,16},{8,24},{16,0},{24,8},{1,17},{9,25},{17,1},{25,9},{2,18},{10... | collective-permute-start | bytes 491528 | tf_op jit(solution)/shard_map/ppermute | solution.py:120
  13.5 5.7 %collective-permute-start.4 = (bf16[128,640]{1,0:T(8,128)(2,1)S(1)}, bf16[128,640]{1,0:T(8,128)(2,1)S(1)}, u32[]{:S(2)}, u32[]{:S(2)}) collective-permute-start(bf16[128,640]{1,0:T(8,128)(2,1)S(1)} %shard_map.75.refs_4_), channel_id=1, source_target_pairs={{0,8},{8,0},{16,24},{24,16},{1,9},{9,1},{17,25},{25,17},{2,10},{10... | collective-permute-start | bytes 491528 | tf_op jit(solution)/shard_map/ppermute | solution.py:120
  13.5 5.7 %collective-permute-start.5 = (bf16[128,640]{1,0:T(8,128)(2,1)S(1)}, bf16[128,640]{1,0:T(8,128)(2,1)S(1)}, u32[]{:S(2)}, u32[]{:S(2)}) collective-permute-start(bf16[128,640]{1,0:T(8,128)(2,1)S(1)} %shard_map.76.refs_5_), channel_id=1, source_target_pairs={{0,8},{8,0},{16,24},{24,16},{1,9},{9,1},{17,25},{25,17},{2,10},{10... | collective-permute-start | bytes 491528 | tf_op jit(solution)/shard_map/ppermute | solution.py:120
  17.4 1.9 %collective-permute-start.6 = (bf16[128,640]{1,0:T(8,128)(2,1)S(1)}, bf16[128,640]{1,0:T(8,128)(2,1)S(1)}, u32[]{:S(2)}, u32[]{:S(2)}) collective-permute-start(bf16[128,640]{1,0:T(8,128)(2,1)S(1)} %collective-permute-done.2.refs_6_), channel_id=1, source_target_pairs={{0,8},{8,0},{16,24},{24,16},{1,9},{9,1},{17,25},{25,17},{2,10},{10... | collective-permute-start | bytes 491528 | tf_op jit(solution)/shard_map/ppermute | solution.py:120
  19.2 1.4 %collective-permute-start.7 = (bf16[128,640]{1,0:T(8,128)(2,1)S(1)}, bf16[128,640]{1,0:T(8,128)(2,1)S(1)}, u32[]{:S(2)}, u32[]{:S(2)}) collective-permute-start(bf16[128,640]{1,0:T(8,128)(2,1)S(1)} %collective-permute-done.3.refs_7_), channel_id=1, source_target_pairs={{0,8},{8,0},{16,24},{24,16},{1,9},{9,1},{17,25},{25,17},{2,10},{10... | collective-permute-start | bytes 491528 | tf_op jit(solution)/shard_map/ppermute | solution.py:120
  39.7 37.1 %collective-permute-start.16 = (bf16[128,3584]{1,0:T(8,128)(2,1)S(1)}, bf16[128,3584]{1,0:T(8,128)(2,1)S(1)}, u32[]{:S(2)}, u32[]{:S(2)}) collective-permute-start(bf16[128,3584]{1,0:T(8,128)(2,1)S(1)} %shard_map.83), channel_id=1, source_target_pairs={{0,1},{1,0},{2,3},{3,2},{4,5},{5,4},{6,7},{7,6},{8,9},{9,8},{10,11... | collective-permute-start | bytes 2752520 | tf_op jit(solution)/shard_map/ppermute | solution.py:469
  41.0 14.9 %collective-permute-start.12 = (bf16[64,3584]{1,0:T(8,128)(2,1)S(1)}, bf16[64,3584]{1,0:T(8,128)(2,1)S(1)}, u32[]{:S(2)}, u32[]{:S(2)}) collective-permute-start(bf16[64,3584]{1,0:T(8,128)(2,1)S(1)} %get-tuple-element.23.refs_0_), channel_id=1, source_target_pairs={{0,2},{6,4},{1,3},{7,5},{8,10},{14,12},{9,11},{15,13},{16,18},{22,... | collective-permute-start | bytes 1376264 | tf_op jit(solution)/shard_map/ppermute | solution.py:453
  51.2 15.7 %collective-permute-start.11 = (bf16[64,3584]{1,0:T(8,128)(2,1)S(1)}, bf16[64,3584]{1,0:T(8,128)(2,1)S(1)}, u32[]{:S(2)}, u32[]{:S(2)}) collective-permute-start(bf16[64,3584]{1,0:T(8,128)(2,1)S(1)} %get-tuple-element.22.refs_0_), channel_id=1, source_target_pairs={{0,2},{6,4},{1,3},{7,5},{8,10},{14,12},{9,11},{15,13},{16,18},{22,... | collective-permute-start | bytes 1376264 | tf_op jit(solution)/shard_map/ppermute | solution.py:453
  52.5 24.2 %collective-permute-start.14 = (bf16[64,3584]{1,0:T(8,128)(2,1)S(1)}, bf16[64,3584]{1,0:T(8,128)(2,1)S(1)}, u32[]{:S(2)}, u32[]{:S(2)}) collective-permute-start(bf16[64,3584]{1,0:T(8,128)(2,1)S(1)} %get-tuple-element.24.refs_0_), channel_id=1, source_target_pairs={{0,2},{6,4},{1,3},{7,5},{8,10},{14,12},{9,11},{15,13},{16,18},{22,... | collective-permute-start | bytes 1376264 | tf_op jit(solution)/shard_map/ppermute | solution.py:453
  56.0 15.4 %collective-permute-start.15 = (bf16[64,3584]{1,0:T(8,128)(2,1)S(1)}, bf16[64,3584]{1,0:T(8,128)(2,1)S(1)}, u32[]{:S(2)}, u32[]{:S(2)}) collective-permute-start(bf16[64,3584]{1,0:T(8,128)(2,1)S(1)} %shard_map.80.refs_2_), channel_id=1, source_target_pairs={{2,4},{4,2},{3,5},{5,3},{10,12},{12,10},{11,13},{13,11},{18,20},{2... | collective-permute-start | bytes 1376264 | tf_op jit(solution)/shard_map/ppermute | solution.py:453
  60.3 34.7 %collective-permute-start.8 = (bf16[128,3584]{1,0:T(8,128)(2,1)S(1)}, bf16[128,3584]{1,0:T(8,128)(2,1)}, u32[]{:S(2)}, u32[]{:S(2)}) collective-permute-start(bf16[128,3584]{1,0:T(8,128)(2,1)S(1)} %shard_map.79), channel_id=1, source_target_pairs={{0,1},{1,0},{2,3},{3,2},{4,5},{5,4},{6,7},{7,6},{8,9},{9,8},{10,11... | collective-permute-start | bytes 2752520 | tf_op jit(solution)/shard_map/ppermute | solution.py:469
  67.0 16.4 %collective-permute-start.13 = (bf16[64,3584]{1,0:T(8,128)(2,1)S(1)}, bf16[64,3584]{1,0:T(8,128)(2,1)S(1)}, u32[]{:S(2)}, u32[]{:S(2)}) collective-permute-start(bf16[64,3584]{1,0:T(8,128)(2,1)S(1)} %shard_map.81.refs_2_), channel_id=1, source_target_pairs={{2,4},{4,2},{3,5},{5,3},{10,12},{12,10},{11,13},{13,11},{18,20},{2... | collective-permute-start | bytes 1376264 | tf_op jit(solution)/shard_map/ppermute | solution.py:453
  71.4 20.9 %collective-permute-start.10 = (bf16[64,3584]{1,0:T(8,128)(2,1)}, bf16[64,3584]{1,0:T(8,128)(2,1)}, u32[]{:S(2)}, u32[]{:S(2)}) collective-permute-start(bf16[64,3584]{1,0:T(8,128)(2,1)} %get-tuple-element.21.refs_0_), channel_id=1, source_target_pairs={{0,2},{6,4},{1,3},{7,5},{8,10},{14,12},{9,11},{15,13},{16,18},{22,... | collective-permute-start | bytes 1376264 | tf_op jit(solution)/shard_map/ppermute | solution.py:453
  76.8 21.5 %collective-permute-start.20 = (bf16[64,3584]{1,0:T(8,128)(2,1)S(1)}, bf16[64,3584]{1,0:T(8,128)(2,1)}, u32[]{:S(2)}, u32[]{:S(2)}) collective-permute-start(bf16[64,3584]{1,0:T(8,128)(2,1)S(1)} %shard_map.84.refs_2_), channel_id=1, source_target_pairs={{2,5},{3,4},{4,3},{5,2},{10,13},{11,12},{12,11},{13,10},{18,21},{1... | collective-permute-start | bytes 1376264 | tf_op jit(solution)/shard_map/ppermute | solution.py:454
  82.0 17.6 %collective-permute-start.19 = (bf16[64,3584]{1,0:T(8,128)(2,1)}, bf16[64,3584]{1,0:T(8,128)(2,1)}, u32[]{:S(2)}, u32[]{:S(2)}) collective-permute-start(bf16[64,3584]{1,0:T(8,128)(2,1)} %slice.19), channel_id=1, source_target_pairs={{0,2},{6,4},{1,3},{7,5},{8,10},{14,12},{9,11},{15,13},{16,18},{22,... | collective-permute-start | bytes 1376264 | tf_op jit(solution)/shard_map/ppermute | solution.py:453
  83.3 0.8 copy-start.2
  84.1 17.2 %collective-permute-start.21 = (bf16[64,3584]{1,0:T(8,128)(2,1)S(1)}, bf16[64,3584]{1,0:T(8,128)(2,1)}, u32[]{:S(2)}, u32[]{:S(2)}) collective-permute-start(bf16[64,3584]{1,0:T(8,128)(2,1)S(1)} %shard_map.82.refs_2_), channel_id=1, source_target_pairs={{4,7},{5,6},{2,1},{3,0},{12,15},{13,14},{10,9},{11,8},{20,23},{21,... | collective-permute-start | bytes 1376264 | tf_op jit(solution)/shard_map/ppermute | solution.py:454
  91.2 1.0 copy-start.3
  92.3 15.2 %collective-permute-start.18 = (bf16[64,3584]{1,0:T(8,128)(2,1)S(1)}, bf16[64,3584]{1,0:T(8,128)(2,1)S(1)}, u32[]{:S(2)}, u32[]{:S(2)}) collective-permute-start(bf16[64,3584]{1,0:T(8,128)(2,1)S(1)} %shard_map.85.refs_2_), channel_id=1, source_target_pairs={{4,7},{5,6},{2,1},{3,0},{12,15},{13,14},{10,9},{11,8},{20,23},{21,... | collective-permute-start | bytes 1376264 | tf_op jit(solution)/shard_map/ppermute | solution.py:454
  95.0 12.4 %collective-permute-start.17 = (bf16[64,3584]{1,0:T(8,128)(2,1)S(1)}, bf16[64,3584]{1,0:T(8,128)(2,1)S(1)}, u32[]{:S(2)}, u32[]{:S(2)}) collective-permute-start(bf16[64,3584]{1,0:T(8,128)(2,1)S(1)} %shard_map.86), channel_id=1, source_target_pairs={{2,5},{3,4},{4,3},{5,2},{10,13},{11,12},{12,11},{13,10},{18,21},{1... | collective-permute-start | bytes 1376264 | tf_op jit(solution)/shard_map/ppermute | solution.py:454
  98.4 13.4 %collective-permute-start.9 = (bf16[64,3584]{1,0:T(8,128)(2,1)S(1)}, bf16[64,3584]{1,0:T(8,128)(2,1)S(1)}, u32[]{:S(2)}, u32[]{:S(2)}) collective-permute-start(bf16[64,3584]{1,0:T(8,128)(2,1)S(1)} %slice.17), channel_id=1, source_target_pairs={{0,2},{6,4},{1,3},{7,5},{8,10},{14,12},{9,11},{15,13},{16,18},{22,... | collective-permute-start | bytes 1376264 | tf_op jit(solution)/shard_map/ppermute | solution.py:453

commit v5 on v4

--- a/solution.py
+++ b/solution.py
@@ -299,7 +299,7 @@
     steps = queries.shape[0]
     heads = steps * HEADS_STEP
     depth = heads * VDIM
-    tile = column_tile(0, size, TILE)
+    tile = column_tile(0, size, 4 * TILE)
     head_step = lambda i: jnp.minimum(i, steps - 1)
     column_step = lambda i: jnp.maximum(i - steps, 0)
     whole = lambda shape: pl.BlockSpec(shape, lambda i: (0, 0))

time: 115 us -> 113 us (0.983)
  Pallas kernels: 38.4 us -> 36.9 us
    pallas_call x1, Pallas kernels: 19 us -> 17.5 us  [attend(): pl.pallas_call(functools.partial(attention_kernel, len(pieces), steps), g...]
where the time goes in v5:
time: 113 us
  starting transfers between devices  38.4 us (34%)
  Pallas kernels  36.9 us (33%)
  waiting for transfers between devices  31 us (27%)
  local copies, waits for them, and re-layouts  5.79 us (5%)
    pallas_call x1, Pallas kernels, attend(): pl.pallas_call(functools.partial(attention_kernel, len(pieces), steps), g...  17.5 us
    ppermute x8, starting transfers between devices, send(): return lax.ppermute(value, 'tp', steps)  16.4 us
    ppermute x8, waiting for transfers between devices, send(): return lax.ppermute(value, 'tp', steps)  16 us
    ppermute x4, starting transfers between devices, send(): lax.ppermute(value, ('tp', 'pp'), [(2 * i + p, 2 * j + 1 - p) for i, j in...  14.9 us
    ppermute x8, waiting for transfers between devices, traded(): lax.ppermute(value, axis, [(i, i ^ step) for i in range(lax.axis_size(axi...  9.3 us
    pallas_call x1, Pallas kernels, project(): pl.pallas_call(project_kernel, grid=(size // tile,), out_shape=[jax.Shape...  8.85 us
    ppermute x4, waiting for transfers between devices, send(): lax.ppermute(value, ('tp', 'pp'), [(2 * i + p, 2 * j + 1 - p) for i, j in...  5.67 us
    ppermute x8, starting transfers between devices, traded(): lax.ppermute(value, axis, [(i, i ^ step) for i in range(lax.axis_size(axi...  5.14 us
  transfers between devices with their start and end apart: 22, of which 11 were waited for; matrix products, arithmetic and copies ran while one was open for 2% of the time, Pallas kernels for 14%

profile of v5, /device:TPU:16, one launch (start us, length us, event | category | flops | bytes accessed | tf_op | source)
XLA Modules:
  0.0 112.6 jit_solution(12899570211148539170)
XLA Ops:
  0.0 1.1 shard_map.74.refs_0_
  1.1 1.6 %collective-permute-start = (bf16[64,640]{1,0:T(8,128)(2,1)S(1)}, bf16[64,640]{1,0:T(8,128)(2,1)S(1)}, u32[]{:S(2)}, u32[]{:S(2)}) collective-permute-start(bf16[64,640]{1,0:T(8,128)(2,1)S(1)} %shard_map.74.refs_0_), channel_id=1, source_target_pairs={{0,2},{2,0},{4,6},{6,4},{1,3},{3,1},{5,7},{7,5},{8,10},{10,8},{12,... | collective-permute-start | bytes 245768 | tf_op jit(solution)/shard_map/ppermute | solution.py:120
  2.7 2.9 %collective-permute-done.refs_1_ = bf16[64,640]{1,0:T(8,128)(2,1)S(1)} collective-permute-done((bf16[64,640]{1,0:T(8,128)(2,1)S(1)}, bf16[64,640]{1,0:T(8,128)(2,1)S(1)}, u32[]{:S(2)}, u32[]{:S(2)}) %collective-permute-start) | collective-permute-done | bytes 81952 | tf_op jit(solution)/shard_map/ppermute | solution.py:120
  5.7 1.4 %copy-done.1 = bf16[1,256,3072]{2,1,0:T(8,128)(2,1)S(1)} copy-done((bf16[1,256,3072]{2,1,0:T(8,128)(2,1)S(1)}, bf16[1,256,3072]{2,1,0:T(8,128)(2,1)}, u32[]{:S(2)}) %copy-start.1) | copy-done | bytes 1572888
  7.1 0.7 copy-done.4
  7.8 2.8 %shard_map.73 = (bf16[2,256,2048]{2,1,0:T(8,128)(2,1)S(1)}, f32[256,1024]{1,0:T(8,128)S(1)}) custom-call(s32[8]{0:T(128)S(1)} %bitcast.11, bf16[256,3072]{1,0:T(8,128)(2,1)S(1)} %bitcast.9), custom_call_target="tpu_custom_call" | custom-call | flops 15728640 | bytes 4718592 | tf_op jit(solution)/shard_map/pallas_call | solution.py:172
  10.6 1.9 %collective-permute-start.2 = (bf16[128,640]{1,0:T(8,128)(2,1)S(1)}, bf16[128,640]{1,0:T(8,128)(2,1)S(1)}, u32[]{:S(2)}, u32[]{:S(2)}) collective-permute-start(bf16[128,640]{1,0:T(8,128)(2,1)S(1)} %shard_map.75.refs_4_), channel_id=1, source_target_pairs={{0,16},{8,24},{16,0},{24,8},{1,17},{9,25},{17,1},{25,9},{2,18},{10... | collective-permute-start | bytes 491528 | tf_op jit(solution)/shard_map/ppermute | solution.py:120
  12.5 1.0 collective-permute-start.3
  13.5 0.5 collective-permute-start.5
  14.0 3.4 %collective-permute-done.2.refs_6_ = bf16[128,640]{1,0:T(8,128)(2,1)S(1)} collective-permute-done((bf16[128,640]{1,0:T(8,128)(2,1)S(1)}, bf16[128,640]{1,0:T(8,128)(2,1)S(1)}, u32[]{:S(2)}, u32[]{:S(2)}) %collective-permute-start.2) | collective-permute-done | bytes 163872 | tf_op jit(solution)/shard_map/ppermute | solution.py:120
  17.4 1.8 %collective-permute-done.3.refs_7_ = bf16[128,640]{1,0:T(8,128)(2,1)S(1)} collective-permute-done((bf16[128,640]{1,0:T(8,128)(2,1)S(1)}, bf16[128,640]{1,0:T(8,128)(2,1)S(1)}, u32[]{:S(2)}, u32[]{:S(2)}) %collective-permute-start.3) | collective-permute-done | bytes 163872 | tf_op jit(solution)/shard_map/ppermute | solution.py:120
  19.3 1.3 %collective-permute-done.7.refs_11_ = bf16[128,640]{1,0:T(8,128)(2,1)S(1)} collective-permute-done((bf16[128,640]{1,0:T(8,128)(2,1)S(1)}, bf16[128,640]{1,0:T(8,128)(2,1)S(1)}, u32[]{:S(2)}, u32[]{:S(2)}) %collective-permute-start.7) | collective-permute-done | bytes 163872 | tf_op jit(solution)/shard_map/ppermute | solution.py:120
  20.6 17.5 %shard_map.77 = (bf16[256,2048]{1,0:T(8,128)(2,1)S(1)}, bf16[64,3584]{1,0:T(8,128)(2,1)S(1)}, bf16[64,3584]{1,0:T(8,128)(2,1)S(1)}, bf16[64,3584]{1,0:T(8,128)(2,1)S(1)}, bf16[64,3584]{1,0:T(8,128)(2,1)S(1)}) custom-call(bf16[2,256,2048]{2,1,0:T(8,128)(2,1)} %copy-done, f32[256,1024]{1,0:T(8,128)S(1)} %get-tuple-element.17.refs_2_.refs_1_, ...), custom_call_target="tpu_custom_call" | custom-call | flops 12348030976 | bytes 20971520 | tf_op jit(solution)/shard_map/pallas_call | solution.py:306
  38.0 0.1 shard_map.83
  38.1 1.4 %collective-permute-start.16 = (bf16[128,3584]{1,0:T(8,128)(2,1)S(1)}, bf16[128,3584]{1,0:T(8,128)(2,1)S(1)}, u32[]{:S(2)}, u32[]{:S(2)}) collective-permute-start(bf16[128,3584]{1,0:T(8,128)(2,1)S(1)} %shard_map.83), channel_id=1, source_target_pairs={{0,1},{1,0},{2,3},{3,2},{4,5},{5,4},{6,7},{7,6},{8,9},{9,8},{10,11... | collective-permute-start | bytes 2752520 | tf_op jit(solution)/shard_map/ppermute | solution.py:469
  39.5 1.5 %collective-permute-start.12 = (bf16[64,3584]{1,0:T(8,128)(2,1)S(1)}, bf16[64,3584]{1,0:T(8,128)(2,1)S(1)}, u32[]{:S(2)}, u32[]{:S(2)}) collective-permute-start(bf16[64,3584]{1,0:T(8,128)(2,1)S(1)} %get-tuple-element.23.refs_0_), channel_id=1, source_target_pairs={{0,2},{6,4},{1,3},{7,5},{8,10},{14,12},{9,11},{15,13},{16,18},{22,... | collective-permute-start | bytes 1376264 | tf_op jit(solution)/shard_map/ppermute | solution.py:453
  41.0 8.9 %shard_map.78 = (bf16[64,3584]{1,0:T(8,128)(2,1)S(1)}, bf16[64,3584]{1,0:T(8,128)(2,1)}, bf16[64,3584]{1,0:T(8,128)(2,1)S(1)}, bf16[64,3584]{1,0:T(8,128)(2,1)S(1)}) custom-call(bf16[256,2048]{1,0:T(8,128)(2,1)S(1)} %get-tuple-element.18.x_ref, bf16[2048,7168]{1,0:T(8,128)(2,1)} %bitcast.13, bf16[2048,7168]{1,0:T(8,128)(2,1)} %bitcast.14), custom_call_target="tpu_custom_call" | custom-call | flops 3758096384 | bytes 14680064 | tf_op jit(solution)/shard_map/pallas_call | solution.py:349
  49.8 1.3 %collective-permute-start.11 = (bf16[64,3584]{1,0:T(8,128)(2,1)S(1)}, bf16[64,3584]{1,0:T(8,128)(2,1)S(1)}, u32[]{:S(2)}, u32[]{:S(2)}) collective-permute-start(bf16[64,3584]{1,0:T(8,128)(2,1)S(1)} %get-tuple-element.22.refs_0_), channel_id=1, source_target_pairs={{0,2},{6,4},{1,3},{7,5},{8,10},{14,12},{9,11},{15,13},{16,18},{22,... | collective-permute-start | bytes 1376264 | tf_op jit(solution)/shard_map/ppermute | solution.py:453
  51.1 1.3 %collective-permute-start.14 = (bf16[64,3584]{1,0:T(8,128)(2,1)S(1)}, bf16[64,3584]{1,0:T(8,128)(2,1)S(1)}, u32[]{:S(2)}, u32[]{:S(2)}) collective-permute-start(bf16[64,3584]{1,0:T(8,128)(2,1)S(1)} %get-tuple-element.24.refs_0_), channel_id=1, source_target_pairs={{0,2},{6,4},{1,3},{7,5},{8,10},{14,12},{9,11},{15,13},{16,18},{22,... | collective-permute-start | bytes 1376264 | tf_op jit(solution)/shard_map/ppermute | solution.py:453
  52.4 2.0 %collective-permute-done.12.refs_1_ = bf16[64,3584]{1,0:T(8,128)(2,1)S(1)} collective-permute-done((bf16[64,3584]{1,0:T(8,128)(2,1)S(1)}, bf16[64,3584]{1,0:T(8,128)(2,1)S(1)}, u32[]{:S(2)}, u32[]{:S(2)}) %collective-permute-start.12) | collective-permute-done | bytes 458784 | tf_op jit(solution)/shard_map/ppermute | solution.py:453
  54.4 0.1 shard_map.80.refs_2_
  54.5 4.1 %collective-permute-start.15 = (bf16[64,3584]{1,0:T(8,128)(2,1)S(1)}, bf16[64,3584]{1,0:T(8,128)(2,1)S(1)}, u32[]{:S(2)}, u32[]{:S(2)}) collective-permute-start(bf16[64,3584]{1,0:T(8,128)(2,1)S(1)} %shard_map.80.refs_2_), channel_id=1, source_target_pairs={{2,4},{4,2},{3,5},{5,3},{10,12},{12,10},{11,13},{13,11},{18,20},{2... | collective-permute-start | bytes 1376264 | tf_op jit(solution)/shard_map/ppermute | solution.py:453
  58.6 0.1 shard_map.79
  58.8 0.6 collective-permute-start.8
  59.3 6.2 %collective-permute-done.11.refs_1_ = bf16[64,3584]{1,0:T(8,128)(2,1)S(1)} collective-permute-done((bf16[64,3584]{1,0:T(8,128)(2,1)S(1)}, bf16[64,3584]{1,0:T(8,128)(2,1)S(1)}, u32[]{:S(2)}, u32[]{:S(2)}) %collective-permute-start.11) | collective-permute-done | bytes 458784 | tf_op jit(solution)/shard_map/ppermute | solution.py:453
  65.5 0.1 shard_map.81.refs_2_
  65.6 4.4 %collective-permute-start.13 = (bf16[64,3584]{1,0:T(8,128)(2,1)S(1)}, bf16[64,3584]{1,0:T(8,128)(2,1)S(1)}, u32[]{:S(2)}, u32[]{:S(2)}) collective-permute-start(bf16[64,3584]{1,0:T(8,128)(2,1)S(1)} %shard_map.81.refs_2_), channel_id=1, source_target_pairs={{2,4},{4,2},{3,5},{5,3},{10,12},{12,10},{11,13},{13,11},{18,20},{2... | collective-permute-start | bytes 1376264 | tf_op jit(solution)/shard_map/ppermute | solution.py:453
  70.1 1.3 %collective-permute-start.10 = (bf16[64,3584]{1,0:T(8,128)(2,1)}, bf16[64,3584]{1,0:T(8,128)(2,1)}, u32[]{:S(2)}, u32[]{:S(2)}) collective-permute-start(bf16[64,3584]{1,0:T(8,128)(2,1)} %get-tuple-element.21.refs_0_), channel_id=1, source_target_pairs={{0,2},{6,4},{1,3},{7,5},{8,10},{14,12},{9,11},{15,13},{16,18},{22,... | collective-permute-start | bytes 1376264 | tf_op jit(solution)/shard_map/ppermute | solution.py:453
  71.4 0.1 shard_map.82.refs_2_
  71.5 3.9 %collective-permute-done.14.refs_1_ = bf16[64,3584]{1,0:T(8,128)(2,1)S(1)} collective-permute-done((bf16[64,3584]{1,0:T(8,128)(2,1)S(1)}, bf16[64,3584]{1,0:T(8,128)(2,1)S(1)}, u32[]{:S(2)}, u32[]{:S(2)}) %collective-permute-start.14) | collective-permute-done | bytes 458784 | tf_op jit(solution)/shard_map/ppermute | solution.py:453
  75.4 0.1 shard_map.84.refs_2_
  75.5 4.4 %collective-permute-start.20 = (bf16[64,3584]{1,0:T(8,128)(2,1)S(1)}, bf16[64,3584]{1,0:T(8,128)(2,1)}, u32[]{:S(2)}, u32[]{:S(2)}) collective-permute-start(bf16[64,3584]{1,0:T(8,128)(2,1)S(1)} %shard_map.84.refs_2_), channel_id=1, source_target_pairs={{2,5},{3,4},{4,3},{5,2},{10,13},{11,12},{12,11},{13,10},{18,21},{1... | collective-permute-start | bytes 1376264 | tf_op jit(solution)/shard_map/ppermute | solution.py:454
  79.9 0.8 slice.19
  80.7 1.3 %collective-permute-start.19 = (bf16[64,3584]{1,0:T(8,128)(2,1)}, bf16[64,3584]{1,0:T(8,128)(2,1)}, u32[]{:S(2)}, u32[]{:S(2)}) collective-permute-start(bf16[64,3584]{1,0:T(8,128)(2,1)} %slice.19), channel_id=1, source_target_pairs={{0,2},{6,4},{1,3},{7,5},{8,10},{14,12},{9,11},{15,13},{16,18},{22,... | collective-permute-start | bytes 1376264 | tf_op jit(solution)/shard_map/ppermute | solution.py:453
  82.0 0.8 copy-done.2
  82.8 7.0 %collective-permute-start.21 = (bf16[64,3584]{1,0:T(8,128)(2,1)S(1)}, bf16[64,3584]{1,0:T(8,128)(2,1)}, u32[]{:S(2)}, u32[]{:S(2)}) collective-permute-start(bf16[64,3584]{1,0:T(8,128)(2,1)S(1)} %shard_map.82.refs_2_), channel_id=1, source_target_pairs={{4,7},{5,6},{2,1},{3,0},{12,15},{13,14},{10,9},{11,8},{20,23},{21,... | collective-permute-start | bytes 1376264 | tf_op jit(solution)/shard_map/ppermute | solution.py:454
  89.9 1.0 copy-done.3
  91.0 1.3 %collective-permute-start.18 = (bf16[64,3584]{1,0:T(8,128)(2,1)S(1)}, bf16[64,3584]{1,0:T(8,128)(2,1)S(1)}, u32[]{:S(2)}, u32[]{:S(2)}) collective-permute-start(bf16[64,3584]{1,0:T(8,128)(2,1)S(1)} %shard_map.85.refs_2_), channel_id=1, source_target_pairs={{4,7},{5,6},{2,1},{3,0},{12,15},{13,14},{10,9},{11,8},{20,23},{21,... | collective-permute-start | bytes 1376264 | tf_op jit(solution)/shard_map/ppermute | solution.py:454
  92.3 1.3 %shard_map.86 = bf16[64,3584]{1,0:T(8,128)(2,1)S(1)} custom-call(bf16[64,3584]{1,0:T(8,128)(2,1)} %get-tuple-element.21.refs_0_, bf16[64,3584]{1,0:T(8,128)(2,1)} %collective-permute-done.10.refs_1_, bf16[64,3584]{1,0:T(8,128)(2,1)S(1)} %shard_map.85.refs_2_), custom_call_target="tpu_custom_call" | custom-call | tf_op jit(solution)/shard_map/pallas_call | solution.py:379
  93.6 2.1 %collective-permute-start.17 = (bf16[64,3584]{1,0:T(8,128)(2,1)S(1)}, bf16[64,3584]{1,0:T(8,128)(2,1)S(1)}, u32[]{:S(2)}, u32[]{:S(2)}) collective-permute-start(bf16[64,3584]{1,0:T(8,128)(2,1)S(1)} %shard_map.86), channel_id=1, source_target_pairs={{2,5},{3,4},{4,3},{5,2},{10,13},{11,12},{12,11},{13,10},{18,21},{1... | collective-permute-start | bytes 1376264 | tf_op jit(solution)/shard_map/ppermute | solution.py:454
  95.8 1.1 slice.17
  96.8 1.3 %collective-permute-start.9 = (bf16[64,3584]{1,0:T(8,128)(2,1)S(1)}, bf16[64,3584]{1,0:T(8,128)(2,1)S(1)}, u32[]{:S(2)}, u32[]{:S(2)}) collective-permute-start(bf16[64,3584]{1,0:T(8,128)(2,1)S(1)} %slice.17), channel_id=1, source_target_pairs={{0,2},{6,4},{1,3},{7,5},{8,10},{14,12},{9,11},{15,13},{16,18},{22,... | collective-permute-start | bytes 1376264 | tf_op jit(solution)/shard_map/ppermute | solution.py:453
  98.1 1.8 %collective-permute-done.21.refs_2_ = bf16[64,3584]{1,0:T(8,128)(2,1)} collective-permute-done((bf16[64,3584]{1,0:T(8,128)(2,1)S(1)}, bf16[64,3584]{1,0:T(8,128)(2,1)}, u32[]{:S(2)}, u32[]{:S(2)}) %collective-permute-start.21) | collective-permute-done | bytes 458784 | tf_op jit(solution)/shard_map/ppermute | solution.py:454
  100.0 2.4 %shard_map.87.refs_3_ = bf16[64,7168]{1,0:T(8,128)(2,1)} custom-call(s32[3]{0:T(128)S(1)} %add_convert_fusion.flag_ref, bf16[128,3584]{1,0:T(8,128)(2,1)S(1)} %collective-permute-done.16.refs_3_.pair_ref, bf16[64,3584]{1,0:T(8,128)(2,1)} %collective-permute-done.19.refs_0_, bf16[64,3584]{1,0:T(8,128)(2,1)} %collective-permute-done.20.refs_1_, ...), custom_call_target="tpu_custom_call" | custom-call | flops 10000000000 | tf_op jit(solution)/shard_map/pallas_call | solution.py:418
  102.4 3.6 %collective-permute-done.17.refs_1_ = bf16[64,3584]{1,0:T(8,128)(2,1)S(1)} collective-permute-done((bf16[64,3584]{1,0:T(8,128)(2,1)S(1)}, bf16[64,3584]{1,0:T(8,128)(2,1)S(1)}, u32[]{:S(2)}, u32[]{:S(2)}) %collective-permute-start.17) | collective-permute-done | bytes 458784 | tf_op jit(solution)/shard_map/ppermute | solution.py:454
  106.0 0.2 collective-permute-done.18.refs_2_
  106.2 4.0 %collective-permute-done.9.refs_0_ = bf16[64,3584]{1,0:T(8,128)(2,1)S(1)} collective-permute-done((bf16[64,3584]{1,0:T(8,128)(2,1)S(1)}, bf16[64,3584]{1,0:T(8,128)(2,1)S(1)}, u32[]{:S(2)}, u32[]{:S(2)}) %collective-permute-start.9) | collective-permute-done | bytes 458784 | tf_op jit(solution)/shard_map/ppermute | solution.py:453
  110.2 2.3 %shard_map.88 = bf16[64,7168]{1,0:T(8,128)(2,1)} custom-call(s32[3]{0:T(128)S(1)} %add_convert_fusion.flag_ref, bf16[128,3584]{1,0:T(8,128)(2,1)} %collective-permute-done.8.pair_ref, bf16[64,3584]{1,0:T(8,128)(2,1)S(1)} %collective-permute-done.9.refs_0_, bf16[64,3584]{1,0:T(8,128)(2,1)S(1)} %collective-permute-done.17.refs_1_, ...), custom_call_target="tpu_custom_call", output_to_operand_aliasing={{}: (5, {})} | custom-call | flops 10000000000 | tf_op jit(solution)/shard_map/pallas_call | solution.py:418
  (28 shorter events, 0.4 us)
Async XLA Ops:
  1.1 4.5 %collective-permute-start = (bf16[64,640]{1,0:T(8,128)(2,1)S(1)}, bf16[64,640]{1,0:T(8,128)(2,1)S(1)}, u32[]{:S(2)}, u32[]{:S(2)}) collective-permute-start(bf16[64,640]{1,0:T(8,128)(2,1)S(1)} %shard_map.74.refs_0_), channel_id=1, source_target_pairs={{0,2},{2,0},{4,6},{6,4},{1,3},{3,1},{5,7},{7,5},{8,10},{10,8},{12,... | collective-permute-start | bytes 245768 | tf_op jit(solution)/shard_map/ppermute | solution.py:120
  5.6 6.9 %collective-permute-start.1 = (bf16[128,640]{1,0:T(8,128)(2,1)S(1)}, bf16[128,640]{1,0:T(8,128)(2,1)S(1)}, u32[]{:S(2)}, u32[]{:S(2)}) collective-permute-start(bf16[128,640]{1,0:T(8,128)(2,1)S(1)} %shard_map.75.refs_4_), channel_id=1, source_target_pairs={{0,4},{2,6},{4,0},{6,2},{1,5},{3,7},{5,1},{7,3},{8,12},{10,14},{12... | collective-permute-start | bytes 491528 | tf_op jit(solution)/shard_map/ppermute | solution.py:120
  5.7 1.4 %copy-start.1 = (bf16[1,256,3072]{2,1,0:T(8,128)(2,1)S(1)}, bf16[1,256,3072]{2,1,0:T(8,128)(2,1)}, u32[]{:S(2)}) copy-start(bf16[1,256,3072]{2,1,0:T(8,128)(2,1)} %param.7) | copy-start | bytes 4718596
  7.1 0.7 copy-start.4
  7.8 11.4 %copy-start.5 = (bf16[1,64,7168]{2,1,0:T(8,128)(2,1)S(1)}, bf16[1,64,7168]{2,1,0:T(8,128)(2,1)}, u32[]{:S(2)}) copy-start(bf16[1,64,7168]{2,1,0:T(8,128)(2,1)} %param.12) | copy-start | bytes 2752516
  10.6 10.0 %copy-start = (bf16[2,256,2048]{2,1,0:T(8,128)(2,1)}, bf16[2,256,2048]{2,1,0:T(8,128)(2,1)S(1)}, u32[]{:S(2)}) copy-start(bf16[2,256,2048]{2,1,0:T(8,128)(2,1)S(1)} %get-tuple-element.16.refs_1_.refs_0_) | copy-start | bytes 6291460
  10.6 6.8 %collective-permute-start.2 = (bf16[128,640]{1,0:T(8,128)(2,1)S(1)}, bf16[128,640]{1,0:T(8,128)(2,1)S(1)}, u32[]{:S(2)}, u32[]{:S(2)}) collective-permute-start(bf16[128,640]{1,0:T(8,128)(2,1)S(1)} %shard_map.75.refs_4_), channel_id=1, source_target_pairs={{0,16},{8,24},{16,0},{24,8},{1,17},{9,25},{17,1},{25,9},{2,18},{10... | collective-permute-start | bytes 491528 | tf_op jit(solution)/shard_map/ppermute | solution.py:120
  12.5 6.7 %collective-permute-start.3 = (bf16[128,640]{1,0:T(8,128)(2,1)S(1)}, bf16[128,640]{1,0:T(8,128)(2,1)S(1)}, u32[]{:S(2)}, u32[]{:S(2)}) collective-permute-start(bf16[128,640]{1,0:T(8,128)(2,1)S(1)} %shard_map.76.refs_5_), channel_id=1, source_target_pairs={{0,16},{8,24},{16,0},{24,8},{1,17},{9,25},{17,1},{25,9},{2,18},{10... | collective-permute-start | bytes 491528 | tf_op jit(solution)/shard_map/ppermute | solution.py:120
  13.5 5.7 %collective-permute-start.4 = (bf16[128,640]{1,0:T(8,128)(2,1)S(1)}, bf16[128,640]{1,0:T(8,128)(2,1)S(1)}, u32[]{:S(2)}, u32[]{:S(2)}) collective-permute-start(bf16[128,640]{1,0:T(8,128)(2,1)S(1)} %shard_map.75.refs_4_), channel_id=1, source_target_pairs={{0,8},{8,0},{16,24},{24,16},{1,9},{9,1},{17,25},{25,17},{2,10},{10... | collective-permute-start | bytes 491528 | tf_op jit(solution)/shard_map/ppermute | solution.py:120
  13.5 5.7 %collective-permute-start.5 = (bf16[128,640]{1,0:T(8,128)(2,1)S(1)}, bf16[128,640]{1,0:T(8,128)(2,1)S(1)}, u32[]{:S(2)}, u32[]{:S(2)}) collective-permute-start(bf16[128,640]{1,0:T(8,128)(2,1)S(1)} %shard_map.76.refs_5_), channel_id=1, source_target_pairs={{0,8},{8,0},{16,24},{24,16},{1,9},{9,1},{17,25},{25,17},{2,10},{10... | collective-permute-start | bytes 491528 | tf_op jit(solution)/shard_map/ppermute | solution.py:120
  17.4 1.9 %collective-permute-start.6 = (bf16[128,640]{1,0:T(8,128)(2,1)S(1)}, bf16[128,640]{1,0:T(8,128)(2,1)S(1)}, u32[]{:S(2)}, u32[]{:S(2)}) collective-permute-start(bf16[128,640]{1,0:T(8,128)(2,1)S(1)} %collective-permute-done.2.refs_6_), channel_id=1, source_target_pairs={{0,8},{8,0},{16,24},{24,16},{1,9},{9,1},{17,25},{25,17},{2,10},{10... | collective-permute-start | bytes 491528 | tf_op jit(solution)/shard_map/ppermute | solution.py:120
  19.2 1.4 %collective-permute-start.7 = (bf16[128,640]{1,0:T(8,128)(2,1)S(1)}, bf16[128,640]{1,0:T(8,128)(2,1)S(1)}, u32[]{:S(2)}, u32[]{:S(2)}) collective-permute-start(bf16[128,640]{1,0:T(8,128)(2,1)S(1)} %collective-permute-done.3.refs_7_), channel_id=1, source_target_pairs={{0,8},{8,0},{16,24},{24,16},{1,9},{9,1},{17,25},{25,17},{2,10},{10... | collective-permute-start | bytes 491528 | tf_op jit(solution)/shard_map/ppermute | solution.py:120
  38.1 37.2 %collective-permute-start.16 = (bf16[128,3584]{1,0:T(8,128)(2,1)S(1)}, bf16[128,3584]{1,0:T(8,128)(2,1)S(1)}, u32[]{:S(2)}, u32[]{:S(2)}) collective-permute-start(bf16[128,3584]{1,0:T(8,128)(2,1)S(1)} %shard_map.83), channel_id=1, source_target_pairs={{0,1},{1,0},{2,3},{3,2},{4,5},{5,4},{6,7},{7,6},{8,9},{9,8},{10,11... | collective-permute-start | bytes 2752520 | tf_op jit(solution)/shard_map/ppermute | solution.py:469
  39.5 14.9 %collective-permute-start.12 = (bf16[64,3584]{1,0:T(8,128)(2,1)S(1)}, bf16[64,3584]{1,0:T(8,128)(2,1)S(1)}, u32[]{:S(2)}, u32[]{:S(2)}) collective-permute-start(bf16[64,3584]{1,0:T(8,128)(2,1)S(1)} %get-tuple-element.23.refs_0_), channel_id=1, source_target_pairs={{0,2},{6,4},{1,3},{7,5},{8,10},{14,12},{9,11},{15,13},{16,18},{22,... | collective-permute-start | bytes 1376264 | tf_op jit(solution)/shard_map/ppermute | solution.py:453
  49.8 15.7 %collective-permute-start.11 = (bf16[64,3584]{1,0:T(8,128)(2,1)S(1)}, bf16[64,3584]{1,0:T(8,128)(2,1)S(1)}, u32[]{:S(2)}, u32[]{:S(2)}) collective-permute-start(bf16[64,3584]{1,0:T(8,128)(2,1)S(1)} %get-tuple-element.22.refs_0_), channel_id=1, source_target_pairs={{0,2},{6,4},{1,3},{7,5},{8,10},{14,12},{9,11},{15,13},{16,18},{22,... | collective-permute-start | bytes 1376264 | tf_op jit(solution)/shard_map/ppermute | solution.py:453
  51.1 24.2 %collective-permute-start.14 = (bf16[64,3584]{1,0:T(8,128)(2,1)S(1)}, bf16[64,3584]{1,0:T(8,128)(2,1)S(1)}, u32[]{:S(2)}, u32[]{:S(2)}) collective-permute-start(bf16[64,3584]{1,0:T(8,128)(2,1)S(1)} %get-tuple-element.24.refs_0_), channel_id=1, source_target_pairs={{0,2},{6,4},{1,3},{7,5},{8,10},{14,12},{9,11},{15,13},{16,18},{22,... | collective-permute-start | bytes 1376264 | tf_op jit(solution)/shard_map/ppermute | solution.py:453
  54.5 15.6 %collective-permute-start.15 = (bf16[64,3584]{1,0:T(8,128)(2,1)S(1)}, bf16[64,3584]{1,0:T(8,128)(2,1)S(1)}, u32[]{:S(2)}, u32[]{:S(2)}) collective-permute-start(bf16[64,3584]{1,0:T(8,128)(2,1)S(1)} %shard_map.80.refs_2_), channel_id=1, source_target_pairs={{2,4},{4,2},{3,5},{5,3},{10,12},{12,10},{11,13},{13,11},{18,20},{2... | collective-permute-start | bytes 1376264 | tf_op jit(solution)/shard_map/ppermute | solution.py:453
  58.8 34.9 %collective-permute-start.8 = (bf16[128,3584]{1,0:T(8,128)(2,1)S(1)}, bf16[128,3584]{1,0:T(8,128)(2,1)}, u32[]{:S(2)}, u32[]{:S(2)}) collective-permute-start(bf16[128,3584]{1,0:T(8,128)(2,1)S(1)} %shard_map.79), channel_id=1, source_target_pairs={{0,1},{1,0},{2,3},{3,2},{4,5},{5,4},{6,7},{7,6},{8,9},{9,8},{10,11... | collective-permute-start | bytes 2752520 | tf_op jit(solution)/shard_map/ppermute | solution.py:469
  65.6 16.4 %collective-permute-start.13 = (bf16[64,3584]{1,0:T(8,128)(2,1)S(1)}, bf16[64,3584]{1,0:T(8,128)(2,1)S(1)}, u32[]{:S(2)}, u32[]{:S(2)}) collective-permute-start(bf16[64,3584]{1,0:T(8,128)(2,1)S(1)} %shard_map.81.refs_2_), channel_id=1, source_target_pairs={{2,4},{4,2},{3,5},{5,3},{10,12},{12,10},{11,13},{13,11},{18,20},{2... | collective-permute-start | bytes 1376264 | tf_op jit(solution)/shard_map/ppermute | solution.py:453
  70.1 20.9 %collective-permute-start.10 = (bf16[64,3584]{1,0:T(8,128)(2,1)}, bf16[64,3584]{1,0:T(8,128)(2,1)}, u32[]{:S(2)}, u32[]{:S(2)}) collective-permute-start(bf16[64,3584]{1,0:T(8,128)(2,1)} %get-tuple-element.21.refs_0_), channel_id=1, source_target_pairs={{0,2},{6,4},{1,3},{7,5},{8,10},{14,12},{9,11},{15,13},{16,18},{22,... | collective-permute-start | bytes 1376264 | tf_op jit(solution)/shard_map/ppermute | solution.py:453
  75.5 21.3 %collective-permute-start.20 = (bf16[64,3584]{1,0:T(8,128)(2,1)S(1)}, bf16[64,3584]{1,0:T(8,128)(2,1)}, u32[]{:S(2)}, u32[]{:S(2)}) collective-permute-start(bf16[64,3584]{1,0:T(8,128)(2,1)S(1)} %shard_map.84.refs_2_), channel_id=1, source_target_pairs={{2,5},{3,4},{4,3},{5,2},{10,13},{11,12},{12,11},{13,10},{18,21},{1... | collective-permute-start | bytes 1376264 | tf_op jit(solution)/shard_map/ppermute | solution.py:454
  80.7 17.4 %collective-permute-start.19 = (bf16[64,3584]{1,0:T(8,128)(2,1)}, bf16[64,3584]{1,0:T(8,128)(2,1)}, u32[]{:S(2)}, u32[]{:S(2)}) collective-permute-start(bf16[64,3584]{1,0:T(8,128)(2,1)} %slice.19), channel_id=1, source_target_pairs={{0,2},{6,4},{1,3},{7,5},{8,10},{14,12},{9,11},{15,13},{16,18},{22,... | collective-permute-start | bytes 1376264 | tf_op jit(solution)/shard_map/ppermute | solution.py:453
  82.0 0.8 copy-start.2
  82.8 17.2 %collective-permute-start.21 = (bf16[64,3584]{1,0:T(8,128)(2,1)S(1)}, bf16[64,3584]{1,0:T(8,128)(2,1)}, u32[]{:S(2)}, u32[]{:S(2)}) collective-permute-start(bf16[64,3584]{1,0:T(8,128)(2,1)S(1)} %shard_map.82.refs_2_), channel_id=1, source_target_pairs={{4,7},{5,6},{2,1},{3,0},{12,15},{13,14},{10,9},{11,8},{20,23},{21,... | collective-permute-start | bytes 1376264 | tf_op jit(solution)/shard_map/ppermute | solution.py:454
  89.9 1.0 copy-start.3
  91.0 15.2 %collective-permute-start.18 = (bf16[64,3584]{1,0:T(8,128)(2,1)S(1)}, bf16[64,3584]{1,0:T(8,128)(2,1)S(1)}, u32[]{:S(2)}, u32[]{:S(2)}) collective-permute-start(bf16[64,3584]{1,0:T(8,128)(2,1)S(1)} %shard_map.85.refs_2_), channel_id=1, source_target_pairs={{4,7},{5,6},{2,1},{3,0},{12,15},{13,14},{10,9},{11,8},{20,23},{21,... | collective-permute-start | bytes 1376264 | tf_op jit(solution)/shard_map/ppermute | solution.py:454
  93.6 12.4 %collective-permute-start.17 = (bf16[64,3584]{1,0:T(8,128)(2,1)S(1)}, bf16[64,3584]{1,0:T(8,128)(2,1)S(1)}, u32[]{:S(2)}, u32[]{:S(2)}) collective-permute-start(bf16[64,3584]{1,0:T(8,128)(2,1)S(1)} %shard_map.86), channel_id=1, source_target_pairs={{2,5},{3,4},{4,3},{5,2},{10,13},{11,12},{12,11},{13,10},{18,21},{1... | collective-permute-start | bytes 1376264 | tf_op jit(solution)/shard_map/ppermute | solution.py:454
  96.8 13.4 %collective-permute-start.9 = (bf16[64,3584]{1,0:T(8,128)(2,1)S(1)}, bf16[64,3584]{1,0:T(8,128)(2,1)S(1)}, u32[]{:S(2)}, u32[]{:S(2)}) collective-permute-start(bf16[64,3584]{1,0:T(8,128)(2,1)S(1)} %slice.17), channel_id=1, source_target_pairs={{0,2},{6,4},{1,3},{7,5},{8,10},{14,12},{9,11},{15,13},{16,18},{22,... | collective-permute-start | bytes 1376264 | tf_op jit(solution)/shard_map/ppermute | solution.py:453

commit v6 on v5

--- a/solution.py
+++ b/solution.py
@@ -22,7 +22,7 @@
 MIB = 1024 * 1024
 PREPARE_VMEM = 16 * MIB
 PROJECT_VMEM = 24 * MIB
-ATTEND_VMEM = 48 * MIB
+ATTEND_VMEM = 40 * MIB
 ADD_VMEM = 8 * MIB
 FINAL_FLOPS = 10**10
 FIRST_SHARE = 50
@@ -309,7 +309,7 @@
         out_shape=[
             jax.ShapeDtypeStruct((rows, depth), jnp.bfloat16),
         ]
-        + [jax.ShapeDtypeStruct((rows // blocks, size), jnp.bfloat16)] * blocks,
+        + [pltpu.VMEM((rows // blocks, size), jnp.bfloat16)] * blocks,
         in_specs=[
             pl.BlockSpec(memory_space=pltpu.VMEM),
             pl.BlockSpec(memory_space=pltpu.VMEM),
@@ -344,12 +344,12 @@
 
 def project(rows, weights, lo, size, blocks):
     count, depth = rows.shape
-    tile = column_tile(lo, size, TILE)
+    tile = column_tile(lo, size, 2 * TILE)
     block = count // blocks
     return pl.pallas_call(
         project_kernel,
         grid=(size // tile,),
-        out_shape=[jax.ShapeDtypeStruct((block, size), jnp.bfloat16)] * blocks,
+        out_shape=[pltpu.VMEM((block, size), jnp.bfloat16)] * blocks,
         in_specs=[
             pl.BlockSpec((count, depth), lambda i: (0, 0)),
             pl.BlockSpec((depth // 2, tile), lambda i: (0, i + lo // tile)),
@@ -378,7 +378,7 @@
 def add_after(values, earlier):
     return pl.pallas_call(
         functools.partial(add_kernel, len(values)),
-        out_shape=jax.ShapeDtypeStruct(values[0].shape, jnp.bfloat16),
+        out_shape=pltpu.VMEM(values[0].shape, jnp.bfloat16),
         in_specs=[pl.BlockSpec(memory_space=pltpu.VMEM)] * len(values)
         + [pl.BlockSpec(memory_space=pl.ANY)] * len(earlier),
         out_specs=pl.BlockSpec(memory_space=pltpu.VMEM),
@@ -396,7 +396,7 @@
     rows, size = own.shape
     return pl.pallas_call(
         pair_kernel,
-        out_shape=jax.ShapeDtypeStruct((2 * rows, size), jnp.bfloat16),
+        out_shape=pltpu.VMEM((2 * rows, size), jnp.bfloat16),
         in_specs=[pl.BlockSpec(memory_space=pltpu.VMEM)] * 3,
         out_specs=pl.BlockSpec(memory_space=pltpu.VMEM),
         compiler_params=pltpu.CompilerParams(vmem_limit_bytes=ADD_VMEM),

time: 113 us -> 112 us (level)
  Pallas kernels: 36.9 us -> 34.2 us
  local copies, waits for them, and re-layouts: 5.79 us -> 6.96 us
    pallas_call x1, Pallas kernels: 17.5 us -> 15.5 us  [attend(): pl.pallas_call(functools.partial(attention_kernel, len(pieces), steps), g...]
    ppermute x8, waiting for transfers between devices: 9.3 us -> 8.13 us  [traded(): lax.ppermute(value, axis, [(i, i ^ step) for i in range(lax.axis_size(axi...]
    slice x1, local copies, waits for them, and re-layouts: 0.06 us -> 1.22 us  [local(): rest = residual[0][:, lo:lo + size]]
    unnamed x12 -> x10, local copies, waits for them, and re-layouts: 3.87 us -> 3.87 us
  transfers between devices with their start and end apart: 22 -> 22, of which waited for: 11 -> 11; matrix products, arithmetic and copies ran while one was open for 2% -> 3% of each run, Pallas kernels for 14% -> 14%
where the time goes in v6:
time: 112 us; the launch traced here: 111 us
  starting transfers between devices  39.4 us (35%)
  Pallas kernels  34.2 us (31%)
  waiting for transfers between devices  30.3 us (27%)
  local copies, waits for them, and re-layouts  6.96 us (6%)
    ppermute x8, starting transfers between devices, send(): return lax.ppermute(value, 'tp', steps)  16.4 us
    ppermute x8, waiting for transfers between devices, send(): return lax.ppermute(value, 'tp', steps)  16.3 us
    ppermute x4, starting transfers between devices, send(): lax.ppermute(value, ('tp', 'pp'), [(2 * i + p, 2 * j + 1 - p) for i, j in...  15.9 us
    pallas_call x1, Pallas kernels, attend(): pl.pallas_call(functools.partial(attention_kernel, len(pieces), steps), g...  15.5 us
    ppermute x8, waiting for transfers between devices, traded(): lax.ppermute(value, axis, [(i, i ^ step) for i in range(lax.axis_size(axi...  8.13 us
    pallas_call x1, Pallas kernels, project(): pl.pallas_call(project_kernel, grid=(size // tile,), out_shape=[pltpu.VME...  8.07 us
    ppermute x4, waiting for transfers between devices, send(): lax.ppermute(value, ('tp', 'pp'), [(2 * i + p, 2 * j + 1 - p) for i, j in...  5.77 us
    ppermute x8, starting transfers between devices, traded(): lax.ppermute(value, axis, [(i, i ^ step) for i in range(lax.axis_size(axi...  5.15 us
  transfers between devices with their start and end apart: 22, of which 11 were waited for; matrix products, arithmetic and copies ran while one was open for 3% of the time, Pallas kernels for 14%

profile of v6, /device:TPU:16, one launch (start us, length us, event | category | flops | bytes accessed | tf_op | source)
XLA Modules:
  0.0 111.3 jit_solution(3745055226972076531)
XLA Ops:
  0.0 1.1 shard_map.74.refs_0_
  1.1 1.6 %collective-permute-start = (bf16[64,640]{1,0:T(8,128)(2,1)S(1)}, bf16[64,640]{1,0:T(8,128)(2,1)S(1)}, u32[]{:S(2)}, u32[]{:S(2)}) collective-permute-start(bf16[64,640]{1,0:T(8,128)(2,1)S(1)} %shard_map.74.refs_0_), channel_id=1, source_target_pairs={{0,2},{2,0},{4,6},{6,4},{1,3},{3,1},{5,7},{7,5},{8,10},{10,8},{12,... | collective-permute-start | bytes 245768 | tf_op jit(solution)/shard_map/ppermute | solution.py:120
  2.7 2.9 %collective-permute-done.refs_1_ = bf16[64,640]{1,0:T(8,128)(2,1)S(1)} collective-permute-done((bf16[64,640]{1,0:T(8,128)(2,1)S(1)}, bf16[64,640]{1,0:T(8,128)(2,1)S(1)}, u32[]{:S(2)}, u32[]{:S(2)}) %collective-permute-start) | collective-permute-done | bytes 81952 | tf_op jit(solution)/shard_map/ppermute | solution.py:120
  5.7 1.4 %copy-done = bf16[1,256,3072]{2,1,0:T(8,128)(2,1)S(1)} copy-done((bf16[1,256,3072]{2,1,0:T(8,128)(2,1)S(1)}, bf16[1,256,3072]{2,1,0:T(8,128)(2,1)}, u32[]{:S(2)}) %copy-start) | copy-done | bytes 1572888
  7.1 0.7 copy-done.3
  7.8 2.8 %shard_map.73 = (bf16[2,256,2048]{2,1,0:T(8,128)(2,1)S(1)}, f32[256,1024]{1,0:T(8,128)S(1)}) custom-call(s32[8]{0:T(128)S(1)} %bitcast.11, bf16[256,3072]{1,0:T(8,128)(2,1)S(1)} %bitcast.9), custom_call_target="tpu_custom_call" | custom-call | flops 15728640 | bytes 4718592 | tf_op jit(solution)/shard_map/pallas_call | solution.py:172
  10.6 1.9 %collective-permute-start.2 = (bf16[128,640]{1,0:T(8,128)(2,1)S(1)}, bf16[128,640]{1,0:T(8,128)(2,1)S(1)}, u32[]{:S(2)}, u32[]{:S(2)}) collective-permute-start(bf16[128,640]{1,0:T(8,128)(2,1)S(1)} %shard_map.75.refs_4_), channel_id=1, source_target_pairs={{0,16},{8,24},{16,0},{24,8},{1,17},{9,25},{17,1},{25,9},{2,18},{10... | collective-permute-start | bytes 491528 | tf_op jit(solution)/shard_map/ppermute | solution.py:120
  12.5 1.0 collective-permute-start.3
  13.5 0.5 collective-permute-start.5
  14.0 3.4 %collective-permute-done.2.refs_6_ = bf16[128,640]{1,0:T(8,128)(2,1)S(1)} collective-permute-done((bf16[128,640]{1,0:T(8,128)(2,1)S(1)}, bf16[128,640]{1,0:T(8,128)(2,1)S(1)}, u32[]{:S(2)}, u32[]{:S(2)}) %collective-permute-start.2) | collective-permute-done | bytes 163872 | tf_op jit(solution)/shard_map/ppermute | solution.py:120
  17.4 1.8 %collective-permute-done.3.refs_7_ = bf16[128,640]{1,0:T(8,128)(2,1)S(1)} collective-permute-done((bf16[128,640]{1,0:T(8,128)(2,1)S(1)}, bf16[128,640]{1,0:T(8,128)(2,1)S(1)}, u32[]{:S(2)}, u32[]{:S(2)}) %collective-permute-start.3) | collective-permute-done | bytes 163872 | tf_op jit(solution)/shard_map/ppermute | solution.py:120
  19.1 1.2 %fusion = (bf16[64,3584]{1,0:T(8,128)(2,1)S(1)}, bf16[64,3584]{1,0:T(8,128)(2,1)S(1)}) fusion(bf16[64,7168]{1,0:T(8,128)(2,1)} %bitcast.16), kind=kLoop, calls=%fused_computation.1 | loop fusion | bytes 1835008 | tf_op jit(solution)/shard_map/slice | solution.py:467
  20.4 0.1 collective-permute-done.7.refs_11_
  20.5 15.5 %shard_map.77 = (bf16[256,2048]{1,0:T(8,128)(2,1)S(1)}, bf16[64,3584]{1,0:T(8,128)(2,1)S(1)}, bf16[64,3584]{1,0:T(8,128)(2,1)S(1)}, bf16[64,3584]{1,0:T(8,128)(2,1)S(1)}, bf16[64,3584]{1,0:T(8,128)(2,1)S(1)}) custom-call(bf16[2,256,2048]{2,1,0:T(8,128)(2,1)S(1)} %get-tuple-element.16.refs_1_.refs_0_, f32[256,1024]{1,0:T(8,128)S(1)} %get-tuple-element.17.refs_2_.refs_1_, ...), custom_call_target="tpu_custom_call" | custom-call | flops 12348030976 | bytes 20971520 | tf_op jit(solution)/shard_map/pallas_call | solution.py:306
  36.1 0.1 shard_map.83
  36.2 1.4 %collective-permute-start.16 = (bf16[128,3584]{1,0:T(8,128)(2,1)S(1)}, bf16[128,3584]{1,0:T(8,128)(2,1)S(1)}, u32[]{:S(2)}, u32[]{:S(2)}) collective-permute-start(bf16[128,3584]{1,0:T(8,128)(2,1)S(1)} %shard_map.83), channel_id=1, source_target_pairs={{0,1},{1,0},{2,3},{3,2},{4,5},{5,4},{6,7},{7,6},{8,9},{9,8},{10,11... | collective-permute-start | bytes 2752520 | tf_op jit(solution)/shard_map/ppermute | solution.py:469
  37.6 1.5 %collective-permute-start.12 = (bf16[64,3584]{1,0:T(8,128)(2,1)S(1)}, bf16[64,3584]{1,0:T(8,128)(2,1)S(1)}, u32[]{:S(2)}, u32[]{:S(2)}) collective-permute-start(bf16[64,3584]{1,0:T(8,128)(2,1)S(1)} %get-tuple-element.23.refs_0_), channel_id=1, source_target_pairs={{0,2},{6,4},{1,3},{7,5},{8,10},{14,12},{9,11},{15,13},{16,18},{22,... | collective-permute-start | bytes 1376264 | tf_op jit(solution)/shard_map/ppermute | solution.py:453
  39.1 8.1 %shard_map.78 = (bf16[64,3584]{1,0:T(8,128)(2,1)S(1)}, bf16[64,3584]{1,0:T(8,128)(2,1)}, bf16[64,3584]{1,0:T(8,128)(2,1)S(1)}, bf16[64,3584]{1,0:T(8,128)(2,1)S(1)}) custom-call(bf16[256,2048]{1,0:T(8,128)(2,1)S(1)} %get-tuple-element.18.x_ref, bf16[2048,7168]{1,0:T(8,128)(2,1)} %bitcast.14, bf16[2048,7168]{1,0:T(8,128)(2,1)} %bitcast.15), custom_call_target="tpu_custom_call" | custom-call | flops 3758096384 | bytes 14680064 | tf_op jit(solution)/shard_map/pallas_call | solution.py:349
  47.1 1.3 %collective-permute-start.11 = (bf16[64,3584]{1,0:T(8,128)(2,1)S(1)}, bf16[64,3584]{1,0:T(8,128)(2,1)S(1)}, u32[]{:S(2)}, u32[]{:S(2)}) collective-permute-start(bf16[64,3584]{1,0:T(8,128)(2,1)S(1)} %get-tuple-element.22.refs_0_), channel_id=1, source_target_pairs={{0,2},{6,4},{1,3},{7,5},{8,10},{14,12},{9,11},{15,13},{16,18},{22,... | collective-permute-start | bytes 1376264 | tf_op jit(solution)/shard_map/ppermute | solution.py:453
  48.4 1.3 %collective-permute-start.14 = (bf16[64,3584]{1,0:T(8,128)(2,1)S(1)}, bf16[64,3584]{1,0:T(8,128)(2,1)S(1)}, u32[]{:S(2)}, u32[]{:S(2)}) collective-permute-start(bf16[64,3584]{1,0:T(8,128)(2,1)S(1)} %get-tuple-element.24.refs_0_), channel_id=1, source_target_pairs={{0,2},{6,4},{1,3},{7,5},{8,10},{14,12},{9,11},{15,13},{16,18},{22,... | collective-permute-start | bytes 1376264 | tf_op jit(solution)/shard_map/ppermute | solution.py:453
  49.7 3.3 %collective-permute-done.12.refs_1_ = bf16[64,3584]{1,0:T(8,128)(2,1)S(1)} collective-permute-done((bf16[64,3584]{1,0:T(8,128)(2,1)S(1)}, bf16[64,3584]{1,0:T(8,128)(2,1)S(1)}, u32[]{:S(2)}, u32[]{:S(2)}) %collective-permute-start.12) | collective-permute-done | bytes 458784 | tf_op jit(solution)/shard_map/ppermute | solution.py:453
  53.0 0.1 shard_map.80.refs_2_
  53.1 4.1 %collective-permute-start.15 = (bf16[64,3584]{1,0:T(8,128)(2,1)S(1)}, bf16[64,3584]{1,0:T(8,128)(2,1)S(1)}, u32[]{:S(2)}, u32[]{:S(2)}) collective-permute-start(bf16[64,3584]{1,0:T(8,128)(2,1)S(1)} %shard_map.80.refs_2_), channel_id=1, source_target_pairs={{2,4},{4,2},{3,5},{5,3},{10,12},{12,10},{11,13},{13,11},{18,20},{2... | collective-permute-start | bytes 1376264 | tf_op jit(solution)/shard_map/ppermute | solution.py:453
  57.2 0.1 shard_map.79
  57.3 0.6 collective-permute-start.8
  57.9 4.9 %collective-permute-done.11.refs_1_ = bf16[64,3584]{1,0:T(8,128)(2,1)S(1)} collective-permute-done((bf16[64,3584]{1,0:T(8,128)(2,1)S(1)}, bf16[64,3584]{1,0:T(8,128)(2,1)S(1)}, u32[]{:S(2)}, u32[]{:S(2)}) %collective-permute-start.11) | collective-permute-done | bytes 458784 | tf_op jit(solution)/shard_map/ppermute | solution.py:453
  62.9 0.1 shard_map.81.refs_2_
  63.0 4.4 %collective-permute-start.13 = (bf16[64,3584]{1,0:T(8,128)(2,1)S(1)}, bf16[64,3584]{1,0:T(8,128)(2,1)S(1)}, u32[]{:S(2)}, u32[]{:S(2)}) collective-permute-start(bf16[64,3584]{1,0:T(8,128)(2,1)S(1)} %shard_map.81.refs_2_), channel_id=1, source_target_pairs={{2,4},{4,2},{3,5},{5,3},{10,12},{12,10},{11,13},{13,11},{18,20},{2... | collective-permute-start | bytes 1376264 | tf_op jit(solution)/shard_map/ppermute | solution.py:453
  67.4 1.3 %collective-permute-start.10 = (bf16[64,3584]{1,0:T(8,128)(2,1)}, bf16[64,3584]{1,0:T(8,128)(2,1)}, u32[]{:S(2)}, u32[]{:S(2)}) collective-permute-start(bf16[64,3584]{1,0:T(8,128)(2,1)} %get-tuple-element.21.refs_0_), channel_id=1, source_target_pairs={{0,2},{6,4},{1,3},{7,5},{8,10},{14,12},{9,11},{15,13},{16,18},{22,... | collective-permute-start | bytes 1376264 | tf_op jit(solution)/shard_map/ppermute | solution.py:453
  68.7 0.1 shard_map.82.refs_2_
  68.8 3.9 %collective-permute-done.14.refs_1_ = bf16[64,3584]{1,0:T(8,128)(2,1)S(1)} collective-permute-done((bf16[64,3584]{1,0:T(8,128)(2,1)S(1)}, bf16[64,3584]{1,0:T(8,128)(2,1)S(1)}, u32[]{:S(2)}, u32[]{:S(2)}) %collective-permute-start.14) | collective-permute-done | bytes 458784 | tf_op jit(solution)/shard_map/ppermute | solution.py:453
  72.8 4.3 %collective-permute-start.20 = (bf16[64,3584]{1,0:T(8,128)(2,1)S(1)}, bf16[64,3584]{1,0:T(8,128)(2,1)}, u32[]{:S(2)}, u32[]{:S(2)}) collective-permute-start(bf16[64,3584]{1,0:T(8,128)(2,1)S(1)} %shard_map.84.refs_2_), channel_id=1, source_target_pairs={{2,5},{3,4},{4,3},{5,2},{10,13},{11,12},{12,11},{13,10},{18,21},{1... | collective-permute-start | bytes 1376264 | tf_op jit(solution)/shard_map/ppermute | solution.py:454
  77.1 0.8 slice.19
  78.0 1.3 %collective-permute-start.19 = (bf16[64,3584]{1,0:T(8,128)(2,1)}, bf16[64,3584]{1,0:T(8,128)(2,1)}, u32[]{:S(2)}, u32[]{:S(2)}) collective-permute-start(bf16[64,3584]{1,0:T(8,128)(2,1)} %slice.19), channel_id=1, source_target_pairs={{0,2},{6,4},{1,3},{7,5},{8,10},{14,12},{9,11},{15,13},{16,18},{22,... | collective-permute-start | bytes 1376264 | tf_op jit(solution)/shard_map/ppermute | solution.py:453
  79.3 0.8 copy-done.1
  80.1 7.0 %collective-permute-start.21 = (bf16[64,3584]{1,0:T(8,128)(2,1)S(1)}, bf16[64,3584]{1,0:T(8,128)(2,1)}, u32[]{:S(2)}, u32[]{:S(2)}) collective-permute-start(bf16[64,3584]{1,0:T(8,128)(2,1)S(1)} %shard_map.82.refs_2_), channel_id=1, source_target_pairs={{4,7},{5,6},{2,1},{3,0},{12,15},{13,14},{10,9},{11,8},{20,23},{21,... | collective-permute-start | bytes 1376264 | tf_op jit(solution)/shard_map/ppermute | solution.py:454
  87.2 1.0 copy-done.2
  88.3 1.3 %collective-permute-start.18 = (bf16[64,3584]{1,0:T(8,128)(2,1)S(1)}, bf16[64,3584]{1,0:T(8,128)(2,1)S(1)}, u32[]{:S(2)}, u32[]{:S(2)}) collective-permute-start(bf16[64,3584]{1,0:T(8,128)(2,1)S(1)} %shard_map.85.refs_2_), channel_id=1, source_target_pairs={{4,7},{5,6},{2,1},{3,0},{12,15},{13,14},{10,9},{11,8},{20,23},{21,... | collective-permute-start | bytes 1376264 | tf_op jit(solution)/shard_map/ppermute | solution.py:454
  89.6 1.3 %shard_map.86 = bf16[64,3584]{1,0:T(8,128)(2,1)S(1)} custom-call(bf16[64,3584]{1,0:T(8,128)(2,1)} %get-tuple-element.21.refs_0_, bf16[64,3584]{1,0:T(8,128)(2,1)} %collective-permute-done.10.refs_1_, bf16[64,3584]{1,0:T(8,128)(2,1)S(1)} %shard_map.85.refs_2_), custom_call_target="tpu_custom_call" | custom-call | tf_op jit(solution)/shard_map/pallas_call | solution.py:379
  90.9 3.2 %collective-permute-start.17 = (bf16[64,3584]{1,0:T(8,128)(2,1)S(1)}, bf16[64,3584]{1,0:T(8,128)(2,1)S(1)}, u32[]{:S(2)}, u32[]{:S(2)}) collective-permute-start(bf16[64,3584]{1,0:T(8,128)(2,1)S(1)} %shard_map.86), channel_id=1, source_target_pairs={{2,5},{3,4},{4,3},{5,2},{10,13},{11,12},{12,11},{13,10},{18,21},{1... | collective-permute-start | bytes 1376264 | tf_op jit(solution)/shard_map/ppermute | solution.py:454
  94.1 1.1 slice.17
  95.2 1.3 %collective-permute-start.9 = (bf16[64,3584]{1,0:T(8,128)(2,1)S(1)}, bf16[64,3584]{1,0:T(8,128)(2,1)S(1)}, u32[]{:S(2)}, u32[]{:S(2)}) collective-permute-start(bf16[64,3584]{1,0:T(8,128)(2,1)S(1)} %slice.17), channel_id=1, source_target_pairs={{0,2},{6,4},{1,3},{7,5},{8,10},{14,12},{9,11},{15,13},{16,18},{22,... | collective-permute-start | bytes 1376264 | tf_op jit(solution)/shard_map/ppermute | solution.py:453
  96.5 0.7 collective-permute-done.21.refs_2_
  97.3 2.4 %shard_map.87.refs_3_ = bf16[64,7168]{1,0:T(8,128)(2,1)} custom-call(s32[3]{0:T(128)S(1)} %add_convert_fusion.flag_ref, bf16[128,3584]{1,0:T(8,128)(2,1)S(1)} %collective-permute-done.16.refs_3_.pair_ref, bf16[64,3584]{1,0:T(8,128)(2,1)} %collective-permute-done.19.refs_0_, bf16[64,3584]{1,0:T(8,128)(2,1)} %collective-permute-done.20.refs_1_, ...), custom_call_target="tpu_custom_call" | custom-call | flops 10000000000 | tf_op jit(solution)/shard_map/pallas_call | solution.py:418
  99.7 4.8 %collective-permute-done.17.refs_1_ = bf16[64,3584]{1,0:T(8,128)(2,1)S(1)} collective-permute-done((bf16[64,3584]{1,0:T(8,128)(2,1)S(1)}, bf16[64,3584]{1,0:T(8,128)(2,1)S(1)}, u32[]{:S(2)}, u32[]{:S(2)}) %collective-permute-start.17) | collective-permute-done | bytes 458784 | tf_op jit(solution)/shard_map/ppermute | solution.py:454
  104.5 0.2 collective-permute-done.18.refs_2_
  104.7 4.2 %collective-permute-done.9.refs_0_ = bf16[64,3584]{1,0:T(8,128)(2,1)S(1)} collective-permute-done((bf16[64,3584]{1,0:T(8,128)(2,1)S(1)}, bf16[64,3584]{1,0:T(8,128)(2,1)S(1)}, u32[]{:S(2)}, u32[]{:S(2)}) %collective-permute-start.9) | collective-permute-done | bytes 458784 | tf_op jit(solution)/shard_map/ppermute | solution.py:453
  108.9 2.3 %shard_map.88 = bf16[64,7168]{1,0:T(8,128)(2,1)} custom-call(s32[3]{0:T(128)S(1)} %add_convert_fusion.flag_ref, bf16[128,3584]{1,0:T(8,128)(2,1)} %collective-permute-done.8.pair_ref, bf16[64,3584]{1,0:T(8,128)(2,1)S(1)} %collective-permute-done.9.refs_0_, bf16[64,3584]{1,0:T(8,128)(2,1)S(1)} %collective-permute-done.17.refs_1_, ...), custom_call_target="tpu_custom_call", output_to_operand_aliasing={{}: (5, {})} | custom-call | flops 10000000000 | tf_op jit(solution)/shard_map/pallas_call | solution.py:418
  (26 shorter events, 0.4 us)
Async XLA Ops:
  1.1 4.5 %collective-permute-start = (bf16[64,640]{1,0:T(8,128)(2,1)S(1)}, bf16[64,640]{1,0:T(8,128)(2,1)S(1)}, u32[]{:S(2)}, u32[]{:S(2)}) collective-permute-start(bf16[64,640]{1,0:T(8,128)(2,1)S(1)} %shard_map.74.refs_0_), channel_id=1, source_target_pairs={{0,2},{2,0},{4,6},{6,4},{1,3},{3,1},{5,7},{7,5},{8,10},{10,8},{12,... | collective-permute-start | bytes 245768 | tf_op jit(solution)/shard_map/ppermute | solution.py:120
  5.6 6.8 %collective-permute-start.1 = (bf16[128,640]{1,0:T(8,128)(2,1)S(1)}, bf16[128,640]{1,0:T(8,128)(2,1)S(1)}, u32[]{:S(2)}, u32[]{:S(2)}) collective-permute-start(bf16[128,640]{1,0:T(8,128)(2,1)S(1)} %shard_map.75.refs_4_), channel_id=1, source_target_pairs={{0,4},{2,6},{4,0},{6,2},{1,5},{3,7},{5,1},{7,3},{8,12},{10,14},{12... | collective-permute-start | bytes 491528 | tf_op jit(solution)/shard_map/ppermute | solution.py:120
  5.7 1.4 %copy-start = (bf16[1,256,3072]{2,1,0:T(8,128)(2,1)S(1)}, bf16[1,256,3072]{2,1,0:T(8,128)(2,1)}, u32[]{:S(2)}) copy-start(bf16[1,256,3072]{2,1,0:T(8,128)(2,1)} %param.7) | copy-start | bytes 4718596
  7.1 0.7 copy-start.3
  7.8 12.8 %copy-start.4 = (bf16[1,512,4096]{2,1,0:T(8,128)(2,1)S(1)}, bf16[1,512,4096]{2,1,0:T(8,128)(2,1)}, u32[]{:S(2)}) copy-start(bf16[1,512,4096]{2,1,0:T(8,128)(2,1)} %param.10) | copy-start | bytes 12582916
  10.6 6.8 %collective-permute-start.2 = (bf16[128,640]{1,0:T(8,128)(2,1)S(1)}, bf16[128,640]{1,0:T(8,128)(2,1)S(1)}, u32[]{:S(2)}, u32[]{:S(2)}) collective-permute-start(bf16[128,640]{1,0:T(8,128)(2,1)S(1)} %shard_map.75.refs_4_), channel_id=1, source_target_pairs={{0,16},{8,24},{16,0},{24,8},{1,17},{9,25},{17,1},{25,9},{2,18},{10... | collective-permute-start | bytes 491528 | tf_op jit(solution)/shard_map/ppermute | solution.py:120
  12.5 6.7 %collective-permute-start.3 = (bf16[128,640]{1,0:T(8,128)(2,1)S(1)}, bf16[128,640]{1,0:T(8,128)(2,1)S(1)}, u32[]{:S(2)}, u32[]{:S(2)}) collective-permute-start(bf16[128,640]{1,0:T(8,128)(2,1)S(1)} %shard_map.76.refs_5_), channel_id=1, source_target_pairs={{0,16},{8,24},{16,0},{24,8},{1,17},{9,25},{17,1},{25,9},{2,18},{10... | collective-permute-start | bytes 491528 | tf_op jit(solution)/shard_map/ppermute | solution.py:120
  13.5 6.9 %collective-permute-start.4 = (bf16[128,640]{1,0:T(8,128)(2,1)S(1)}, bf16[128,640]{1,0:T(8,128)(2,1)S(1)}, u32[]{:S(2)}, u32[]{:S(2)}) collective-permute-start(bf16[128,640]{1,0:T(8,128)(2,1)S(1)} %shard_map.75.refs_4_), channel_id=1, source_target_pairs={{0,8},{8,0},{16,24},{24,16},{1,9},{9,1},{17,25},{25,17},{2,10},{10... | collective-permute-start | bytes 491528 | tf_op jit(solution)/shard_map/ppermute | solution.py:120
  13.5 6.9 %collective-permute-start.5 = (bf16[128,640]{1,0:T(8,128)(2,1)S(1)}, bf16[128,640]{1,0:T(8,128)(2,1)S(1)}, u32[]{:S(2)}, u32[]{:S(2)}) collective-permute-start(bf16[128,640]{1,0:T(8,128)(2,1)S(1)} %shard_map.76.refs_5_), channel_id=1, source_target_pairs={{0,8},{8,0},{16,24},{24,16},{1,9},{9,1},{17,25},{25,17},{2,10},{10... | collective-permute-start | bytes 491528 | tf_op jit(solution)/shard_map/ppermute | solution.py:120
  17.4 3.0 %collective-permute-start.6 = (bf16[128,640]{1,0:T(8,128)(2,1)S(1)}, bf16[128,640]{1,0:T(8,128)(2,1)S(1)}, u32[]{:S(2)}, u32[]{:S(2)}) collective-permute-start(bf16[128,640]{1,0:T(8,128)(2,1)S(1)} %collective-permute-done.2.refs_6_), channel_id=1, source_target_pairs={{0,8},{8,0},{16,24},{24,16},{1,9},{9,1},{17,25},{25,17},{2,10},{10... | collective-permute-start | bytes 491528 | tf_op jit(solution)/shard_map/ppermute | solution.py:120
  19.1 1.4 %collective-permute-start.7 = (bf16[128,640]{1,0:T(8,128)(2,1)S(1)}, bf16[128,640]{1,0:T(8,128)(2,1)S(1)}, u32[]{:S(2)}, u32[]{:S(2)}) collective-permute-start(bf16[128,640]{1,0:T(8,128)(2,1)S(1)} %collective-permute-done.3.refs_7_), channel_id=1, source_target_pairs={{0,8},{8,0},{16,24},{24,16},{1,9},{9,1},{17,25},{25,17},{2,10},{10... | collective-permute-start | bytes 491528 | tf_op jit(solution)/shard_map/ppermute | solution.py:120
  36.2 36.5 %collective-permute-start.16 = (bf16[128,3584]{1,0:T(8,128)(2,1)S(1)}, bf16[128,3584]{1,0:T(8,128)(2,1)S(1)}, u32[]{:S(2)}, u32[]{:S(2)}) collective-permute-start(bf16[128,3584]{1,0:T(8,128)(2,1)S(1)} %shard_map.83), channel_id=1, source_target_pairs={{0,1},{1,0},{2,3},{3,2},{4,5},{5,4},{6,7},{7,6},{8,9},{9,8},{10,11... | collective-permute-start | bytes 2752520 | tf_op jit(solution)/shard_map/ppermute | solution.py:469
  37.6 15.4 %collective-permute-start.12 = (bf16[64,3584]{1,0:T(8,128)(2,1)S(1)}, bf16[64,3584]{1,0:T(8,128)(2,1)S(1)}, u32[]{:S(2)}, u32[]{:S(2)}) collective-permute-start(bf16[64,3584]{1,0:T(8,128)(2,1)S(1)} %get-tuple-element.23.refs_0_), channel_id=1, source_target_pairs={{0,2},{6,4},{1,3},{7,5},{8,10},{14,12},{9,11},{15,13},{16,18},{22,... | collective-permute-start | bytes 1376264 | tf_op jit(solution)/shard_map/ppermute | solution.py:453
  47.1 15.7 %collective-permute-start.11 = (bf16[64,3584]{1,0:T(8,128)(2,1)S(1)}, bf16[64,3584]{1,0:T(8,128)(2,1)S(1)}, u32[]{:S(2)}, u32[]{:S(2)}) collective-permute-start(bf16[64,3584]{1,0:T(8,128)(2,1)S(1)} %get-tuple-element.22.refs_0_), channel_id=1, source_target_pairs={{0,2},{6,4},{1,3},{7,5},{8,10},{14,12},{9,11},{15,13},{16,18},{22,... | collective-permute-start | bytes 1376264 | tf_op jit(solution)/shard_map/ppermute | solution.py:453
  48.4 24.3 %collective-permute-start.14 = (bf16[64,3584]{1,0:T(8,128)(2,1)S(1)}, bf16[64,3584]{1,0:T(8,128)(2,1)S(1)}, u32[]{:S(2)}, u32[]{:S(2)}) collective-permute-start(bf16[64,3584]{1,0:T(8,128)(2,1)S(1)} %get-tuple-element.24.refs_0_), channel_id=1, source_target_pairs={{0,2},{6,4},{1,3},{7,5},{8,10},{14,12},{9,11},{15,13},{16,18},{22,... | collective-permute-start | bytes 1376264 | tf_op jit(solution)/shard_map/ppermute | solution.py:453
  53.1 14.3 %collective-permute-start.15 = (bf16[64,3584]{1,0:T(8,128)(2,1)S(1)}, bf16[64,3584]{1,0:T(8,128)(2,1)S(1)}, u32[]{:S(2)}, u32[]{:S(2)}) collective-permute-start(bf16[64,3584]{1,0:T(8,128)(2,1)S(1)} %shard_map.80.refs_2_), channel_id=1, source_target_pairs={{2,4},{4,2},{3,5},{5,3},{10,12},{12,10},{11,13},{13,11},{18,20},{2... | collective-permute-start | bytes 1376264 | tf_op jit(solution)/shard_map/ppermute | solution.py:453
  57.3 33.6 %collective-permute-start.8 = (bf16[128,3584]{1,0:T(8,128)(2,1)S(1)}, bf16[128,3584]{1,0:T(8,128)(2,1)}, u32[]{:S(2)}, u32[]{:S(2)}) collective-permute-start(bf16[128,3584]{1,0:T(8,128)(2,1)S(1)} %shard_map.79), channel_id=1, source_target_pairs={{0,1},{1,0},{2,3},{3,2},{4,5},{5,4},{6,7},{7,6},{8,9},{9,8},{10,11... | collective-permute-start | bytes 2752520 | tf_op jit(solution)/shard_map/ppermute | solution.py:469
  63.0 16.3 %collective-permute-start.13 = (bf16[64,3584]{1,0:T(8,128)(2,1)S(1)}, bf16[64,3584]{1,0:T(8,128)(2,1)S(1)}, u32[]{:S(2)}, u32[]{:S(2)}) collective-permute-start(bf16[64,3584]{1,0:T(8,128)(2,1)S(1)} %shard_map.81.refs_2_), channel_id=1, source_target_pairs={{2,4},{4,2},{3,5},{5,3},{10,12},{12,10},{11,13},{13,11},{18,20},{2... | collective-permute-start | bytes 1376264 | tf_op jit(solution)/shard_map/ppermute | solution.py:453
  67.4 20.9 %collective-permute-start.10 = (bf16[64,3584]{1,0:T(8,128)(2,1)}, bf16[64,3584]{1,0:T(8,128)(2,1)}, u32[]{:S(2)}, u32[]{:S(2)}) collective-permute-start(bf16[64,3584]{1,0:T(8,128)(2,1)} %get-tuple-element.21.refs_0_), channel_id=1, source_target_pairs={{0,2},{6,4},{1,3},{7,5},{8,10},{14,12},{9,11},{15,13},{16,18},{22,... | collective-permute-start | bytes 1376264 | tf_op jit(solution)/shard_map/ppermute | solution.py:453
  72.8 22.4 %collective-permute-start.20 = (bf16[64,3584]{1,0:T(8,128)(2,1)S(1)}, bf16[64,3584]{1,0:T(8,128)(2,1)}, u32[]{:S(2)}, u32[]{:S(2)}) collective-permute-start(bf16[64,3584]{1,0:T(8,128)(2,1)S(1)} %shard_map.84.refs_2_), channel_id=1, source_target_pairs={{2,5},{3,4},{4,3},{5,2},{10,13},{11,12},{12,11},{13,10},{18,21},{1... | collective-permute-start | bytes 1376264 | tf_op jit(solution)/shard_map/ppermute | solution.py:454
  78.0 18.5 %collective-permute-start.19 = (bf16[64,3584]{1,0:T(8,128)(2,1)}, bf16[64,3584]{1,0:T(8,128)(2,1)}, u32[]{:S(2)}, u32[]{:S(2)}) collective-permute-start(bf16[64,3584]{1,0:T(8,128)(2,1)} %slice.19), channel_id=1, source_target_pairs={{0,2},{6,4},{1,3},{7,5},{8,10},{14,12},{9,11},{15,13},{16,18},{22,... | collective-permute-start | bytes 1376264 | tf_op jit(solution)/shard_map/ppermute | solution.py:453
  79.3 0.8 copy-start.1
  80.1 17.2 %collective-permute-start.21 = (bf16[64,3584]{1,0:T(8,128)(2,1)S(1)}, bf16[64,3584]{1,0:T(8,128)(2,1)}, u32[]{:S(2)}, u32[]{:S(2)}) collective-permute-start(bf16[64,3584]{1,0:T(8,128)(2,1)S(1)} %shard_map.82.refs_2_), channel_id=1, source_target_pairs={{4,7},{5,6},{2,1},{3,0},{12,15},{13,14},{10,9},{11,8},{20,23},{21,... | collective-permute-start | bytes 1376264 | tf_op jit(solution)/shard_map/ppermute | solution.py:454
  87.1 1.0 copy-start.2
  88.3 16.4 %collective-permute-start.18 = (bf16[64,3584]{1,0:T(8,128)(2,1)S(1)}, bf16[64,3584]{1,0:T(8,128)(2,1)S(1)}, u32[]{:S(2)}, u32[]{:S(2)}) collective-permute-start(bf16[64,3584]{1,0:T(8,128)(2,1)S(1)} %shard_map.85.refs_2_), channel_id=1, source_target_pairs={{4,7},{5,6},{2,1},{3,0},{12,15},{13,14},{10,9},{11,8},{20,23},{21,... | collective-permute-start | bytes 1376264 | tf_op jit(solution)/shard_map/ppermute | solution.py:454
  90.9 13.6 %collective-permute-start.17 = (bf16[64,3584]{1,0:T(8,128)(2,1)S(1)}, bf16[64,3584]{1,0:T(8,128)(2,1)S(1)}, u32[]{:S(2)}, u32[]{:S(2)}) collective-permute-start(bf16[64,3584]{1,0:T(8,128)(2,1)S(1)} %shard_map.86), channel_id=1, source_target_pairs={{2,5},{3,4},{4,3},{5,2},{10,13},{11,12},{12,11},{13,10},{18,21},{1... | collective-permute-start | bytes 1376264 | tf_op jit(solution)/shard_map/ppermute | solution.py:454
  95.2 13.7 %collective-permute-start.9 = (bf16[64,3584]{1,0:T(8,128)(2,1)S(1)}, bf16[64,3584]{1,0:T(8,128)(2,1)S(1)}, u32[]{:S(2)}, u32[]{:S(2)}) collective-permute-start(bf16[64,3584]{1,0:T(8,128)(2,1)S(1)} %slice.17), channel_id=1, source_target_pairs={{0,2},{6,4},{1,3},{7,5},{8,10},{14,12},{9,11},{15,13},{16,18},{22,... | collective-permute-start | bytes 1376264 | tf_op jit(solution)/shard_map/ppermute | solution.py:453

commit v7 on v6

--- a/solution.py
+++ b/solution.py
@@ -172,7 +172,7 @@
     return pl.pallas_call(
         functools.partial(prepare_kernel, block_len, key_rows, masks),
         out_shape=[
-            jax.ShapeDtypeStruct((heads // HEADS_STEP, rows, HEADS_STEP * 2 * LANES), jnp.bfloat16),
+            pltpu.VMEM((heads // HEADS_STEP, rows, HEADS_STEP * 2 * LANES), jnp.bfloat16),
             jax.ShapeDtypeStruct((rows, key_count), jnp.float32),
         ],
         in_specs=[

time: 112 us -> 112 us (level)
  no operation moved by 1% of the time
where the time goes in v7:
time: 112 us; the launch traced here: 111 us
  starting transfers between devices  39.4 us (35%)
  Pallas kernels  34.2 us (31%)
  waiting for transfers between devices  30.3 us (27%)
  local copies, waits for them, and re-layouts  6.96 us (6%)
    ppermute x8, starting transfers between devices, send(): return lax.ppermute(value, 'tp', steps)  16.4 us
    ppermute x8, waiting for transfers between devices, send(): return lax.ppermute(value, 'tp', steps)  16.3 us
    ppermute x4, starting transfers between devices, send(): lax.ppermute(value, ('tp', 'pp'), [(2 * i + p, 2 * j + 1 - p) for i, j in...  15.9 us
    pallas_call x1, Pallas kernels, attend(): pl.pallas_call(functools.partial(attention_kernel, len(pieces), steps), g...  15.5 us
    ppermute x8, waiting for transfers between devices, traded(): lax.ppermute(value, axis, [(i, i ^ step) for i in range(lax.axis_size(axi...  8.13 us
    pallas_call x1, Pallas kernels, project(): pl.pallas_call(project_kernel, grid=(size // tile,), out_shape=[pltpu.VME...  8.07 us
    ppermute x4, waiting for transfers between devices, send(): lax.ppermute(value, ('tp', 'pp'), [(2 * i + p, 2 * j + 1 - p) for i, j in...  5.77 us
    ppermute x8, starting transfers between devices, traded(): lax.ppermute(value, axis, [(i, i ^ step) for i in range(lax.axis_size(axi...  5.15 us
  transfers between devices with their start and end apart: 22, of which 11 were waited for; matrix products, arithmetic and copies ran while one was open for 3% of the time, Pallas kernels for 14%

profile of v7, /device:TPU:16, one launch (start us, length us, event | category | flops | bytes accessed | tf_op | source)
XLA Modules:
  0.0 111.3 jit_solution(3745055226972076531)
XLA Ops:
  0.0 1.1 shard_map.74.refs_0_
  1.1 1.6 %collective-permute-start = (bf16[64,640]{1,0:T(8,128)(2,1)S(1)}, bf16[64,640]{1,0:T(8,128)(2,1)S(1)}, u32[]{:S(2)}, u32[]{:S(2)}) collective-permute-start(bf16[64,640]{1,0:T(8,128)(2,1)S(1)} %shard_map.74.refs_0_), channel_id=1, source_target_pairs={{0,2},{2,0},{4,6},{6,4},{1,3},{3,1},{5,7},{7,5},{8,10},{10,8},{12,... | collective-permute-start | bytes 245768 | tf_op jit(solution)/shard_map/ppermute | solution.py:120
  2.7 2.9 %collective-permute-done.refs_1_ = bf16[64,640]{1,0:T(8,128)(2,1)S(1)} collective-permute-done((bf16[64,640]{1,0:T(8,128)(2,1)S(1)}, bf16[64,640]{1,0:T(8,128)(2,1)S(1)}, u32[]{:S(2)}, u32[]{:S(2)}) %collective-permute-start) | collective-permute-done | bytes 81952 | tf_op jit(solution)/shard_map/ppermute | solution.py:120
  5.7 1.4 %copy-done = bf16[1,256,3072]{2,1,0:T(8,128)(2,1)S(1)} copy-done((bf16[1,256,3072]{2,1,0:T(8,128)(2,1)S(1)}, bf16[1,256,3072]{2,1,0:T(8,128)(2,1)}, u32[]{:S(2)}) %copy-start) | copy-done | bytes 1572888
  7.1 0.7 copy-done.3
  7.8 2.8 %shard_map.73 = (bf16[2,256,2048]{2,1,0:T(8,128)(2,1)S(1)}, f32[256,1024]{1,0:T(8,128)S(1)}) custom-call(s32[8]{0:T(128)S(1)} %bitcast.11, bf16[256,3072]{1,0:T(8,128)(2,1)S(1)} %bitcast.9), custom_call_target="tpu_custom_call" | custom-call | flops 15728640 | bytes 4718592 | tf_op jit(solution)/shard_map/pallas_call | solution.py:172
  10.6 1.9 %collective-permute-start.2 = (bf16[128,640]{1,0:T(8,128)(2,1)S(1)}, bf16[128,640]{1,0:T(8,128)(2,1)S(1)}, u32[]{:S(2)}, u32[]{:S(2)}) collective-permute-start(bf16[128,640]{1,0:T(8,128)(2,1)S(1)} %shard_map.75.refs_4_), channel_id=1, source_target_pairs={{0,16},{8,24},{16,0},{24,8},{1,17},{9,25},{17,1},{25,9},{2,18},{10... | collective-permute-start | bytes 491528 | tf_op jit(solution)/shard_map/ppermute | solution.py:120
  12.5 1.0 collective-permute-start.3
  13.5 0.5 collective-permute-start.5
  14.0 3.4 %collective-permute-done.2.refs_6_ = bf16[128,640]{1,0:T(8,128)(2,1)S(1)} collective-permute-done((bf16[128,640]{1,0:T(8,128)(2,1)S(1)}, bf16[128,640]{1,0:T(8,128)(2,1)S(1)}, u32[]{:S(2)}, u32[]{:S(2)}) %collective-permute-start.2) | collective-permute-done | bytes 163872 | tf_op jit(solution)/shard_map/ppermute | solution.py:120
  17.4 1.8 %collective-permute-done.3.refs_7_ = bf16[128,640]{1,0:T(8,128)(2,1)S(1)} collective-permute-done((bf16[128,640]{1,0:T(8,128)(2,1)S(1)}, bf16[128,640]{1,0:T(8,128)(2,1)S(1)}, u32[]{:S(2)}, u32[]{:S(2)}) %collective-permute-start.3) | collective-permute-done | bytes 163872 | tf_op jit(solution)/shard_map/ppermute | solution.py:120
  19.1 1.2 %fusion = (bf16[64,3584]{1,0:T(8,128)(2,1)S(1)}, bf16[64,3584]{1,0:T(8,128)(2,1)S(1)}) fusion(bf16[64,7168]{1,0:T(8,128)(2,1)} %bitcast.16), kind=kLoop, calls=%fused_computation.1 | loop fusion | bytes 1835008 | tf_op jit(solution)/shard_map/slice | solution.py:467
  20.4 0.1 collective-permute-done.7.refs_11_
  20.5 15.5 %shard_map.77 = (bf16[256,2048]{1,0:T(8,128)(2,1)S(1)}, bf16[64,3584]{1,0:T(8,128)(2,1)S(1)}, bf16[64,3584]{1,0:T(8,128)(2,1)S(1)}, bf16[64,3584]{1,0:T(8,128)(2,1)S(1)}, bf16[64,3584]{1,0:T(8,128)(2,1)S(1)}) custom-call(bf16[2,256,2048]{2,1,0:T(8,128)(2,1)S(1)} %get-tuple-element.16.refs_1_.refs_0_, f32[256,1024]{1,0:T(8,128)S(1)} %get-tuple-element.17.refs_2_.refs_1_, ...), custom_call_target="tpu_custom_call" | custom-call | flops 12348030976 | bytes 20971520 | tf_op jit(solution)/shard_map/pallas_call | solution.py:306
  36.1 0.1 shard_map.83
  36.2 1.4 %collective-permute-start.16 = (bf16[128,3584]{1,0:T(8,128)(2,1)S(1)}, bf16[128,3584]{1,0:T(8,128)(2,1)S(1)}, u32[]{:S(2)}, u32[]{:S(2)}) collective-permute-start(bf16[128,3584]{1,0:T(8,128)(2,1)S(1)} %shard_map.83), channel_id=1, source_target_pairs={{0,1},{1,0},{2,3},{3,2},{4,5},{5,4},{6,7},{7,6},{8,9},{9,8},{10,11... | collective-permute-start | bytes 2752520 | tf_op jit(solution)/shard_map/ppermute | solution.py:469
  37.6 1.5 %collective-permute-start.12 = (bf16[64,3584]{1,0:T(8,128)(2,1)S(1)}, bf16[64,3584]{1,0:T(8,128)(2,1)S(1)}, u32[]{:S(2)}, u32[]{:S(2)}) collective-permute-start(bf16[64,3584]{1,0:T(8,128)(2,1)S(1)} %get-tuple-element.23.refs_0_), channel_id=1, source_target_pairs={{0,2},{6,4},{1,3},{7,5},{8,10},{14,12},{9,11},{15,13},{16,18},{22,... | collective-permute-start | bytes 1376264 | tf_op jit(solution)/shard_map/ppermute | solution.py:453
  39.1 8.1 %shard_map.78 = (bf16[64,3584]{1,0:T(8,128)(2,1)S(1)}, bf16[64,3584]{1,0:T(8,128)(2,1)}, bf16[64,3584]{1,0:T(8,128)(2,1)S(1)}, bf16[64,3584]{1,0:T(8,128)(2,1)S(1)}) custom-call(bf16[256,2048]{1,0:T(8,128)(2,1)S(1)} %get-tuple-element.18.x_ref, bf16[2048,7168]{1,0:T(8,128)(2,1)} %bitcast.14, bf16[2048,7168]{1,0:T(8,128)(2,1)} %bitcast.15), custom_call_target="tpu_custom_call" | custom-call | flops 3758096384 | bytes 14680064 | tf_op jit(solution)/shard_map/pallas_call | solution.py:349
  47.1 1.3 %collective-permute-start.11 = (bf16[64,3584]{1,0:T(8,128)(2,1)S(1)}, bf16[64,3584]{1,0:T(8,128)(2,1)S(1)}, u32[]{:S(2)}, u32[]{:S(2)}) collective-permute-start(bf16[64,3584]{1,0:T(8,128)(2,1)S(1)} %get-tuple-element.22.refs_0_), channel_id=1, source_target_pairs={{0,2},{6,4},{1,3},{7,5},{8,10},{14,12},{9,11},{15,13},{16,18},{22,... | collective-permute-start | bytes 1376264 | tf_op jit(solution)/shard_map/ppermute | solution.py:453
  48.4 1.3 %collective-permute-start.14 = (bf16[64,3584]{1,0:T(8,128)(2,1)S(1)}, bf16[64,3584]{1,0:T(8,128)(2,1)S(1)}, u32[]{:S(2)}, u32[]{:S(2)}) collective-permute-start(bf16[64,3584]{1,0:T(8,128)(2,1)S(1)} %get-tuple-element.24.refs_0_), channel_id=1, source_target_pairs={{0,2},{6,4},{1,3},{7,5},{8,10},{14,12},{9,11},{15,13},{16,18},{22,... | collective-permute-start | bytes 1376264 | tf_op jit(solution)/shard_map/ppermute | solution.py:453
  49.7 3.3 %collective-permute-done.12.refs_1_ = bf16[64,3584]{1,0:T(8,128)(2,1)S(1)} collective-permute-done((bf16[64,3584]{1,0:T(8,128)(2,1)S(1)}, bf16[64,3584]{1,0:T(8,128)(2,1)S(1)}, u32[]{:S(2)}, u32[]{:S(2)}) %collective-permute-start.12) | collective-permute-done | bytes 458784 | tf_op jit(solution)/shard_map/ppermute | solution.py:453
  53.0 0.1 shard_map.80.refs_2_
  53.1 4.1 %collective-permute-start.15 = (bf16[64,3584]{1,0:T(8,128)(2,1)S(1)}, bf16[64,3584]{1,0:T(8,128)(2,1)S(1)}, u32[]{:S(2)}, u32[]{:S(2)}) collective-permute-start(bf16[64,3584]{1,0:T(8,128)(2,1)S(1)} %shard_map.80.refs_2_), channel_id=1, source_target_pairs={{2,4},{4,2},{3,5},{5,3},{10,12},{12,10},{11,13},{13,11},{18,20},{2... | collective-permute-start | bytes 1376264 | tf_op jit(solution)/shard_map/ppermute | solution.py:453
  57.2 0.1 shard_map.79
  57.3 0.6 collective-permute-start.8
  57.9 4.9 %collective-permute-done.11.refs_1_ = bf16[64,3584]{1,0:T(8,128)(2,1)S(1)} collective-permute-done((bf16[64,3584]{1,0:T(8,128)(2,1)S(1)}, bf16[64,3584]{1,0:T(8,128)(2,1)S(1)}, u32[]{:S(2)}, u32[]{:S(2)}) %collective-permute-start.11) | collective-permute-done | bytes 458784 | tf_op jit(solution)/shard_map/ppermute | solution.py:453
  62.9 0.1 shard_map.81.refs_2_
  63.0 4.4 %collective-permute-start.13 = (bf16[64,3584]{1,0:T(8,128)(2,1)S(1)}, bf16[64,3584]{1,0:T(8,128)(2,1)S(1)}, u32[]{:S(2)}, u32[]{:S(2)}) collective-permute-start(bf16[64,3584]{1,0:T(8,128)(2,1)S(1)} %shard_map.81.refs_2_), channel_id=1, source_target_pairs={{2,4},{4,2},{3,5},{5,3},{10,12},{12,10},{11,13},{13,11},{18,20},{2... | collective-permute-start | bytes 1376264 | tf_op jit(solution)/shard_map/ppermute | solution.py:453
  67.4 1.3 %collective-permute-start.10 = (bf16[64,3584]{1,0:T(8,128)(2,1)}, bf16[64,3584]{1,0:T(8,128)(2,1)}, u32[]{:S(2)}, u32[]{:S(2)}) collective-permute-start(bf16[64,3584]{1,0:T(8,128)(2,1)} %get-tuple-element.21.refs_0_), channel_id=1, source_target_pairs={{0,2},{6,4},{1,3},{7,5},{8,10},{14,12},{9,11},{15,13},{16,18},{22,... | collective-permute-start | bytes 1376264 | tf_op jit(solution)/shard_map/ppermute | solution.py:453
  68.7 0.1 shard_map.82.refs_2_
  68.8 3.9 %collective-permute-done.14.refs_1_ = bf16[64,3584]{1,0:T(8,128)(2,1)S(1)} collective-permute-done((bf16[64,3584]{1,0:T(8,128)(2,1)S(1)}, bf16[64,3584]{1,0:T(8,128)(2,1)S(1)}, u32[]{:S(2)}, u32[]{:S(2)}) %collective-permute-start.14) | collective-permute-done | bytes 458784 | tf_op jit(solution)/shard_map/ppermute | solution.py:453
  72.8 4.3 %collective-permute-start.20 = (bf16[64,3584]{1,0:T(8,128)(2,1)S(1)}, bf16[64,3584]{1,0:T(8,128)(2,1)}, u32[]{:S(2)}, u32[]{:S(2)}) collective-permute-start(bf16[64,3584]{1,0:T(8,128)(2,1)S(1)} %shard_map.84.refs_2_), channel_id=1, source_target_pairs={{2,5},{3,4},{4,3},{5,2},{10,13},{11,12},{12,11},{13,10},{18,21},{1... | collective-permute-start | bytes 1376264 | tf_op jit(solution)/shard_map/ppermute | solution.py:454
  77.1 0.8 slice.19
  78.0 1.3 %collective-permute-start.19 = (bf16[64,3584]{1,0:T(8,128)(2,1)}, bf16[64,3584]{1,0:T(8,128)(2,1)}, u32[]{:S(2)}, u32[]{:S(2)}) collective-permute-start(bf16[64,3584]{1,0:T(8,128)(2,1)} %slice.19), channel_id=1, source_target_pairs={{0,2},{6,4},{1,3},{7,5},{8,10},{14,12},{9,11},{15,13},{16,18},{22,... | collective-permute-start | bytes 1376264 | tf_op jit(solution)/shard_map/ppermute | solution.py:453
  79.3 0.8 copy-done.1
  80.1 7.0 %collective-permute-start.21 = (bf16[64,3584]{1,0:T(8,128)(2,1)S(1)}, bf16[64,3584]{1,0:T(8,128)(2,1)}, u32[]{:S(2)}, u32[]{:S(2)}) collective-permute-start(bf16[64,3584]{1,0:T(8,128)(2,1)S(1)} %shard_map.82.refs_2_), channel_id=1, source_target_pairs={{4,7},{5,6},{2,1},{3,0},{12,15},{13,14},{10,9},{11,8},{20,23},{21,... | collective-permute-start | bytes 1376264 | tf_op jit(solution)/shard_map/ppermute | solution.py:454
  87.2 1.0 copy-done.2
  88.3 1.3 %collective-permute-start.18 = (bf16[64,3584]{1,0:T(8,128)(2,1)S(1)}, bf16[64,3584]{1,0:T(8,128)(2,1)S(1)}, u32[]{:S(2)}, u32[]{:S(2)}) collective-permute-start(bf16[64,3584]{1,0:T(8,128)(2,1)S(1)} %shard_map.85.refs_2_), channel_id=1, source_target_pairs={{4,7},{5,6},{2,1},{3,0},{12,15},{13,14},{10,9},{11,8},{20,23},{21,... | collective-permute-start | bytes 1376264 | tf_op jit(solution)/shard_map/ppermute | solution.py:454
  89.6 1.3 %shard_map.86 = bf16[64,3584]{1,0:T(8,128)(2,1)S(1)} custom-call(bf16[64,3584]{1,0:T(8,128)(2,1)} %get-tuple-element.21.refs_0_, bf16[64,3584]{1,0:T(8,128)(2,1)} %collective-permute-done.10.refs_1_, bf16[64,3584]{1,0:T(8,128)(2,1)S(1)} %shard_map.85.refs_2_), custom_call_target="tpu_custom_call" | custom-call | tf_op jit(solution)/shard_map/pallas_call | solution.py:379
  90.9 3.2 %collective-permute-start.17 = (bf16[64,3584]{1,0:T(8,128)(2,1)S(1)}, bf16[64,3584]{1,0:T(8,128)(2,1)S(1)}, u32[]{:S(2)}, u32[]{:S(2)}) collective-permute-start(bf16[64,3584]{1,0:T(8,128)(2,1)S(1)} %shard_map.86), channel_id=1, source_target_pairs={{2,5},{3,4},{4,3},{5,2},{10,13},{11,12},{12,11},{13,10},{18,21},{1... | collective-permute-start | bytes 1376264 | tf_op jit(solution)/shard_map/ppermute | solution.py:454
  94.1 1.1 slice.17
  95.2 1.3 %collective-permute-start.9 = (bf16[64,3584]{1,0:T(8,128)(2,1)S(1)}, bf16[64,3584]{1,0:T(8,128)(2,1)S(1)}, u32[]{:S(2)}, u32[]{:S(2)}) collective-permute-start(bf16[64,3584]{1,0:T(8,128)(2,1)S(1)} %slice.17), channel_id=1, source_target_pairs={{0,2},{6,4},{1,3},{7,5},{8,10},{14,12},{9,11},{15,13},{16,18},{22,... | collective-permute-start | bytes 1376264 | tf_op jit(solution)/shard_map/ppermute | solution.py:453
  96.5 0.7 collective-permute-done.21.refs_2_
  97.3 2.4 %shard_map.87.refs_3_ = bf16[64,7168]{1,0:T(8,128)(2,1)} custom-call(s32[3]{0:T(128)S(1)} %add_convert_fusion.flag_ref, bf16[128,3584]{1,0:T(8,128)(2,1)S(1)} %collective-permute-done.16.refs_3_.pair_ref, bf16[64,3584]{1,0:T(8,128)(2,1)} %collective-permute-done.19.refs_0_, bf16[64,3584]{1,0:T(8,128)(2,1)} %collective-permute-done.20.refs_1_, ...), custom_call_target="tpu_custom_call" | custom-call | flops 10000000000 | tf_op jit(solution)/shard_map/pallas_call | solution.py:418
  99.7 4.8 %collective-permute-done.17.refs_1_ = bf16[64,3584]{1,0:T(8,128)(2,1)S(1)} collective-permute-done((bf16[64,3584]{1,0:T(8,128)(2,1)S(1)}, bf16[64,3584]{1,0:T(8,128)(2,1)S(1)}, u32[]{:S(2)}, u32[]{:S(2)}) %collective-permute-start.17) | collective-permute-done | bytes 458784 | tf_op jit(solution)/shard_map/ppermute | solution.py:454
  104.5 0.2 collective-permute-done.18.refs_2_
  104.7 4.2 %collective-permute-done.9.refs_0_ = bf16[64,3584]{1,0:T(8,128)(2,1)S(1)} collective-permute-done((bf16[64,3584]{1,0:T(8,128)(2,1)S(1)}, bf16[64,3584]{1,0:T(8,128)(2,1)S(1)}, u32[]{:S(2)}, u32[]{:S(2)}) %collective-permute-start.9) | collective-permute-done | bytes 458784 | tf_op jit(solution)/shard_map/ppermute | solution.py:453
  108.9 2.3 %shard_map.88 = bf16[64,7168]{1,0:T(8,128)(2,1)} custom-call(s32[3]{0:T(128)S(1)} %add_convert_fusion.flag_ref, bf16[128,3584]{1,0:T(8,128)(2,1)} %collective-permute-done.8.pair_ref, bf16[64,3584]{1,0:T(8,128)(2,1)S(1)} %collective-permute-done.9.refs_0_, bf16[64,3584]{1,0:T(8,128)(2,1)S(1)} %collective-permute-done.17.refs_1_, ...), custom_call_target="tpu_custom_call", output_to_operand_aliasing={{}: (5, {})} | custom-call | flops 10000000000 | tf_op jit(solution)/shard_map/pallas_call | solution.py:418
  (26 shorter events, 0.4 us)
Async XLA Ops:
  1.1 4.5 %collective-permute-start = (bf16[64,640]{1,0:T(8,128)(2,1)S(1)}, bf16[64,640]{1,0:T(8,128)(2,1)S(1)}, u32[]{:S(2)}, u32[]{:S(2)}) collective-permute-start(bf16[64,640]{1,0:T(8,128)(2,1)S(1)} %shard_map.74.refs_0_), channel_id=1, source_target_pairs={{0,2},{2,0},{4,6},{6,4},{1,3},{3,1},{5,7},{7,5},{8,10},{10,8},{12,... | collective-permute-start | bytes 245768 | tf_op jit(solution)/shard_map/ppermute | solution.py:120
  5.6 6.8 %collective-permute-start.1 = (bf16[128,640]{1,0:T(8,128)(2,1)S(1)}, bf16[128,640]{1,0:T(8,128)(2,1)S(1)}, u32[]{:S(2)}, u32[]{:S(2)}) collective-permute-start(bf16[128,640]{1,0:T(8,128)(2,1)S(1)} %shard_map.75.refs_4_), channel_id=1, source_target_pairs={{0,4},{2,6},{4,0},{6,2},{1,5},{3,7},{5,1},{7,3},{8,12},{10,14},{12... | collective-permute-start | bytes 491528 | tf_op jit(solution)/shard_map/ppermute | solution.py:120
  5.7 1.4 %copy-start = (bf16[1,256,3072]{2,1,0:T(8,128)(2,1)S(1)}, bf16[1,256,3072]{2,1,0:T(8,128)(2,1)}, u32[]{:S(2)}) copy-start(bf16[1,256,3072]{2,1,0:T(8,128)(2,1)} %param.7) | copy-start | bytes 4718596
  7.1 0.7 copy-start.3
  7.8 12.8 %copy-start.4 = (bf16[1,512,4096]{2,1,0:T(8,128)(2,1)S(1)}, bf16[1,512,4096]{2,1,0:T(8,128)(2,1)}, u32[]{:S(2)}) copy-start(bf16[1,512,4096]{2,1,0:T(8,128)(2,1)} %param.10) | copy-start | bytes 12582916
  10.6 6.8 %collective-permute-start.2 = (bf16[128,640]{1,0:T(8,128)(2,1)S(1)}, bf16[128,640]{1,0:T(8,128)(2,1)S(1)}, u32[]{:S(2)}, u32[]{:S(2)}) collective-permute-start(bf16[128,640]{1,0:T(8,128)(2,1)S(1)} %shard_map.75.refs_4_), channel_id=1, source_target_pairs={{0,16},{8,24},{16,0},{24,8},{1,17},{9,25},{17,1},{25,9},{2,18},{10... | collective-permute-start | bytes 491528 | tf_op jit(solution)/shard_map/ppermute | solution.py:120
  12.5 6.7 %collective-permute-start.3 = (bf16[128,640]{1,0:T(8,128)(2,1)S(1)}, bf16[128,640]{1,0:T(8,128)(2,1)S(1)}, u32[]{:S(2)}, u32[]{:S(2)}) collective-permute-start(bf16[128,640]{1,0:T(8,128)(2,1)S(1)} %shard_map.76.refs_5_), channel_id=1, source_target_pairs={{0,16},{8,24},{16,0},{24,8},{1,17},{9,25},{17,1},{25,9},{2,18},{10... | collective-permute-start | bytes 491528 | tf_op jit(solution)/shard_map/ppermute | solution.py:120
  13.5 6.9 %collective-permute-start.4 = (bf16[128,640]{1,0:T(8,128)(2,1)S(1)}, bf16[128,640]{1,0:T(8,128)(2,1)S(1)}, u32[]{:S(2)}, u32[]{:S(2)}) collective-permute-start(bf16[128,640]{1,0:T(8,128)(2,1)S(1)} %shard_map.75.refs_4_), channel_id=1, source_target_pairs={{0,8},{8,0},{16,24},{24,16},{1,9},{9,1},{17,25},{25,17},{2,10},{10... | collective-permute-start | bytes 491528 | tf_op jit(solution)/shard_map/ppermute | solution.py:120
  13.5 6.9 %collective-permute-start.5 = (bf16[128,640]{1,0:T(8,128)(2,1)S(1)}, bf16[128,640]{1,0:T(8,128)(2,1)S(1)}, u32[]{:S(2)}, u32[]{:S(2)}) collective-permute-start(bf16[128,640]{1,0:T(8,128)(2,1)S(1)} %shard_map.76.refs_5_), channel_id=1, source_target_pairs={{0,8},{8,0},{16,24},{24,16},{1,9},{9,1},{17,25},{25,17},{2,10},{10... | collective-permute-start | bytes 491528 | tf_op jit(solution)/shard_map/ppermute | solution.py:120
  17.4 3.0 %collective-permute-start.6 = (bf16[128,640]{1,0:T(8,128)(2,1)S(1)}, bf16[128,640]{1,0:T(8,128)(2,1)S(1)}, u32[]{:S(2)}, u32[]{:S(2)}) collective-permute-start(bf16[128,640]{1,0:T(8,128)(2,1)S(1)} %collective-permute-done.2.refs_6_), channel_id=1, source_target_pairs={{0,8},{8,0},{16,24},{24,16},{1,9},{9,1},{17,25},{25,17},{2,10},{10... | collective-permute-start | bytes 491528 | tf_op jit(solution)/shard_map/ppermute | solution.py:120
  19.1 1.4 %collective-permute-start.7 = (bf16[128,640]{1,0:T(8,128)(2,1)S(1)}, bf16[128,640]{1,0:T(8,128)(2,1)S(1)}, u32[]{:S(2)}, u32[]{:S(2)}) collective-permute-start(bf16[128,640]{1,0:T(8,128)(2,1)S(1)} %collective-permute-done.3.refs_7_), channel_id=1, source_target_pairs={{0,8},{8,0},{16,24},{24,16},{1,9},{9,1},{17,25},{25,17},{2,10},{10... | collective-permute-start | bytes 491528 | tf_op jit(solution)/shard_map/ppermute | solution.py:120
  36.2 36.5 %collective-permute-start.16 = (bf16[128,3584]{1,0:T(8,128)(2,1)S(1)}, bf16[128,3584]{1,0:T(8,128)(2,1)S(1)}, u32[]{:S(2)}, u32[]{:S(2)}) collective-permute-start(bf16[128,3584]{1,0:T(8,128)(2,1)S(1)} %shard_map.83), channel_id=1, source_target_pairs={{0,1},{1,0},{2,3},{3,2},{4,5},{5,4},{6,7},{7,6},{8,9},{9,8},{10,11... | collective-permute-start | bytes 2752520 | tf_op jit(solution)/shard_map/ppermute | solution.py:469
  37.6 15.4 %collective-permute-start.12 = (bf16[64,3584]{1,0:T(8,128)(2,1)S(1)}, bf16[64,3584]{1,0:T(8,128)(2,1)S(1)}, u32[]{:S(2)}, u32[]{:S(2)}) collective-permute-start(bf16[64,3584]{1,0:T(8,128)(2,1)S(1)} %get-tuple-element.23.refs_0_), channel_id=1, source_target_pairs={{0,2},{6,4},{1,3},{7,5},{8,10},{14,12},{9,11},{15,13},{16,18},{22,... | collective-permute-start | bytes 1376264 | tf_op jit(solution)/shard_map/ppermute | solution.py:453
  47.1 15.7 %collective-permute-start.11 = (bf16[64,3584]{1,0:T(8,128)(2,1)S(1)}, bf16[64,3584]{1,0:T(8,128)(2,1)S(1)}, u32[]{:S(2)}, u32[]{:S(2)}) collective-permute-start(bf16[64,3584]{1,0:T(8,128)(2,1)S(1)} %get-tuple-element.22.refs_0_), channel_id=1, source_target_pairs={{0,2},{6,4},{1,3},{7,5},{8,10},{14,12},{9,11},{15,13},{16,18},{22,... | collective-permute-start | bytes 1376264 | tf_op jit(solution)/shard_map/ppermute | solution.py:453
  48.4 24.3 %collective-permute-start.14 = (bf16[64,3584]{1,0:T(8,128)(2,1)S(1)}, bf16[64,3584]{1,0:T(8,128)(2,1)S(1)}, u32[]{:S(2)}, u32[]{:S(2)}) collective-permute-start(bf16[64,3584]{1,0:T(8,128)(2,1)S(1)} %get-tuple-element.24.refs_0_), channel_id=1, source_target_pairs={{0,2},{6,4},{1,3},{7,5},{8,10},{14,12},{9,11},{15,13},{16,18},{22,... | collective-permute-start | bytes 1376264 | tf_op jit(solution)/shard_map/ppermute | solution.py:453
  53.1 14.3 %collective-permute-start.15 = (bf16[64,3584]{1,0:T(8,128)(2,1)S(1)}, bf16[64,3584]{1,0:T(8,128)(2,1)S(1)}, u32[]{:S(2)}, u32[]{:S(2)}) collective-permute-start(bf16[64,3584]{1,0:T(8,128)(2,1)S(1)} %shard_map.80.refs_2_), channel_id=1, source_target_pairs={{2,4},{4,2},{3,5},{5,3},{10,12},{12,10},{11,13},{13,11},{18,20},{2... | collective-permute-start | bytes 1376264 | tf_op jit(solution)/shard_map/ppermute | solution.py:453
  57.3 33.6 %collective-permute-start.8 = (bf16[128,3584]{1,0:T(8,128)(2,1)S(1)}, bf16[128,3584]{1,0:T(8,128)(2,1)}, u32[]{:S(2)}, u32[]{:S(2)}) collective-permute-start(bf16[128,3584]{1,0:T(8,128)(2,1)S(1)} %shard_map.79), channel_id=1, source_target_pairs={{0,1},{1,0},{2,3},{3,2},{4,5},{5,4},{6,7},{7,6},{8,9},{9,8},{10,11... | collective-permute-start | bytes 2752520 | tf_op jit(solution)/shard_map/ppermute | solution.py:469
  63.0 16.3 %collective-permute-start.13 = (bf16[64,3584]{1,0:T(8,128)(2,1)S(1)}, bf16[64,3584]{1,0:T(8,128)(2,1)S(1)}, u32[]{:S(2)}, u32[]{:S(2)}) collective-permute-start(bf16[64,3584]{1,0:T(8,128)(2,1)S(1)} %shard_map.81.refs_2_), channel_id=1, source_target_pairs={{2,4},{4,2},{3,5},{5,3},{10,12},{12,10},{11,13},{13,11},{18,20},{2... | collective-permute-start | bytes 1376264 | tf_op jit(solution)/shard_map/ppermute | solution.py:453
  67.4 20.9 %collective-permute-start.10 = (bf16[64,3584]{1,0:T(8,128)(2,1)}, bf16[64,3584]{1,0:T(8,128)(2,1)}, u32[]{:S(2)}, u32[]{:S(2)}) collective-permute-start(bf16[64,3584]{1,0:T(8,128)(2,1)} %get-tuple-element.21.refs_0_), channel_id=1, source_target_pairs={{0,2},{6,4},{1,3},{7,5},{8,10},{14,12},{9,11},{15,13},{16,18},{22,... | collective-permute-start | bytes 1376264 | tf_op jit(solution)/shard_map/ppermute | solution.py:453
  72.8 22.4 %collective-permute-start.20 = (bf16[64,3584]{1,0:T(8,128)(2,1)S(1)}, bf16[64,3584]{1,0:T(8,128)(2,1)}, u32[]{:S(2)}, u32[]{:S(2)}) collective-permute-start(bf16[64,3584]{1,0:T(8,128)(2,1)S(1)} %shard_map.84.refs_2_), channel_id=1, source_target_pairs={{2,5},{3,4},{4,3},{5,2},{10,13},{11,12},{12,11},{13,10},{18,21},{1... | collective-permute-start | bytes 1376264 | tf_op jit(solution)/shard_map/ppermute | solution.py:454
  78.0 18.5 %collective-permute-start.19 = (bf16[64,3584]{1,0:T(8,128)(2,1)}, bf16[64,3584]{1,0:T(8,128)(2,1)}, u32[]{:S(2)}, u32[]{:S(2)}) collective-permute-start(bf16[64,3584]{1,0:T(8,128)(2,1)} %slice.19), channel_id=1, source_target_pairs={{0,2},{6,4},{1,3},{7,5},{8,10},{14,12},{9,11},{15,13},{16,18},{22,... | collective-permute-start | bytes 1376264 | tf_op jit(solution)/shard_map/ppermute | solution.py:453
  79.3 0.8 copy-start.1
  80.1 17.2 %collective-permute-start.21 = (bf16[64,3584]{1,0:T(8,128)(2,1)S(1)}, bf16[64,3584]{1,0:T(8,128)(2,1)}, u32[]{:S(2)}, u32[]{:S(2)}) collective-permute-start(bf16[64,3584]{1,0:T(8,128)(2,1)S(1)} %shard_map.82.refs_2_), channel_id=1, source_target_pairs={{4,7},{5,6},{2,1},{3,0},{12,15},{13,14},{10,9},{11,8},{20,23},{21,... | collective-permute-start | bytes 1376264 | tf_op jit(solution)/shard_map/ppermute | solution.py:454
  87.1 1.0 copy-start.2
  88.3 16.4 %collective-permute-start.18 = (bf16[64,3584]{1,0:T(8,128)(2,1)S(1)}, bf16[64,3584]{1,0:T(8,128)(2,1)S(1)}, u32[]{:S(2)}, u32[]{:S(2)}) collective-permute-start(bf16[64,3584]{1,0:T(8,128)(2,1)S(1)} %shard_map.85.refs_2_), channel_id=1, source_target_pairs={{4,7},{5,6},{2,1},{3,0},{12,15},{13,14},{10,9},{11,8},{20,23},{21,... | collective-permute-start | bytes 1376264 | tf_op jit(solution)/shard_map/ppermute | solution.py:454
  90.9 13.6 %collective-permute-start.17 = (bf16[64,3584]{1,0:T(8,128)(2,1)S(1)}, bf16[64,3584]{1,0:T(8,128)(2,1)S(1)}, u32[]{:S(2)}, u32[]{:S(2)}) collective-permute-start(bf16[64,3584]{1,0:T(8,128)(2,1)S(1)} %shard_map.86), channel_id=1, source_target_pairs={{2,5},{3,4},{4,3},{5,2},{10,13},{11,12},{12,11},{13,10},{18,21},{1... | collective-permute-start | bytes 1376264 | tf_op jit(solution)/shard_map/ppermute | solution.py:454
  95.2 13.7 %collective-permute-start.9 = (bf16[64,3584]{1,0:T(8,128)(2,1)S(1)}, bf16[64,3584]{1,0:T(8,128)(2,1)S(1)}, u32[]{:S(2)}, u32[]{:S(2)}) collective-permute-start(bf16[64,3584]{1,0:T(8,128)(2,1)S(1)} %slice.17), channel_id=1, source_target_pairs={{0,2},{6,4},{1,3},{7,5},{8,10},{14,12},{9,11},{15,13},{16,18},{22,... | collective-permute-start | bytes 1376264 | tf_op jit(solution)/shard_map/ppermute | solution.py:453
